TPU v7x, 32 devices: a whole 2x2x4 slice. The times are simulated.
32 devices in a mesh: dp: 16 (over z, x, core), fsdp: 2 (over y).
Axes of the slice: x: 2, y: 2, z: 4, core: 2. Of those that a mesh axis runs over, the one named last changes fastest.
Arguments:
- inputs: bfloat16 [32, 2048, 768], P('dp', 'fsdp'), may hold values from -6 to 6
- cotangent: bfloat16 [32, 2048, 768], P('dp', 'fsdp'), may hold values from -6 to 6
- lengths: int32 [32], P('dp'), may hold values from 512 to 2048, as said below
- w_query: float32 [768, 768], P(None, ('dp', 'fsdp')), may hold values from -0.0546875 to 0.0546875
- w_key: float32 [768, 768], P(None, ('dp', 'fsdp')), may hold values from -0.21875 to 0.21875
- w_value: float32 [768, 768], P(None, ('dp', 'fsdp')), may hold values from -0.21875 to 0.21875
- w_out: float32 [768, 768], P(None, ('dp', 'fsdp')), may hold values from -0.875 to 0.875
- w_gate: float32 [768, 2048], P(None, ('dp', 'fsdp')), may hold values from -0.21875 to 0.21875
- w_up: float32 [768, 2048], P(None, ('dp', 'fsdp')), may hold values from -0.21875 to 0.21875
- w_down: float32 [2048, 768], P(None, ('dp', 'fsdp')), may hold values from -0.125 to 0.125
- gain_attn: float32 [768], P(('dp', 'fsdp')), may hold values from 0.5 to 1.5
- gain_ffn: float32 [768], P(('dp', 'fsdp')), may hold values from 0.5 to 1.5
- bias_table: float32 [32, 12], replicated, may hold values from -3 to 3
Outputs:
- output: float32 [32, 2048, 768], P('dp', 'fsdp')
- grad_inputs: float32 [32, 2048, 768], P('dp', 'fsdp')
- grad_w_query: float32 [768, 768], P(None, ('dp', 'fsdp'))
- grad_w_key: float32 [768, 768], P(None, ('dp', 'fsdp'))
- grad_w_value: float32 [768, 768], P(None, ('dp', 'fsdp'))
- grad_w_out: float32 [768, 768], P(None, ('dp', 'fsdp'))
- grad_w_gate: float32 [768, 2048], P(None, ('dp', 'fsdp'))
- grad_w_up: float32 [768, 2048], P(None, ('dp', 'fsdp'))
- grad_w_down: float32 [2048, 768], P(None, ('dp', 'fsdp'))
- grad_gain_attn: float32 [768], P(('dp', 'fsdp'))
- grad_gain_ffn: float32 [768], P(('dp', 'fsdp'))
- grad_bias_table: float32 [32, 12], replicated
Inputs may be any that keep to these rules, and one draw needn't show every extreme that they name: `lengths`: each entry counts the valid tokens of one sequence, which fill the start of its slot of 2048; the first sequence fills its whole slot and the second has the least length.
All inputs are finite; a program needn't handle non-finite values.
Results may differ from a plain program's by a relative error of at most 0.015.
The roundings to bfloat16 on the way count: a program that leaves them out, or rounds other values in their place, can miss the bound.
Values may be sent and summed in bfloat16 or wider, within the bound.
No kernel may reach another device: no remote copies, remote signals or barrier semaphores. Data moves between devices by JAX's collectives and lax.ppermute only.
A program may use at most 320 MiB of HBM per device.

v0:
```python
import jax
import jax.numpy as jnp
from jax import lax
from jax.sharding import PartitionSpec as P

D = 768
HEADS = 12
HEAD_DIM = 64
FF = 2048
BUCKETS = 32
SLOT = 2048
MB = 2
SEQ_MB = 1


EPSILON = 1e-06
MASKED = -1000000000.0
PRECISE = lax.Precision.HIGHEST
THRESHOLDS = (12, 16, 23, 32, 46, 64, 91)


def bucket_of(offsets):
    distance = jnp.abs(offsets)
    larger = jnp.full(offsets.shape, 8, jnp.int32)
    for threshold in THRESHOLDS:
        larger = larger + (distance >= threshold).astype(jnp.int32)
    nearby = jnp.where(distance < 8, distance, larger)
    return jnp.where(offsets > 0, 16, 0).astype(jnp.int32) + nearby


def rms_factor(values):
    return lax.rsqrt(jnp.mean(values * values, axis=-1, keepdims=True) + EPSILON)


def norm_back(grad_normed, values, factor, gain):
    scaled = grad_normed * gain
    return factor * scaled - values * (factor * factor * factor) * jnp.mean(
        scaled * values, axis=-1, keepdims=True
    )


def gelu_tanh(values):
    return jax.nn.gelu(values, approximate=True)


def inner_rows(first_operand, second_operand):
    return lax.dot_general(
        first_operand, second_operand, (((0,), (0,)), ((), ())), preferred_element_type=jnp.float32
    )


def times_transposed(first_operand, second_operand):
    return lax.dot_general(
        first_operand, second_operand, (((1,), (1,)), ((), ())), preferred_element_type=jnp.float32
    )


def skew_expand(vector, row_count, col_count):
    head_count = vector.shape[0]
    full_width = row_count + col_count
    spread = jnp.broadcast_to(vector[:, None, :], (head_count, row_count, full_width + 1))
    spread = spread.reshape(head_count, row_count * (full_width + 1))[:, : row_count * full_width]
    return spread.reshape(head_count, row_count, full_width)[:, :, row_count:]


def skew_reduce(grid_values, row_count, col_count):
    head_count = grid_values.shape[0]
    full_width = row_count + col_count
    padded = jnp.pad(grid_values, ((0, 0), (0, 0), (row_count, 0))).reshape(
        head_count, row_count * full_width
    )
    padded = jnp.pad(padded, ((0, 0), (0, row_count))).reshape(
        head_count, row_count, full_width + 1
    )
    return jnp.sum(padded, axis=1)


def to_pairs(matrix, seq_count, row_count):
    return matrix.reshape(seq_count, row_count, HEADS // 2, 2 * HEAD_DIM).transpose(2, 0, 1, 3)


def from_pairs(stacked):
    pair_count, seq_count, row_count, lane_width = stacked.shape
    return stacked.transpose(1, 2, 0, 3).reshape(seq_count * row_count, pair_count * lane_width)


def pair_scores(query_pair, key_pair, bias_pair, key_valid):
    seq_count, row_count = (query_pair.shape[0], query_pair.shape[1])
    key_count = key_pair.shape[1]
    raw_scores = jnp.einsum(
        "sqhd,skhd->shqk",
        query_pair.reshape(seq_count, row_count, 2, HEAD_DIM),
        key_pair.reshape(seq_count, key_count, 2, HEAD_DIM),
        preferred_element_type=jnp.float32,
    )
    biased = raw_scores + skew_expand(bias_pair, row_count, key_count)[None]
    return jnp.where(key_valid[:, None, None, :], biased, MASKED)


def per_device(
    inputs,
    cotangent,
    lengths,
    w_query,
    w_key,
    w_value,
    w_out,
    w_gate,
    w_up,
    w_down,
    gain_attn,
    gain_ffn,
    bias_table,
):
    row_count = inputs.shape[1]
    features = inputs.shape[2]
    seq_count = SEQ_MB
    token_rows = seq_count * row_count
    key_count = SLOT
    offset = lax.axis_index("fsdp") * row_count
    low_query = w_query.astype(jnp.bfloat16)
    low_key = w_key.astype(jnp.bfloat16)
    low_value = w_value.astype(jnp.bfloat16)
    low_out = w_out.astype(jnp.bfloat16)
    low_gate = w_gate.astype(jnp.bfloat16)
    low_up = w_up.astype(jnp.bfloat16)
    low_down = w_down.astype(jnp.bfloat16)
    low_gain_one = gain_attn.astype(jnp.bfloat16)
    low_gain_two = gain_ffn.astype(jnp.bfloat16)
    columns = jnp.arange(row_count + key_count + 1, dtype=jnp.int32) - row_count - offset
    onehot = (bucket_of(columns)[:, None] == jnp.arange(BUCKETS, dtype=jnp.int32)[None, :]).astype(
        jnp.float32
    )
    relative = jnp.dot(onehot, bias_table, precision=PRECISE).T.reshape(
        HEADS // 2, 2, row_count + key_count + 1
    )
    grad_query_w = jnp.zeros((D, D), jnp.float32)
    grad_key_w = jnp.zeros((D, D), jnp.float32)
    grad_value_w = jnp.zeros((D, D), jnp.float32)
    grad_out_w = jnp.zeros((D, D), jnp.float32)
    grad_gate_w = jnp.zeros((D, FF), jnp.float32)
    grad_up_w = jnp.zeros((D, FF), jnp.float32)
    grad_down_w = jnp.zeros((FF, D), jnp.float32)
    grad_gain_one = jnp.zeros((D,), jnp.float32)
    grad_gain_two = jnp.zeros((D,), jnp.float32)
    relative_grad = jnp.zeros(relative.shape, jnp.float32)
    outputs = []
    input_grads = []
    for micro_batch in range(MB):
        fetched = (
            lax.all_gather(low_query, ("dp", "fsdp"), axis=1, tiled=True),
            lax.all_gather(low_key, ("dp", "fsdp"), axis=1, tiled=True),
            lax.all_gather(low_value, ("dp", "fsdp"), axis=1, tiled=True),
            lax.all_gather(low_out, ("dp", "fsdp"), axis=1, tiled=True),
            lax.all_gather(low_gate, ("dp", "fsdp"), axis=1, tiled=True),
            lax.all_gather(low_up, ("dp", "fsdp"), axis=1, tiled=True),
            lax.all_gather(low_down, ("dp", "fsdp"), axis=1, tiled=True),
            lax.all_gather(low_gain_one, ("dp", "fsdp"), axis=0, tiled=True),
            lax.all_gather(low_gain_two, ("dp", "fsdp"), axis=0, tiled=True),
        )
        (
            query_weight,
            key_weight,
            value_weight,
            out_weight,
            gate_weight,
            up_weight,
            down_weight,
            gain_one,
            gain_two,
        ) = fetched
        scale_one = gain_one.astype(jnp.float32)
        scale_two = gain_two.astype(jnp.float32)
        first_row = micro_batch * seq_count
        block_lengths = lengths[first_row : first_row + seq_count]
        row_values = (
            inputs[first_row : first_row + seq_count]
            .reshape(token_rows, features)
            .astype(jnp.float32)
        )
        factor_one = rms_factor(row_values)
        normed = (row_values * factor_one * scale_one).astype(jnp.bfloat16)
        queries = jnp.dot(normed, query_weight, preferred_element_type=jnp.float32).astype(
            jnp.bfloat16
        )
        key_rows = jnp.dot(normed, key_weight, preferred_element_type=jnp.float32).astype(
            jnp.bfloat16
        )
        value_rows = jnp.dot(normed, value_weight, preferred_element_type=jnp.float32).astype(
            jnp.bfloat16
        )
        query_pairs = to_pairs(queries, seq_count, row_count)
        key_own = to_pairs(key_rows, seq_count, row_count)
        value_own = to_pairs(value_rows, seq_count, row_count)
        key_all, value_all = (
            lax.all_gather(key_own, "fsdp", axis=2, tiled=True),
            lax.all_gather(value_own, "fsdp", axis=2, tiled=True),
        )
        key_valid = jnp.arange(key_count, dtype=jnp.int32)[None, :] < block_lengths[:, None]
        positions = offset + jnp.arange(row_count, dtype=jnp.int32)
        own_valid = positions[None, :] < block_lengths[:, None]

        def forward_pair(carried, members):
            query_pair, key_pair, value_pair, bias_pair = members
            scores = pair_scores(query_pair, key_pair, bias_pair, key_valid)
            row_max = jnp.max(scores, axis=-1, keepdims=True)
            exponent = jnp.exp(scores - row_max)
            row_sum = jnp.sum(exponent, axis=-1, keepdims=True)
            probs_low = (exponent / row_sum).astype(jnp.bfloat16)
            mixed_pair = jnp.einsum(
                "shqk,skhd->sqhd",
                probs_low,
                value_pair.reshape(seq_count, key_count, 2, HEAD_DIM),
                preferred_element_type=jnp.float32,
            )
            return (
                carried,
                (mixed_pair.reshape(seq_count, row_count, 2 * HEAD_DIM), row_max, row_sum),
            )

        unused, (mixed_pairs, row_maxes, row_sums) = lax.scan(
            forward_pair, 0, (query_pairs, key_all, value_all, relative)
        )
        attended = from_pairs(mixed_pairs).astype(jnp.bfloat16)
        hidden = row_values + jnp.dot(attended, out_weight, preferred_element_type=jnp.float32)
        factor_two = rms_factor(hidden)
        normed_ffn = (hidden * factor_two * scale_two).astype(jnp.bfloat16)
        gate_value = jnp.dot(normed_ffn, gate_weight, preferred_element_type=jnp.float32)
        up_value = jnp.dot(normed_ffn, up_weight, preferred_element_type=jnp.float32)
        activation, gelu_back = jax.vjp(gelu_tanh, gate_value)
        activated = (activation * up_value).astype(jnp.bfloat16)
        output_rows = hidden + jnp.dot(activated, down_weight, preferred_element_type=jnp.float32)
        outputs.append(output_rows.reshape(seq_count, row_count, features))
        back_weights = (
            lax.all_gather(low_query, ("dp", "fsdp"), axis=1, tiled=True),
            lax.all_gather(low_key, ("dp", "fsdp"), axis=1, tiled=True),
            lax.all_gather(low_value, ("dp", "fsdp"), axis=1, tiled=True),
            lax.all_gather(low_out, ("dp", "fsdp"), axis=1, tiled=True),
            lax.all_gather(low_gate, ("dp", "fsdp"), axis=1, tiled=True),
            lax.all_gather(low_up, ("dp", "fsdp"), axis=1, tiled=True),
            lax.all_gather(low_down, ("dp", "fsdp"), axis=1, tiled=True),
            lax.all_gather(low_gain_one, ("dp", "fsdp"), axis=0, tiled=True),
            lax.all_gather(low_gain_two, ("dp", "fsdp"), axis=0, tiled=True),
        )
        (
            back_query,
            back_key,
            back_value,
            back_out,
            back_gate,
            back_up,
            back_down,
            unused_one,
            unused_two,
        ) = back_weights
        valid_rows = own_valid.astype(jnp.float32).reshape(token_rows, 1)
        seed = (
            cotangent[first_row : first_row + seq_count]
            .reshape(token_rows, features)
            .astype(jnp.float32)
            * valid_rows
        )
        seed_low = seed.astype(jnp.bfloat16)
        grad_down_w = grad_down_w + inner_rows(activated, seed_low)
        grad_activated = times_transposed(seed_low, back_down)
        grad_gate = gelu_back(grad_activated * up_value)[0].astype(jnp.bfloat16)
        grad_up = (grad_activated * activation).astype(jnp.bfloat16)
        grad_gate_w = grad_gate_w + inner_rows(normed_ffn, grad_gate)
        grad_up_w = grad_up_w + inner_rows(normed_ffn, grad_up)
        grad_normed_ffn = times_transposed(grad_gate, back_gate) + times_transposed(
            grad_up, back_up
        )
        grad_gain_two = grad_gain_two + jnp.sum(grad_normed_ffn * hidden * factor_two, axis=0)
        grad_hidden = seed + norm_back(grad_normed_ffn, hidden, factor_two, scale_two)
        grad_branch = grad_hidden.astype(jnp.bfloat16)
        grad_out_w = grad_out_w + inner_rows(attended, grad_branch)
        grad_attended = to_pairs(
            times_transposed(grad_branch, back_out).astype(jnp.bfloat16), seq_count, row_count
        )

        def query_side_back(
            query_pair, key_pair, value_pair, bias_pair, row_max, row_sum, grad_pair
        ):
            scores = pair_scores(query_pair, key_pair, bias_pair, key_valid)
            probabilities = jnp.exp(scores - row_max) / row_sum
            grad_four = grad_pair.reshape(seq_count, row_count, 2, HEAD_DIM)
            grad_probs = jnp.einsum(
                "sqhd,skhd->shqk",
                grad_four,
                value_pair.reshape(seq_count, key_count, 2, HEAD_DIM),
                preferred_element_type=jnp.float32,
            )
            row_dot = jnp.sum(probabilities * grad_probs, axis=-1, keepdims=True)
            grad_scores = probabilities * (grad_probs - row_dot)
            bias_grad = skew_reduce(jnp.sum(grad_scores, axis=0), row_count, key_count)
            scores_low = grad_scores.astype(jnp.bfloat16)
            grad_query = jnp.einsum(
                "shqk,skhd->sqhd",
                scores_low,
                key_pair.reshape(seq_count, key_count, 2, HEAD_DIM),
                preferred_element_type=jnp.float32,
            )
            return (
                probabilities,
                grad_four,
                scores_low,
                grad_query.reshape(seq_count, row_count, 2 * HEAD_DIM),
                bias_grad,
                row_dot,
            )

        def backward_pair(carried, members):
            query_pair, key_pair, value_pair, bias_pair, row_max, row_sum, grad_pair = members
            probabilities, grad_four, scores_low, grad_query, bias_grad, unused_dot = (
                query_side_back(
                    query_pair, key_pair, value_pair, bias_pair, row_max, row_sum, grad_pair
                )
            )
            grad_key = jnp.einsum(
                "shqk,sqhd->skhd",
                scores_low,
                query_pair.reshape(seq_count, row_count, 2, HEAD_DIM),
                preferred_element_type=jnp.float32,
            )
            grad_value = jnp.einsum(
                "shqk,sqhd->skhd",
                probabilities.astype(jnp.bfloat16),
                grad_four,
                preferred_element_type=jnp.float32,
            )
            return (
                carried,
                (
                    grad_query,
                    grad_key.reshape(seq_count, key_count, 2 * HEAD_DIM),
                    grad_value.reshape(seq_count, key_count, 2 * HEAD_DIM),
                    bias_grad,
                ),
            )

        unused, (query_grad_pairs, key_grad_pairs, value_grad_pairs, bias_grads) = lax.scan(
            backward_pair,
            0,
            (query_pairs, key_all, value_all, relative, row_maxes, row_sums, grad_attended),
        )
        key_grad_own, value_grad_own = (
            lax.psum_scatter(
                key_grad_pairs.astype(jnp.bfloat16), "fsdp", scatter_dimension=2, tiled=True
            ).astype(jnp.float32),
            lax.psum_scatter(
                value_grad_pairs.astype(jnp.bfloat16), "fsdp", scatter_dimension=2, tiled=True
            ).astype(jnp.float32),
        )
        relative_grad = relative_grad + bias_grads
        grad_queries = from_pairs(query_grad_pairs).astype(jnp.bfloat16)
        grad_keys = from_pairs(key_grad_own).astype(jnp.bfloat16)
        grad_values = from_pairs(value_grad_own).astype(jnp.bfloat16)
        grad_query_w = grad_query_w + inner_rows(normed, grad_queries)
        grad_key_w = grad_key_w + inner_rows(normed, grad_keys)
        grad_value_w = grad_value_w + inner_rows(normed, grad_values)
        grad_normed = (
            times_transposed(grad_queries, back_query)
            + times_transposed(grad_keys, back_key)
            + times_transposed(grad_values, back_value)
        )
        grad_gain_one = grad_gain_one + jnp.sum(grad_normed * row_values * factor_one, axis=0)
        grad_rows = grad_hidden + norm_back(grad_normed, row_values, factor_one, scale_one)
        input_grads.append(grad_rows.reshape(seq_count, row_count, features))
    table_grad = jnp.dot(
        onehot.T, relative_grad.reshape(HEADS, row_count + key_count + 1).T, precision=PRECISE
    )
    table_total = lax.psum(table_grad, ("dp", "fsdp"))
    shares = (
        lax.psum_scatter(grad_query_w, ("dp", "fsdp"), scatter_dimension=1, tiled=True),
        lax.psum_scatter(grad_key_w, ("dp", "fsdp"), scatter_dimension=1, tiled=True),
        lax.psum_scatter(grad_value_w, ("dp", "fsdp"), scatter_dimension=1, tiled=True),
        lax.psum_scatter(grad_out_w, ("dp", "fsdp"), scatter_dimension=1, tiled=True),
        lax.psum_scatter(grad_gate_w, ("dp", "fsdp"), scatter_dimension=1, tiled=True),
        lax.psum_scatter(grad_up_w, ("dp", "fsdp"), scatter_dimension=1, tiled=True),
        lax.psum_scatter(grad_down_w, ("dp", "fsdp"), scatter_dimension=1, tiled=True),
        lax.psum_scatter(grad_gain_one, ("dp", "fsdp"), scatter_dimension=0, tiled=True),
        lax.psum_scatter(grad_gain_two, ("dp", "fsdp"), scatter_dimension=0, tiled=True),
    )
    return (
        jnp.concatenate(outputs, axis=0),
        jnp.concatenate(input_grads, axis=0),
        shares[0],
        shares[1],
        shares[2],
        shares[3],
        shares[4],
        shares[5],
        shares[6],
        shares[7],
        shares[8],
        table_total,
    )


def solution(mesh):
    return jax.shard_map(
        per_device,
        mesh=mesh,
        in_specs=(
            P("dp", "fsdp", None),
            P("dp", "fsdp", None),
            P("dp"),
            P(None, ("dp", "fsdp")),
            P(None, ("dp", "fsdp")),
            P(None, ("dp", "fsdp")),
            P(None, ("dp", "fsdp")),
            P(None, ("dp", "fsdp")),
            P(None, ("dp", "fsdp")),
            P(None, ("dp", "fsdp")),
            P(("dp", "fsdp")),
            P(("dp", "fsdp")),
            P(),
        ),
        out_specs=(
            P("dp", "fsdp", None),
            P("dp", "fsdp", None),
            P(None, ("dp", "fsdp")),
            P(None, ("dp", "fsdp")),
            P(None, ("dp", "fsdp")),
            P(None, ("dp", "fsdp")),
            P(None, ("dp", "fsdp")),
            P(None, ("dp", "fsdp")),
            P(None, ("dp", "fsdp")),
            P(("dp", "fsdp")),
            P(("dp", "fsdp")),
            P(),
        ),
        check_vma=False,
    )
```

profile of v0, /device:TPU:0, one launch (start us, length us, event | category | flops | bytes accessed | tf_op | source)
XLA Modules:
  0.0 7452.4 jit_solution(2384855834112509040)
XLA Ops:
  72.4 52.7 all-gather.18.cloned.1.call-done
  227.7 46.4 all-gather.32.cloned.1.call-done
  274.3 952.1 %while.69 = (s32[]{:T(128)}, bf16[6,1,1024,128]{2,3,1,0:T(8,128)(2,1)S(1)}, f32[6,1,2,1024,1]{3,2,4,1,0:T(2,128)S(1)}, f32[6,1,2,1024,1]{3,2,4,1,0:T(2,128)S(1)}...) while((s32[]{:T(128)}, ...), condition=%wide.region_10.11_spmd.clone, body=%wide.region_7.10_spmd.clone.sunk | while | flops 1107294208 | bytes 298512512 | solution.py:221
  1228.1 960.8 %while.68 = (s32[]{:T(128)}, bf16[6,1,1024,128]{2,3,1,0:T(8,128)(2,1)}, f32[6,1,2,1024,1]{3,2,4,1,0:T(2,128)S(1)}, f32[6,1,2,1024,1]{3,2,4,1,0:T(2,128)S(1)}, bf...) while((s32[]{:T(128)}, ...), condition=%wide.region_4.5_spmd.clone, body=%wide.region_1.4_spmd.clone.sunk | while | flops 1107294208 | bytes 298512512 | solution.py:221
  2293.9 2113.9 %while.70 = (s32[]{:T(128)}, bf16[6,1,1024,128]{2,3,1,0:T(8,128)(2,1)}, bf16[6,1,2048,128]{2,3,1,0:T(8,128)(2,1)}, bf16[6,1,2048,128]{2,3,1,0:T(8,128)(2,1)}, f3...) while((s32[]{:T(128)}, ...), condition=%wide.region_16.17_spmd.clone, body=%wide.region_13.16_spmd.clone.sunk | while | flops 2736779264 | bytes 686077120 | solution.py:341
  2543.8 54.9 reshape.786
  2895.6 55.1 reshape.786
  3247.5 54.9 reshape.786
  3599.3 55.1 reshape.786
  3951.2 54.9 reshape.786
  4303.0 55.1 reshape.786
  4420.9 2111.4 %while.71 = (s32[]{:T(128)}, bf16[6,1,1024,128]{2,3,1,0:T(8,128)(2,1)S(1)}, bf16[6,1,2048,128]{2,3,1,0:T(8,128)(2,1)}, bf16[6,1,2048,128]{2,3,1,0:T(8,128)(2,1)}...) while((s32[]{:T(128)}, ...), condition=%wide.region_24.25_spmd.clone, body=%wide.region_21.24_spmd.clone.sunk | while | flops 2736779264 | bytes 672707776 | solution.py:341
  4670.5 54.9 reshape.790
  5021.2 55.1 reshape.790
  5372.0 54.9 reshape.790
  5722.7 55.1 reshape.790
  6073.5 54.9 reshape.790
  6424.2 55.1 reshape.790
  6771.6 104.7 %reduce-scatter.26.cloned.1.call-done = f32[768,24]{0,1:T(8,128)} async-done(((f32[768,768]{0,1:T(8,128)}), f32[768,24]{0,1:T(8,128)}) %reduce-scatter.26.cloned.1.call-update) | async-done | bytes 73744 | tf_op jit(solution)/shard_map/reduce_scatter | solution.py:377
  6876.3 119.6 %reduce-scatter.28.cloned.1.call-done = f32[768,64]{0,1:T(8,128)} async-done(((f32[768,2048]{0,1:T(8,128)}), f32[768,64]{0,1:T(8,128)}) %reduce-scatter.28.cloned.1.call-update) | async-done | bytes 196624 | tf_op jit(solution)/shard_map/reduce_scatter | solution.py:378
  6995.8 120.9 %reduce-scatter.30.cloned.1.call-done = f32[768,64]{0,1:T(8,128)} async-done(((f32[768,2048]{0,1:T(8,128)}), f32[768,64]{0,1:T(8,128)}) %reduce-scatter.30.cloned.1.call-update) | async-done | bytes 196624 | tf_op jit(solution)/shard_map/reduce_scatter | solution.py:379
  7116.8 119.6 %reduce-scatter.32.cloned.1.call-done = f32[2048,24]{0,1:T(8,128)} async-done(((f32[2048,768]{0,1:T(8,128)}), f32[2048,24]{0,1:T(8,128)}) %reduce-scatter.32.cloned.1.call-update) | async-done | bytes 196624 | tf_op jit(solution)/shard_map/reduce_scatter | solution.py:380
  7236.3 105.1 %reduce-scatter.22.cloned.1.call-done = f32[768,24]{0,1:T(8,128)} async-done(((f32[768,768]{0,1:T(8,128)}), f32[768,24]{0,1:T(8,128)}) %reduce-scatter.22.cloned.1.call-update) | async-done | bytes 73744 | tf_op jit(solution)/shard_map/reduce_scatter | solution.py:375
  7341.4 103.9 %reduce-scatter.24.cloned.1.call-done = f32[768,24]{0,1:T(8,128)} async-done(((f32[768,768]{0,1:T(8,128)}), f32[768,24]{0,1:T(8,128)}) %reduce-scatter.24.cloned.1.call-update) | async-done | bytes 73744 | tf_op jit(solution)/shard_map/reduce_scatter | solution.py:376
  (883 shorter events, 5941.1 us)
Async XLA Ops:
  7.2 61.3 all-gather.12.cloned.1.call-start
  8.8 116.4 %all-gather.18.cloned.1.call-start = ((), (), s32[]{:S(2)}) async-start(), calls=%async_computation.14 | async-start | bytes 1216512 | tf_op jit(solution)/shard_map/all_gather | solution.py:152
  10.4 171.4 %all-gather.16.cloned.1.call-start = ((), (), s32[]{:S(2)}) async-start(), calls=%async_computation.13 | async-start | bytes 1216512 | tf_op jit(solution)/shard_map/all_gather | solution.py:151
  11.9 215.7 %all-gather.30.cloned.1.call-start = ((), (), s32[]{:S(2)}) async-start(), calls=%async_computation.20 | async-start | bytes 4718592 | tf_op jit(solution)/shard_map/all_gather | solution.py:197
  72.4 201.6 %all-gather.32.cloned.1.call-start = ((), (), s32[]{:S(2)}) async-start(), calls=%async_computation.21 | async-start | bytes 4718592 | tf_op jit(solution)/shard_map/all_gather | solution.py:196
  129.1 1097.3 %all-gather.14.cloned.1.call-start = ((), (), s32[]{:S(2)}) async-start(), calls=%async_computation.12 | async-start | bytes 4718592 | tf_op jit(solution)/shard_map/all_gather | solution.py:197
  136.0 1090.5 %all-gather.20.cloned.1.call-start = ((), (), s32[]{:S(2)}) async-start(), calls=%async_computation.15 | async-start | bytes 4718592 | tf_op jit(solution)/shard_map/all_gather | solution.py:196
  140.1 2048.8 %all-gather.22.cloned.1.call-start = ((), (), s32[]{:S(2)}) async-start(), calls=%async_computation.16 | async-start | bytes 1216512 | tf_op jit(solution)/shard_map/all_gather | solution.py:154
  141.7 2055.9 %all-gather.24.cloned.1.call-start = ((), (), s32[]{:S(2)}) async-start(), calls=%async_computation.17 | async-start | bytes 3244032 | tf_op jit(solution)/shard_map/all_gather | solution.py:155
  142.4 2064.3 %all-gather.26.cloned.1.call-start = ((), (), s32[]{:S(2)}) async-start(), calls=%async_computation.18 | async-start | bytes 3244032 | tf_op jit(solution)/shard_map/all_gather | solution.py:156
  143.1 2072.7 %all-gather.28.cloned.1.call-start = ((), (), s32[]{:S(2)}) async-start(), calls=%async_computation.19 | async-start | bytes 3244032 | tf_op jit(solution)/shard_map/all_gather | solution.py:157
  144.8 6439.8 %reduce-scatter.12.cloned.1.call-start = ((), (), s32[]{:S(2)}) async-start(), calls=%async_computation.22 | async-start | bytes 4718592 | tf_op jit(solution)/shard_map/reduce_scatter | solution.py:347
  1228.0 960.8 %copy-start.3 = (bf16[1,1024,768]{1,2,0:T(8,128)(2,1)S(1)}, bf16[1,1024,768]{1,2,0:T(8,128)(2,1)}, u32[]{:S(2)}) copy-start(bf16[1,1024,768]{1,2,0:T(8,128)(2,1)} %copy-done.2) | copy-start | bytes 4718596
  4407.9 2181.2 %reduce-scatter.16.cloned.1.call-start = ((), (), s32[]{:S(2)}) async-start(), calls=%async_computation.24 | async-start | bytes 4718592 | tf_op jit(solution)/shard_map/reduce_scatter | solution.py:347
  6532.3 95.4 %reduce-scatter.14.cloned.1.call-start = ((), (), s32[]{:S(2)}) async-start(), calls=%async_computation.23 | async-start | bytes 4718592 | tf_op jit(solution)/shard_map/reduce_scatter | solution.py:350
  6533.5 133.4 %reduce-scatter.18.cloned.1.call-start = ((), (), s32[]{:S(2)}) async-start(), calls=%async_computation.25 | async-start | bytes 4718592 | tf_op jit(solution)/shard_map/reduce_scatter | solution.py:350
  6534.1 237.6 %reduce-scatter.20.cloned.1.call-start = ((), (), s32[]{:S(2)}) async-start(), calls=%async_computation.26 | async-start | bytes 2433024 | tf_op jit(solution)/shard_map/reduce_scatter | solution.py:374
  6540.9 335.4 %reduce-scatter.26.cloned.1.call-start = ((), (), s32[]{:S(2)}) async-start(), calls=%async_computation.29 | async-start | bytes 2433024 | tf_op jit(solution)/shard_map/reduce_scatter | solution.py:377
  6547.9 448.0 %reduce-scatter.28.cloned.1.call-start = ((), (), s32[]{:S(2)}) async-start(), calls=%async_computation.30 | async-start | bytes 6488064 | tf_op jit(solution)/shard_map/reduce_scatter | solution.py:378
  6560.0 556.8 %reduce-scatter.30.cloned.1.call-start = ((), (), s32[]{:S(2)}) async-start(), calls=%async_computation.31 | async-start | bytes 6488064 | tf_op jit(solution)/shard_map/reduce_scatter | solution.py:379
  6572.4 663.9 %reduce-scatter.32.cloned.1.call-start = ((), (), s32[]{:S(2)}) async-start(), calls=%async_computation.32 | async-start | bytes 6488064 | tf_op jit(solution)/shard_map/reduce_scatter | solution.py:380
  6584.5 756.9 %reduce-scatter.22.cloned.1.call-start = ((), (), s32[]{:S(2)}) async-start(), calls=%async_computation.27 | async-start | bytes 2433024 | tf_op jit(solution)/shard_map/reduce_scatter | solution.py:375
  6594.2 851.1 %reduce-scatter.24.cloned.1.call-start = ((), (), s32[]{:S(2)}) async-start(), calls=%async_computation.28 | async-start | bytes 2433024 | tf_op jit(solution)/shard_map/reduce_scatter | solution.py:376
  6689.9 755.5 %copy-start.1 = (f32[32,12]{0,1:T(8,128)S(1)}, f32[32,12]{0,1:T(8,128)}, u32[]{:S(2)}) copy-start(f32[32,12]{0,1:T(8,128)} %param.33) | copy-start | bytes 4612
  (116 other events, 1519.9 us)
Sparse Core Ops, SparseCore 0:
  11.5 56.9 all-gather.11
  71.9 53.1 all-gather.17
  128.7 53.0 all-gather.15
  183.8 43.8 all-gather.29
  229.0 44.9 all-gather.31
  276.0 44.9 all-gather.13
  322.5 44.9 all-gather.19
  371.0 54.1 all-gather.21
  428.6 58.1 all-gather.23
  490.1 57.8 all-gather.25
  550.9 57.8 all-gather.27
  4408.0 43.3 reduce-scatter.11
  6532.4 43.3 reduce-scatter.15
  6577.9 43.3 reduce-scatter.13
  6623.5 43.3 reduce-scatter.17
  6672.6 99.0 reduce-scatter.19
  6778.2 98.0 reduce-scatter.25
  6882.3 113.4 reduce-scatter.27
  7003.0 113.7 reduce-scatter.29
  7122.8 113.4 reduce-scatter.31
  7243.1 98.3 reduce-scatter.21
  7347.3 98.0 reduce-scatter.23
where the time goes:
time: 7470 us; the launch traced here: 7450 us
  local copies, waits for them, and re-layouts  5100 us (68%)
  waiting for transfers between devices  912 us (12%)
  matrix products  878 us (12%)
  other arithmetic  396 us (5%)
  blocking collectives  81.8 us (1%)
    while x156, local copies, waits for them, and re-layouts  2730 us
    reshape x24, local copies, waits for them, and re-layouts, skew_expand(): spread.reshape(head_count, row_count * (full_width + 1))  879 us
    reshape x12, local copies, waits for them, and re-layouts, skew_reduce(): jnp.pad(padded, ((0, 0), (0, row_count)))  439 us
    slice x24, local copies, waits for them, and re-layouts, skew_expand(): spread.reshape(head_count, row_count * (full_width + 1))  410 us
    dot_general x24, matrix products, pair_scores(): jnp.einsum('sqhd,skhd->shqk', query_pair.reshape(seq_count, row_count, 2,...  334 us
    broadcast_in_dim x48, local copies, waits for them, and re-layouts, skew_expand(): jnp.broadcast_to(vector[:, None, :], (head_count, row_count, full_width +...  267 us
    pad x12, local copies, waits for them, and re-layouts, skew_reduce(): jnp.pad(padded, ((0, 0), (0, row_count)))  219 us
  transfers between devices with their start and end apart: 22, of which 13 were waited for; matrix products, arithmetic and copies ran while one was open for 56% of the time, Pallas kernels for 0%

commit v1 on v0

v1 whole, which is shorter than its diff:
```python
import functools, jax, jax.numpy as jnp
from jax import lax
from jax.experimental import pallas as pl
from jax.experimental.pallas import tpu as pltpu

HEAD_DIM = 64
LANES = 128
MASKED = -1000000000.0
VMEM_LIMIT = 60 << 20
f32, bf16 = jnp.float32, jnp.bfloat16


def dot_nt(a, b):
    return lax.dot_general(a, b, (((1,), (1,)), ((), ())), preferred_element_type=f32)


def dot_nn(a, b):
    return lax.dot_general(a, b, (((1,), (0,)), ((), ())), preferred_element_type=f32)


def dot_tn(a, b):
    return lax.dot_general(a, b, (((0,), (0,)), ((), ())), preferred_element_type=f32)


def three_pieces(x):
    hi = x.astype(bf16).astype(f32)
    mid = (x - hi).astype(bf16).astype(f32)
    return hi, mid, x - hi - mid


def skewed(row, width):
    spread = jnp.broadcast_to(row, (LANES, width))
    return pltpu.roll(spread, 0, 1, stride=1, stride_axis=0)


def lane_iota(rows):
    return lax.broadcasted_iota(jnp.int32, (rows, LANES), 1)


def key_extra(rows, length, ones_low, ones_high):
    lanes = lane_iota(rows)
    position = lax.broadcasted_iota(jnp.int32, (rows, LANES), 0)
    ones = ((lanes >= ones_low) & (lanes < ones_high)).astype(f32)
    masked = jnp.where(position < length, 0.0, MASKED)
    return jnp.where(lanes == 6, masked, ones).astype(bf16)


def forward_kernel(q_tile, k_tile, lengths, offset, q_ref, k_ref, v_ref, bias_ref, out_ref, extra_ref, keys, values, strips, scores):
    slots = k_ref.shape[1]
    tile = pl.program_id(2)
    origin = q_tile + k_tile
    chunks = slots // k_tile

    @pl.when(tile == 0)
    def _():
        keys[:, :LANES] = k_ref[0]
        keys[:, LANES:] = key_extra(slots, lengths[pl.program_id(0)], 0, 0)
        turned = v_ref[0].astype(f32).T.astype(bf16)
        for h in range(2):
            values[h, :HEAD_DIM, :] = turned[h * HEAD_DIM : (h + 1) * HEAD_DIM]
            values[h, HEAD_DIM:, :] = jnp.ones((16, slots), bf16)
            strips[h] = skewed(bias_ref[0, h : h + 1, :], strips.shape[2])

    lanes = lane_iota(q_tile)
    pair = q_ref[0].astype(f32)
    const = jnp.where(lanes == 6, 1.0, 0.0).astype(bf16)
    weights = jnp.concatenate(
        [
            jnp.concatenate([jnp.where((lanes < HEAD_DIM) == (h == 0), pair, 0.0).astype(bf16), const], axis=1)
            for h in range(2)
        ],
        axis=0,
    )
    first = offset[0] + tile * q_tile
    top = jnp.full((8, 2 * q_tile), -jnp.inf, f32)
    for c in range(chunks):
        raw = dot_nt(keys[c * k_tile : (c + 1) * k_tile, :], weights)
        base = jnp.clip(c * k_tile - first, -(k_tile + LANES), q_tile + LANES)
        for b in range(k_tile // LANES):
            at = pl.multiple_of(origin - base - b * LANES, LANES)
            both = jnp.concatenate([strips[h, :, pl.ds(at, q_tile)] for h in range(2)], axis=1)
            part = raw[b * LANES : (b + 1) * LANES] + both
            scores[c * k_tile + b * LANES : c * k_tile + (b + 1) * LANES, :] = part
            top = jnp.maximum(top, jnp.max(part.reshape(LANES // 8, 8, 2 * q_tile), axis=0))
    top = jnp.max(top, axis=0, keepdims=True)
    totals = [jnp.zeros((HEAD_DIM + 16, q_tile), f32) for h in range(2)]
    for c in range(chunks):
        weight = jnp.exp(scores[c * k_tile : (c + 1) * k_tile, :] - top).astype(bf16)
        for h in range(2):
            totals[h] += dot_nn(
                values[h, :, c * k_tile : (c + 1) * k_tile], weight[:, h * q_tile : (h + 1) * q_tile]
            )
    mixed, pieces = [], []
    for h in range(2):
        total = totals[h][HEAD_DIM : HEAD_DIM + 1]
        mixed.append(totals[h][:HEAD_DIM] / total)
        pieces += list(three_pieces(-(top[:, h * q_tile : (h + 1) * q_tile] + jnp.log(total))))
    out_ref[0] = jnp.concatenate(mixed, axis=0).T.astype(bf16)
    rows = lax.broadcasted_iota(jnp.int32, (LANES, q_tile), 0)
    stats = jnp.where(rows == 6, 1.0, 0.0)
    for n, piece in enumerate(pieces):
        stats = jnp.where(rows == n, piece, stats)
    extra_ref[0, 0] = stats.T.astype(bf16)


def strip_width(q_tile, k_tile):
    return 2 * (q_tile + k_tile) + 2 * LANES


def attention_forward(qkv, kv, lengths, offset, vector, q_tile, k_tile, pairs):
    seqs, rows, _ = qkv.shape
    keys_of, values_of, k_at, v_at = kv
    slots = keys_of.shape[1]
    width = strip_width(q_tile, k_tile)
    grid = (seqs, pairs, rows // q_tile)
    return pl.pallas_call(
        functools.partial(forward_kernel, q_tile, k_tile),
        grid_spec=pltpu.PrefetchScalarGridSpec(
            num_scalar_prefetch=2,
            grid=grid,
            in_specs=[
                pl.BlockSpec((1, q_tile, LANES), lambda s, p, i, *_: (s, i, p)),
                pl.BlockSpec((1, slots, LANES), lambda s, p, i, *_: (s, 0, p + k_at)),
                pl.BlockSpec((1, slots, LANES), lambda s, p, i, *_: (s, 0, p + v_at)),
                pl.BlockSpec((1, 2, width), lambda s, p, i, *_: (p, 0, 0)),
            ],
            out_specs=[
                pl.BlockSpec((1, q_tile, LANES), lambda s, p, i, *_: (s, i, p)),
                pl.BlockSpec((1, 1, q_tile, LANES), lambda s, p, i, *_: (s, p, i, 0)),
            ],
            scratch_shapes=[
                pltpu.VMEM((slots, 2 * LANES), bf16),
                pltpu.VMEM((2, HEAD_DIM + 16, slots), bf16),
                pltpu.VMEM((2, LANES, width), f32),
                pltpu.VMEM((slots, 2 * q_tile), f32),
            ],
        ),
        out_shape=[
            jax.ShapeDtypeStruct((seqs, rows, pairs * LANES), bf16),
            jax.ShapeDtypeStruct((seqs, pairs, rows, LANES), bf16),
        ],
        compiler_params=pltpu.CompilerParams(vmem_limit_bytes=VMEM_LIMIT),
        name="attention_forward",
    )(lengths, offset, qkv, keys_of, values_of, vector)


def backward_kernel(
    q_tile, k_tile, lengths, offset, q_ref, k_ref, v_ref, a_ref, d_ref, extra_ref, bias_ref,
    dq_ref, dk_ref, dv_ref, bias_out,
    qa, ka, va, da, q_turned, d_turned, dk_acc, dv_acc, dq_acc, strips, sums,
):
    rows, slots = q_ref.shape[1], k_ref.shape[1]
    origin = q_tile + k_tile
    width = strips.shape[2]
    chunks = slots // k_tile
    length = lengths[pl.program_id(0)]
    lanes_k, lanes_q = lane_iota(slots), lane_iota(rows)
    keys, values = k_ref[0].astype(f32), v_ref[0].astype(f32)
    for h in range(2):
        mine = (lanes_k < HEAD_DIM) == (h == 0)
        ka[h, :, :LANES] = jnp.where(mine, keys, 0.0).astype(bf16)
        ka[h, :, LANES:] = key_extra(slots, length, 3 * h, 3 * h + 3)
        va[h, :, :LANES] = jnp.where(mine, values, 0.0).astype(bf16)
        va[h, :, LANES:] = ((lanes_k >= 3 * h) & (lanes_k < 3 * h + 3)).astype(f32).astype(bf16)
        strips[h] = skewed(bias_ref[0, h : h + 1, :], width)
    qa[:, :LANES] = q_ref[0]
    qa[:, LANES:] = extra_ref[0, 0]
    grads = d_ref[0].astype(f32)
    product = grads * a_ref[0].astype(f32)
    hi = product.astype(bf16)
    low = (product - hi.astype(f32)).astype(bf16)
    row_at = lax.broadcasted_iota(jnp.int32, (LANES, LANES), 0)
    lane_at = lax.broadcasted_iota(jnp.int32, (LANES, LANES), 1)
    pick = jnp.where((lane_at < 6) & ((row_at < HEAD_DIM) == (lane_at < 3)), -1.0, 0.0).astype(bf16)
    minus_dot = dot_nn(hi, pick) + dot_nn(low, pick)
    one, two, three = three_pieces(minus_dot)
    which = lanes_q % 3
    da[:, :LANES] = d_ref[0]
    da[:, LANES:] = jnp.where(which == 0, one, jnp.where(which == 1, two, three)).astype(bf16)
    q_turned[...] = q_ref[0].astype(f32).T.astype(bf16)
    d_turned[...] = grads.T.astype(bf16)
    dk_acc[...] = jnp.zeros_like(dk_acc)
    dv_acc[...] = jnp.zeros_like(dv_acc)
    sums[...] = jnp.zeros_like(sums)

    def one_tile(i, carried):
        r0 = pl.multiple_of(i * q_tile, q_tile)
        for c in range(chunks):
            base = jnp.clip(c * k_tile - offset[0] - r0, -(k_tile + LANES), q_tile + LANES)
            cols = slice(c * k_tile, (c + 1) * k_tile)
            dq = None
            for h in range(2):
                own = slice(h * HEAD_DIM, (h + 1) * HEAD_DIM)
                raw = dot_nt(qa[pl.ds(r0, q_tile), :], ka[h, cols, :])
                back = dot_nt(da[pl.ds(r0, q_tile), :], va[h, cols, :])
                probs, grad = [], []
                for b in range(q_tile // LANES):
                    at = pl.multiple_of(origin + base - b * LANES, LANES)
                    part = slice(b * LANES, (b + 1) * LANES)
                    p = jnp.exp(raw[part] + strips[h, :, pl.ds(at, k_tile)])
                    g = p * back[part]
                    sums[h, :, pl.ds(at, k_tile)] += g
                    probs.append(p.astype(bf16))
                    grad.append(g.astype(bf16))
                probs = jnp.concatenate(probs, axis=0)
                grad = jnp.concatenate(grad, axis=0)
                dv_acc[own, cols] += dot_nn(d_turned[own, pl.ds(r0, q_tile)], probs)
                dk_acc[own, cols] += dot_nn(q_turned[own, pl.ds(r0, q_tile)], grad)
                more = dot_nn(grad, ka[h, cols, :LANES])
                dq = more if dq is None else dq + more
            if c == 0:
                dq_acc[...] = dq
            else:
                dq_acc[...] += dq
        dq_ref[0, pl.ds(r0, q_tile), :] = dq_acc[...].astype(bf16)
        return carried

    lax.fori_loop(0, rows // q_tile, one_tile, 0)
    dk_ref[0] = dk_acc[...].T.astype(bf16)
    dv_ref[0] = dv_acc[...].T.astype(bf16)
    mirror = (row_at + lane_at == LANES - 1).astype(f32)
    for h in range(2):
        flipped = lax.dot_general(
            mirror, sums[h], (((1,), (0,)), ((), ())),
            precision=lax.Precision.HIGHEST, preferred_element_type=f32,
        )
        turned = pltpu.roll(flipped, width - (LANES - 1), 1, stride=1, stride_axis=0)
        bias_out[0, 0, h : h + 1, :] = jnp.sum(turned, axis=0, keepdims=True)


def attention_backward(qkv, kv, attended, grad, extra, lengths, offset, vector, q_tile, k_tile, pairs):
    seqs, rows, _ = qkv.shape
    keys_of, values_of, k_at, v_at = kv
    slots = keys_of.shape[1]
    width = strip_width(q_tile, k_tile)
    pair_of = lambda at: lambda s, p, *_: (s, 0, p + at)
    one = pl.Buffered(2)
    spec = lambda r, at: pl.BlockSpec((1, r, LANES), pair_of(at))
    return pl.pallas_call(
        functools.partial(backward_kernel, q_tile, k_tile),
        grid_spec=pltpu.PrefetchScalarGridSpec(
            num_scalar_prefetch=2,
            grid=(seqs, pairs),
            in_specs=[
                spec(rows, 0), spec(slots, k_at), spec(slots, v_at), spec(rows, 0), spec(rows, 0),
                pl.BlockSpec((1, 1, rows, LANES), lambda s, p, *_: (s, p, 0, 0)),
                pl.BlockSpec((1, 2, width), lambda s, p, *_: (p, 0, 0)),
            ],
            out_specs=[
                spec(rows, 0), spec(slots, 0), spec(slots, 0),
                pl.BlockSpec((1, 1, 2, width), lambda s, p, *_: (s, p, 0, 0)),
            ],
            scratch_shapes=[
                pltpu.VMEM((rows, 2 * LANES), bf16),
                pltpu.VMEM((2, slots, 2 * LANES), bf16),
                pltpu.VMEM((2, slots, 2 * LANES), bf16),
                pltpu.VMEM((rows, 2 * LANES), bf16),
                pltpu.VMEM((LANES, rows), bf16),
                pltpu.VMEM((LANES, rows), bf16),
                pltpu.VMEM((LANES, slots), f32),
                pltpu.VMEM((LANES, slots), f32),
                pltpu.VMEM((q_tile, LANES), f32),
                pltpu.VMEM((2, LANES, width), f32),
                pltpu.VMEM((2, LANES, width), f32),
            ],
        ),
        out_shape=[
            jax.ShapeDtypeStruct((seqs, rows, pairs * LANES), bf16),
            jax.ShapeDtypeStruct((seqs, slots, pairs * LANES), bf16),
            jax.ShapeDtypeStruct((seqs, slots, pairs * LANES), bf16),
            jax.ShapeDtypeStruct((seqs, pairs, 2, width), f32),
        ],
        compiler_params=pltpu.CompilerParams(vmem_limit_bytes=VMEM_LIMIT),
        name="attention_backward",
    )(lengths, offset, qkv, keys_of, values_of, attended, grad, extra, vector)


THRESHOLDS = (12, 16, 23, 32, 46, 64, 91)


def bucket_of(offsets):
    distance = jnp.abs(offsets)
    larger = jnp.full(offsets.shape, 8, jnp.int32)
    for threshold in THRESHOLDS:
        larger = larger + (distance >= threshold).astype(jnp.int32)
    nearby = jnp.where(distance < 8, distance, larger)
    return jnp.where(offsets > 0, 16, 0).astype(jnp.int32) + nearby


def bias_onehot(q_tile, k_tile, flip):
    width = strip_width(q_tile, k_tile)
    lane = jnp.arange(width, dtype=jnp.int32)
    lane = jnp.where(lane >= width - LANES, lane - width, lane)
    offs = lane - (q_tile + k_tile)
    if flip:
        offs = -offs
    return (bucket_of(offs)[:, None] == jnp.arange(32, dtype=jnp.int32)[None, :]).astype(f32)


from jax.sharding import PartitionSpec as P

D = 768
HEADS = 12
PAIRS = HEADS // 2
FF = 2048
BUCKETS = 32
EPSILON = 1e-06
PRECISE = lax.Precision.HIGHEST
BOTH = ("dp", "fsdp")
FF_CHUNK = 512


def rms_factor(values):
    return lax.rsqrt(jnp.mean(values * values, axis=-1, keepdims=True) + EPSILON)


def norm_back(grad_normed, values, factor, gain):
    scaled = grad_normed * gain
    return factor * scaled - values * (factor * factor * factor) * jnp.mean(
        scaled * values, axis=-1, keepdims=True
    )


def project_kernel(x_ref, w_ref, gain_ref, out_ref):
    x = x_ref[...].astype(f32)
    normed = (x * rms_factor(x) * gain_ref[...]).astype(bf16)
    for n in range(3):
        part = slice(n * D, (n + 1) * D)
        out_ref[:, part] = dot_nt(normed, w_ref[:, part]).astype(bf16)


def project(x, weights, gain, tile):
    tokens = x.shape[0]
    return pl.pallas_call(
        project_kernel,
        grid=(tokens // tile,),
        in_specs=[
            pl.BlockSpec((tile, D), lambda i: (i, 0)),
            pl.BlockSpec((D, 3 * D), lambda i: (0, 0)),
            pl.BlockSpec((1, D), lambda i: (0, 0)),
        ],
        out_specs=pl.BlockSpec((tile, 3 * D), lambda i: (i, 0)),
        out_shape=jax.ShapeDtypeStruct((tokens, 3 * D), bf16),
        compiler_params=pltpu.CompilerParams(vmem_limit_bytes=VMEM_LIMIT),
        name="project",
    )(x, weights, gain)


def ffn_kernel(
    tile, rows, away, lengths, place, x_ref, a_ref, c_ref, wod_ref, wgu_ref, gain_ref,
    own_ref, away_ref, gh_ref, ga_ref, dod_out, dgu_out, gain_out,
    dod, dgu, gain_acc, hidden_ref, nf_ref, seed_ref, out_acc, dnf_acc, sems,
):
    step = pl.program_id(0)
    steps = pl.num_programs(0)
    at = tile_at(step, place, away, steps)

    @pl.when(step == 0)
    def _():
        dod[...] = jnp.zeros_like(dod)
        dgu[...] = jnp.zeros_like(dgu)
        gain_acc[...] = jnp.zeros_like(gain_acc)

    per_seq = rows // tile
    seq = at // per_seq
    first = place[1] + (at - seq * per_seq) * tile
    position = first + lax.broadcasted_iota(jnp.int32, (tile, D), 0)
    hidden_ref[...] = x_ref[...].astype(f32) + dot_nt(a_ref[...], wod_ref[:, :D])
    hidden = hidden_ref[...]
    factor = rms_factor(hidden)
    gain = gain_ref[...]
    nf_ref[...] = (hidden * factor * gain).astype(bf16)
    seed_ref[...] = jnp.where(position < lengths[seq], c_ref[...].astype(f32), 0.0).astype(bf16)
    out_acc[...] = hidden
    dnf_acc[...] = jnp.zeros_like(dnf_acc)

    def chunk(c, carried):
        f0 = pl.multiple_of(c * FF_CHUNK, FF_CHUNK)
        ff = pl.ds(f0, FF_CHUNK)
        down = pl.ds(pl.multiple_of(D + f0, LANES), FF_CHUNK)
        nf, seed = nf_ref[...], seed_ref[...]
        gate = dot_nt(nf, wgu_ref[ff, :D])
        up = dot_nt(nf, wgu_ref[ff, D:])
        back = dot_nn(seed, wod_ref[:, down])
        square = gate * gate
        root = 0.7978845608028654
        tanh = jnp.tanh(gate * (root + (root * 0.044715) * square))
        half = 0.5 + 0.5 * tanh
        active = gate * half
        slope = half + (0.5 * gate) * (1.0 - tanh * tanh) * (root + (3.0 * root * 0.044715) * square)
        activated = (active * up).astype(bf16)
        grad_gate = (back * up * slope).astype(bf16)
        grad_up = (back * active).astype(bf16)
        out_acc[...] += dot_nt(activated, wod_ref[:, down])
        dnf_acc[...] += dot_nn(grad_gate, wgu_ref[ff, :D]) + dot_nn(grad_up, wgu_ref[ff, D:])
        dod[:, down] += dot_tn(seed, activated)
        dgu[ff, :D] += dot_tn(grad_gate, nf)
        dgu[ff, D:] += dot_tn(grad_up, nf)
        return carried

    lax.fori_loop(0, FF // FF_CHUNK, chunk, 0)
    hidden = hidden_ref[...]
    factor = rms_factor(hidden)
    dnf = dnf_acc[...]
    gain_acc[...] += jnp.sum(dnf * hidden * factor, axis=0, keepdims=True)
    grad_hidden = seed_ref[...].astype(f32) + norm_back(dnf, hidden, factor, gain)
    gh_ref[...] = grad_hidden
    branch = grad_hidden.astype(bf16)
    ga_ref[...] = dot_nn(branch, wod_ref[:, :D]).astype(bf16)
    dod[:, :D] += dot_tn(branch, a_ref[...])

    @pl.when(step < away)
    def _():
        away_ref[...] = out_acc[...].astype(bf16)

    @pl.when(step >= away)
    def _():
        own_ref[...] = out_acc[...]

    @pl.when(step == steps - 1)
    def _():
        gain_out[...] = gain_acc[...]
        one = pltpu.make_async_copy(dod, dod_out, sems.at[0])
        two = pltpu.make_async_copy(dgu, dgu_out, sems.at[1])
        one.start()
        two.start()
        one.wait()
        two.wait()


def tile_at(step, place, away, steps):
    if away == 0:
        return step
    return (step + away * (1 - place[0])) % steps


def away_index(away):
    return lambda i, *_: (jnp.minimum(i, max(away, 1) - 1), 0)


def own_index(away):
    return lambda i, *_: (jnp.maximum(i - away, 0), 0)


def ffn(x, attended, cotangent, wod, wgu, gain, lengths, place, tile, rows, away):
    tokens = x.shape[0]
    steps = tokens // tile
    by_tile = lambda i, lengths, place: (tile_at(i, place, away, steps), 0)
    whole = lambda i, *_: (0, 0)
    single = pl.Buffered(1)
    return pl.pallas_call(
        functools.partial(ffn_kernel, tile, rows, away),
        grid_spec=pltpu.PrefetchScalarGridSpec(
            num_scalar_prefetch=2,
            grid=(steps,),
            in_specs=[
                pl.BlockSpec((tile, D), by_tile),
                pl.BlockSpec((tile, D), by_tile),
                pl.BlockSpec((tile, D), by_tile),
                pl.BlockSpec((D, D + FF), whole, pipeline_mode=single),
                pl.BlockSpec((FF, 2 * D), whole, pipeline_mode=single),
                pl.BlockSpec((1, D), whole),
            ],
            out_specs=[
                pl.BlockSpec((tile, D), own_index(away)),
                pl.BlockSpec((tile, D), away_index(away)),
                pl.BlockSpec((tile, D), by_tile),
                pl.BlockSpec((tile, D), by_tile),
                pl.BlockSpec(memory_space=pl.ANY),
                pl.BlockSpec(memory_space=pl.ANY),
                pl.BlockSpec((1, D), whole),
            ],
            scratch_shapes=[
                pltpu.VMEM((D, D + FF), f32),
                pltpu.VMEM((FF, 2 * D), f32),
                pltpu.VMEM((1, D), f32),
                pltpu.VMEM((tile, D), f32),
                pltpu.VMEM((tile, D), bf16),
                pltpu.VMEM((tile, D), bf16),
                pltpu.VMEM((tile, D), f32),
                pltpu.VMEM((tile, D), f32),
                pltpu.SemaphoreType.DMA((2,)),
            ],
        ),
        out_shape=[
            jax.ShapeDtypeStruct((tokens - away * tile, D), f32),
            jax.ShapeDtypeStruct((max(away, 1) * tile, D), bf16),
            jax.ShapeDtypeStruct((tokens, D), f32),
            jax.ShapeDtypeStruct((tokens, D), bf16),
            jax.ShapeDtypeStruct((D, D + FF), f32),
            jax.ShapeDtypeStruct((FF, 2 * D), f32),
            jax.ShapeDtypeStruct((1, D), f32),
        ],
        compiler_params=pltpu.CompilerParams(vmem_limit_bytes=VMEM_LIMIT),
        name="ffn",
    )(lengths, place, x, attended, cotangent, wod, wgu, gain)


def finish_kernel(
    away, place, x_ref, dq_ref, dk_ref, dv_ref, gh_ref, w_ref, gain_ref, gain_two_ref,
    own_ref, away_ref, dw_ref, acc,
):
    step = pl.program_id(0)

    @pl.when(step == 0)
    def _():
        dw_ref[...] = jnp.zeros_like(dw_ref)
        acc[...] = jnp.zeros_like(acc)

    x = x_ref[...].astype(f32)
    factor = rms_factor(x)
    gain = gain_ref[...]
    normed = (x * factor * gain).astype(bf16)
    grad_normed = None
    for n, ref in enumerate((dq_ref, dk_ref, dv_ref)):
        part = slice(n * D, (n + 1) * D)
        grad = ref[...]
        dw_ref[:, part] += dot_tn(grad, normed)
        more = dot_nn(grad, w_ref[:, part])
        grad_normed = more if grad_normed is None else grad_normed + more
    acc[...] += jnp.sum(grad_normed * x * factor, axis=0, keepdims=True)
    grad_x = gh_ref[...] + norm_back(grad_normed, x, factor, gain)

    @pl.when(step < away)
    def _():
        away_ref[...] = grad_x.astype(bf16)

    @pl.when(step >= away)
    def _():
        own_ref[...] = grad_x

    @pl.when(step == pl.num_programs(0) - 1)
    def _():
        rows = lax.broadcasted_iota(jnp.int32, (LANES, D), 0)
        both = jnp.where(rows == 0, acc[...], jnp.where(rows == 1, gain_two_ref[...], 0.0))
        dw_ref[:, 3 * D :] = both.T


def finish(x, dq, dk, dv, gh, weights, gain, gain_two_grad, place, tile, away):
    tokens = x.shape[0]
    steps = tokens // tile
    by_tile = lambda i, place: (tile_at(i, place, away, steps), 0)
    whole = lambda i, *_: (0, 0)
    block = pl.BlockSpec((tile, D), by_tile)
    return pl.pallas_call(
        functools.partial(finish_kernel, away),
        grid_spec=pltpu.PrefetchScalarGridSpec(
            num_scalar_prefetch=1,
            grid=(steps,),
            in_specs=[
                block, block, block, block, block,
                pl.BlockSpec((D, 3 * D), whole),
                pl.BlockSpec((1, D), whole),
                pl.BlockSpec((1, D), whole),
            ],
            out_specs=[
                pl.BlockSpec((tile, D), own_index(away)),
                pl.BlockSpec((tile, D), away_index(away)),
                pl.BlockSpec((D, 3 * D + LANES), whole),
            ],
            scratch_shapes=[pltpu.VMEM((1, D), f32)],
        ),
        out_shape=[
            jax.ShapeDtypeStruct((tokens - away * tile, D), f32),
            jax.ShapeDtypeStruct((max(away, 1) * tile, D), bf16),
            jax.ShapeDtypeStruct((D, 3 * D + LANES), f32),
        ],
        compiler_params=pltpu.CompilerParams(vmem_limit_bytes=VMEM_LIMIT),
        name="finish",
    )(place, x, dq, dk, dv, gh, weights, gain, gain_two_grad)


def swap_in(block, side):
    mine = lax.dynamic_index_in_dim(block, side, 0, keepdims=False)
    other = lax.dynamic_index_in_dim(block, 1 - side, 0, keepdims=False)
    come = lax.ppermute(other, "fsdp", [(0, 1), (1, 0)])
    return jnp.where(side == 0, jnp.concatenate([mine, come]), jnp.concatenate([come, mine]))


def swap_out(own, away, side):
    come = lax.ppermute(away, "fsdp", [(0, 1), (1, 0)]).astype(f32)
    return jnp.where(side == 0, jnp.stack([own, come]), jnp.stack([come, own]))


def turned(weight):
    return weight.astype(bf16).T


def per_device(
    sides, inputs, cotangent, lengths, w_query, w_key, w_value, w_out, w_gate, w_up, w_down,
    gain_attn, gain_ffn, bias_table,
):
    seqs, own_rows, _ = inputs.shape
    slots = own_rows * sides
    side = lax.axis_index("fsdp")
    share = gain_attn.shape[0]
    gains = jnp.pad(jnp.stack([gain_attn, gain_ffn], axis=1).astype(bf16), ((0, 0), (0, LANES - 2)))
    packed = jnp.concatenate([turned(w_query), turned(w_key), turned(w_value), gains], axis=1)
    wqkv = lax.all_gather(packed, BOTH, axis=0, tiled=True)
    gain_rows = wqkv[:, 3 * D : 3 * D + 2].astype(f32).T
    wod = lax.all_gather(jnp.concatenate([turned(w_out), turned(w_down)], axis=1), BOTH, axis=0, tiled=True)
    wgu = lax.all_gather(jnp.concatenate([turned(w_gate), turned(w_up)], axis=1), BOTH, axis=0, tiled=True)
    swap = seqs == 2 and sides == 2
    if swap:
        x, seed = swap_in(inputs, side), swap_in(cotangent, side)
        lengths = lax.dynamic_slice_in_dim(lengths, side, 1)
        seqs, rows, first = 1, slots, jnp.zeros((), jnp.int32)
    else:
        x, seed = inputs.reshape(-1, D), cotangent.reshape(-1, D)
        rows, first = own_rows, side * own_rows
    tile = min(512, own_rows)
    away = own_rows // tile if swap else 0
    place = jnp.stack([side, first]).astype(jnp.int32)
    origin = place[1:]
    one_hot = bias_onehot(tile, 512, False)
    vector = jnp.dot(one_hot, bias_table, precision=PRECISE).T.reshape(PAIRS, 2, -1)
    flipped = jnp.dot(bias_onehot(tile, 512, True), bias_table, precision=PRECISE).T.reshape(PAIRS, 2, -1)

    qkv = project(x, wqkv, gain_rows[0:1], tile).reshape(seqs, rows, 3 * D)
    if rows < slots:
        kv = lax.all_gather(qkv[:, :, D:], "fsdp", axis=1, tiled=True)
        sources = (kv, kv, 0, PAIRS)
    else:
        sources = (qkv, qkv, PAIRS, 2 * PAIRS)
    attended, extra = attention_forward(qkv, sources, lengths, origin, flipped, tile, 512, PAIRS)
    own, away_out, grad_hidden, grad_attended, dod, dgu, gain_two = ffn(
        x, attended.reshape(-1, D), seed, wod, wgu, gain_rows[1:2], lengths, place, tile, rows, away
    )
    if swap:
        output = swap_out(own, away_out, side)
    else:
        output = own.reshape(seqs, rows, D)
    out_down = lax.psum_scatter(dod.astype(bf16), BOTH, scatter_dimension=0, tiled=True).astype(f32)
    gate_up = lax.psum_scatter(dgu.astype(bf16), BOTH, scatter_dimension=0, tiled=True).astype(f32)
    dq, dk, dv, strips = attention_backward(
        qkv, sources, attended, grad_attended.reshape(seqs, rows, D), extra, lengths, origin, vector,
        tile, 512, PAIRS,
    )
    if rows < slots:
        dk = lax.psum_scatter(dk, "fsdp", scatter_dimension=1, tiled=True)
        dv = lax.psum_scatter(dv, "fsdp", scatter_dimension=1, tiled=True)
    diagonals = jnp.sum(strips, axis=0).reshape(HEADS, -1)
    table = lax.psum(jnp.dot(diagonals, one_hot, precision=PRECISE).T, BOTH)
    flat = lambda a: a.reshape(-1, D)
    own, away_grad, dw = finish(
        x, flat(dq), flat(dk), flat(dv), grad_hidden, wqkv, gain_rows[0:1], gain_two, place, tile, away
    )
    if swap:
        grad_inputs = swap_out(own, away_grad, side)
    else:
        grad_inputs = own.reshape(seqs, rows, D)
    query_key = lax.psum_scatter(dw.astype(bf16), BOTH, scatter_dimension=0, tiled=True).astype(f32)
    return (
        output,
        grad_inputs,
        query_key[:, :D].T,
        query_key[:, D : 2 * D].T,
        query_key[:, 2 * D : 3 * D].T,
        out_down[:, :D].T,
        gate_up[:, :D].T,
        gate_up[:, D:].T,
        out_down[:, D:].T,
        query_key[:, 3 * D],
        query_key[:, 3 * D + 1],
        table,
    )


def solution(mesh):
    tokens = P("dp", "fsdp", None)
    columns = P(None, BOTH)
    return jax.shard_map(
        functools.partial(per_device, mesh.shape["fsdp"]),
        mesh=mesh,
        in_specs=(tokens, tokens, P("dp")) + (columns,) * 7 + (P(BOTH), P(BOTH), P()),
        out_specs=(tokens, tokens) + (columns,) * 7 + (P(BOTH), P(BOTH), P()),
        check_vma=False,
    )
```

time: 7470 us -> 898 us (0.12)
  local copies, waits for them, and re-layouts: 5100 us -> 11.9 us
  matrix products: 878 us -> 4.16 us
  waiting for transfers between devices: 912 us -> 265 us
  Pallas kernels: 0 us -> 431 us
  other arithmetic: 396 us -> 47.8 us
    while x156 -> x0, local copies, waits for them, and re-layouts: 2730 us -> none
    reshape x38 -> x3, local copies, waits for them, and re-layouts: 1320 us -> 1.54 us  [the longest x1 0.74 us: per_device(): jnp.dot(bias_onehot(tile, 512, True), bias_table, precision=PRECISE)]
    dot_general x128 -> x3, matrix products: 878 us -> 4.16 us  [the longest x1 1.76 us: per_device(): jnp.dot(bias_onehot(tile, 512, True), bias_table, precision=PRECISE)]
    reduce_scatter x11 -> x2, waiting for transfers between devices: 743 us -> 197 us  [the longest x1 118 us: per_device(): lax.psum_scatter(dgu.astype(bf16), BOTH, scatter_dimension=0, tiled=True)]
    pallas_call x0 -> x5, Pallas kernels: none -> 431 us  [the longest x1 190 us: attention_backward(): pl.pallas_call(functools.partial(backward_kernel, q_tile, k_tile), grid_s...]
    slice x27 -> x2, local copies, waits for them, and re-layouts: 418 us -> 1.3 us  [the longest x1 0.7 us: per_device(): query_key[:, 3 * D + 1]]
    broadcast_in_dim x48 -> x0, local copies, waits for them, and re-layouts: 267 us -> none  [skew_expand(): jnp.broadcast_to(vector[:, None, :], (head_count, row_count, full_width +...]
    pad x12 -> x0, local copies, waits for them, and re-layouts: 219 us -> none  [skew_reduce(): jnp.pad(padded, ((0, 0), (0, row_count)))]
  transfers between devices with their start and end apart: 22 -> 10, of which waited for: 13 -> 4; matrix products, arithmetic and copies ran while one was open for 56% -> 6% of each run, Pallas kernels for 0% -> 13%
where the time goes in v1:
time: 898 us; the launch traced here: 890 us
  Pallas kernels  431 us (48%)
  waiting for transfers between devices  265 us (30%)
  blocking collectives  111 us (12%)
  other arithmetic  47.8 us (5%)
  between operations  14.7 us (2%)
  local copies, waits for them, and re-layouts  11.9 us (1%)
    pallas_call x1, Pallas kernels, attention_backward(): pl.pallas_call(functools.partial(backward_kernel, q_tile, k_tile), grid_s...  190 us
    reduce_scatter x1, waiting for transfers between devices, per_device(): lax.psum_scatter(dgu.astype(bf16), BOTH, scatter_dimension=0, tiled=True)  118 us
    psum x1, blocking collectives, per_device(): table = lax.psum(jnp.dot(diagonals, one_hot, precision=PRECISE).T, BOTH)  111 us
    pallas_call x1, Pallas kernels, attention_forward(): pl.pallas_call(functools.partial(forward_kernel, q_tile, k_tile), grid_sp...  103 us
    pallas_call x1, Pallas kernels, ffn(): pl.pallas_call(functools.partial(ffn_kernel, tile, rows, away), grid_spec...  98.8 us
    reduce_scatter x1, waiting for transfers between devices, per_device(): lax.psum_scatter(dod.astype(bf16), BOTH, scatter_dimension=0, tiled=True)  79.5 us
    ppermute x2, waiting for transfers between devices, swap_in(): come = lax.ppermute(other, 'fsdp', [(0, 1), (1, 0)])  67.4 us
    pallas_call x1, Pallas kernels, finish(): pl.pallas_call(functools.partial(finish_kernel, away), grid_spec=pltpu.Pr...  27.6 us
  transfers between devices with their start and end apart: 10, of which 4 were waited for; matrix products, arithmetic and copies ran while one was open for 6% of the time, Pallas kernels for 13%

profile of v1, /device:TPU:0, one launch (start us, length us, event | category | flops | bytes accessed | tf_op | source)
XLA Modules:
  0.0 890.5 jit_solution(6470556987886274870)
XLA Ops:
  15.0 3.4 dynamic-slice_bitcast_fusion.3
  18.4 3.0 collective-permute-start
  23.3 1.8 convolution_bitcast_fusion.1
  25.9 1.8 convolution_bitcast_fusion
  28.9 30.9 %collective-permute-done = bf16[1024,768]{1,0:T(8,128)(2,1)} collective-permute-done((bf16[1024,768]{1,0:T(8,128)(2,1)}, bf16[1024,768]{1,0:T(8,128)(2,1)}, u32[]{:S(2)}, u32[]{:S(2)}) %collective-permute-start) | collective-permute-done | bytes 1572896 | tf_op jit(solution)/shard_map/ppermute | solution.py:576
  59.9 3.6 maximum_select_fusion.2.x_ref
  63.5 36.4 %collective-permute-done.1 = bf16[1024,768]{1,0:T(8,128)(2,1)} collective-permute-done((bf16[1024,768]{1,0:T(8,128)(2,1)}, bf16[1024,768]{1,0:T(8,128)(2,1)}, u32[]{:S(2)}, u32[]{:S(2)}) %collective-permute-start.1) | collective-permute-done | bytes 1572896 | tf_op jit(solution)/shard_map/ppermute | solution.py:576
  99.9 3.6 maximum_select_fusion.3.c_ref
  105.2 12.2 %project.1 = bf16[2048,2304]{1,0:T(8,128)(2,1)} custom-call(bf16[2048,768]{1,0:T(8,128)(2,1)} %maximum_select_fusion.2.x_ref, bf16[768,2432]{1,0:T(8,128)(2,1)} %all-gather.4.cloned.1.call-done.w_ref, f32[1,768]{1,0:T(1,128)} %get-tuple-element.56.gain_ref), custom_call_target="tpu_custom_call" | custom-call | tf_op jit(solution)/shard_map/project/pallas_call | solution.py:334
  117.4 102.6 %attention_forward.1 = (bf16[1,2048,768]{2,1,0:T(8,128)(2,1)}, bf16[1,6,2048,128]{3,2,1,0:T(8,128)(2,1)}) custom-call(s32[1]{0:T(128)} %dynamic_slice.16.lengths, s32[1]{0:T(128)} %constant.21.clone.1.offset, bf16[1,2048,2304]{2,1,0:T(8,128)(2,1)} %bitcast.63, bf16[1,2048,2304]{2,1,0:T(8,128)(2,1)} %bitcast.64, bf16[1,2048,2304]{2,1,0:T(8,128)(2,1)} %bitcast.65, ...), custom_call_target="tpu_custom_call" | custom-call | tf_op jit(solution)/shard_map/attention_forward/pallas_call | solution.py:116
  220.0 98.8 %ffn.1 = (f32[1024,768]{1,0:T(8,128)}, bf16[1024,768]{1,0:T(8,128)(2,1)}, f32[2048,768]{1,0:T(8,128)}, bf16[2048,768]{1,0:T(8,128)(2,1)}, f32[768,2816]{1,0:T(8,...) custom-call(s32[1]{0:T(128)} %dynamic_slice.16.lengths, s32[2]{0:T(128)} %pad_add_fusion.place, ...), custom_call_target="tpu_custom_call" | custom-call | tf_op jit(solution)/shard_map/ffn/pallas_call | solution.py:451
  318.9 189.6 %attention_backward.1 = (bf16[1,2048,768]{2,1,0:T(8,128)(2,1)}, bf16[1,2048,768]{2,1,0:T(8,128)(2,1)}, bf16[1,2048,768]{2,1,0:T(8,128)(2,1)}, f32[1,6,2,2304]{3,2,1,0:T(2,128)}) custom-call(s32[1]{0:T(128)} %dynamic_slice.16.lengths, s32[1]{0:T(128)} %constant.21.clone.1.offset, bf16[1,2048,2304]{2,1,0:T(8,128)(2,1)} %bitcast.66, ...), custom_call_target="tpu_custom_call" | custom-call | tf_op jit(solution)/shard_map/attention_backward/pallas_call | solution.py:239
  508.5 27.6 %finish.1 = (f32[1024,768]{1,0:T(8,128)}, bf16[1024,768]{1,0:T(8,128)(2,1)}, f32[768,2432]{1,0:T(8,128)}) custom-call(s32[2]{0:T(128)} %pad_add_fusion.place, bf16[2048,768]{1,0:T(8,128)(2,1)} %maximum_select_fusion.2.x_ref, bf16[2048,768]{1,0:T(8,128)(2,1)} %bitcast.72, bf16[2048,768]{1,0:T(8,128)(2,1)} %bitcast.73, bf16[2048,768]{1,0:T(8,128)(2,1)} %bitcast.74, ...), custom_call_target="tpu_custom_call" | custom-call | tf_op jit(solution)/shard_map/finish/pallas_call | solution.py:545
  536.1 5.4 convert_element_type.180
  541.5 5.9 convert_element_type.182
  547.5 8.2 convert_element_type.184
  555.7 1.8 collective-permute-start.3
  558.5 111.2 %psum.7 = f32[32,12]{0,1:T(8,128)} all-reduce(f32[32,12]{0,1:T(8,128)S(1)} %fusion), channel_id=1, replica_groups=mesh['dp'=16,'fsdp'=2] {'dp','fsdp'}, use_global_device_ids=true, to_apply=%region_3.4 | all-reduce | flops 384 | bytes 3072 | tf_op jit(solution)/shard_map/psum | solution.py:643
  669.8 1.7 bitcast_convert_fusion
  671.4 2.9 maximum_select_fusion.1
  674.4 1.8 bitcast_convert_fusion.1
  676.8 2.9 maximum_select_fusion
  682.1 79.5 %reduce-scatter.6.cloned.1.call-done = bf16[24,2816]{1,0:T(8,128)(2,1)} async-done(((bf16[768,2816]{1,0:T(8,128)(2,1)}), bf16[24,2816]{1,0:T(8,128)(2,1)}) %reduce-scatter.6.cloned.1.call-update) | async-done | bytes 135184 | tf_op jit(solution)/shard_map/reduce_scatter | solution.py:633
  763.8 117.6 %reduce-scatter.8.cloned.1.call-done = bf16[64,1536]{1,0:T(8,128)(2,1)} async-done(((bf16[2048,1536]{1,0:T(8,128)(2,1)}), bf16[64,1536]{1,0:T(8,128)(2,1)}) %reduce-scatter.8.cloned.1.call-update) | async-done | bytes 196624 | tf_op jit(solution)/shard_map/reduce_scatter | solution.py:634
  (65 shorter events, 21.6 us)
Async XLA Ops:
  7.2 16.1 %copy-start = (f32[32,12]{0,1:T(8,128)S(1)}, f32[32,12]{0,1:T(8,128)}, u32[]{:S(2)}) copy-start(f32[32,12]{0,1:T(8,128)} %param.25) | copy-start | bytes 4612
  7.2 96.3 %all-gather.4.cloned.1.call-start = ((), (), s32[]{:S(2)}) async-start(), calls=%async_computation.3 | async-start | bytes 3852288 | tf_op jit(solution)/shard_map/all_gather | solution.py:599
  10.5 209.5 %all-gather.6.cloned.1.call-start = ((), (), s32[]{:S(2)}) async-start(), calls=%async_computation.4 | async-start | bytes 4460544 | tf_op jit(solution)/shard_map/all_gather | solution.py:601
  13.1 206.9 %all-gather.8.cloned.1.call-start = ((), (), s32[]{:S(2)}) async-start(), calls=%async_computation.5 | async-start | bytes 6488064 | tf_op jit(solution)/shard_map/all_gather | solution.py:602
  14.9 664.8 %reduce-scatter.10.cloned.1.call-start = ((), (), s32[]{:S(2)}) async-start(), calls=%async_computation.8 | async-start | bytes 3852288
  15.0 6.4 copy-start.2
  18.4 4.3 copy-start.6
  18.4 41.5 %collective-permute-start = (bf16[1024,768]{1,0:T(8,128)(2,1)}, bf16[1024,768]{1,0:T(8,128)(2,1)}, u32[]{:S(2)}, u32[]{:S(2)}) collective-permute-start(bf16[1024,768]{1,0:T(8,128)(2,1)} %get-tuple-element.49), channel_id=1, source_target_pairs={{0,1},{1,0},{2,3},{3,2},{4,5},{5,4},{6,7},{7,6},{8,9},{9,8},{10,11... | collective-permute-start | bytes 4718600 | tf_op jit(solution)/shard_map/ppermute | solution.py:576
  22.7 77.2 %collective-permute-start.1 = (bf16[1024,768]{1,0:T(8,128)(2,1)}, bf16[1024,768]{1,0:T(8,128)(2,1)}, u32[]{:S(2)}, u32[]{:S(2)}) collective-permute-start(bf16[1024,768]{1,0:T(8,128)(2,1)} %get-tuple-element.47), channel_id=1, source_target_pairs={{0,1},{1,0},{2,3},{3,2},{4,5},{5,4},{6,7},{7,6},{8,9},{9,8},{10,11... | collective-permute-start | bytes 4718600 | tf_op jit(solution)/shard_map/ppermute | solution.py:576
  541.5 220.1 %reduce-scatter.6.cloned.1.call-start = ((), (), s32[]{:S(2)}) async-start(), calls=%async_computation.6 | async-start | bytes 4460544 | tf_op jit(solution)/shard_map/reduce_scatter | solution.py:633
  547.4 334.0 %reduce-scatter.8.cloned.1.call-start = ((), (), s32[]{:S(2)}) async-start(), calls=%async_computation.7 | async-start | bytes 6488064 | tf_op jit(solution)/shard_map/reduce_scatter | solution.py:634
  555.7 2.1 copy-start.5
  555.7 115.7 %copy-start.4 = (f32[1024,768]{1,0:T(8,128)S(1)}, f32[1024,768]{1,0:T(8,128)}, u32[]{:S(2)}) copy-start(f32[1024,768]{1,0:T(8,128)} %get-tuple-element.38) | copy-start | bytes 9437188
  555.7 114.0 %collective-permute-start.3 = (bf16[1024,768]{1,0:T(8,128)(2,1)}, bf16[1024,768]{1,0:T(8,128)(2,1)}, u32[]{:S(2)}, u32[]{:S(2)}) collective-permute-start(bf16[1024,768]{1,0:T(8,128)(2,1)} %get-tuple-element.39), channel_id=1, source_target_pairs={{0,1},{1,0},{2,3},{3,2},{4,5},{5,4},{6,7},{7,6},{8,9},{9,8},{10,11... | collective-permute-start | bytes 4718600 | tf_op jit(solution)/shard_map/ppermute | solution.py:581
  557.5 116.9 %collective-permute-start.2 = (bf16[1024,768]{1,0:T(8,128)(2,1)}, bf16[1024,768]{1,0:T(8,128)(2,1)}, u32[]{:S(2)}, u32[]{:S(2)}) collective-permute-start(bf16[1024,768]{1,0:T(8,128)(2,1)} %get-tuple-element.30), channel_id=1, source_target_pairs={{0,1},{1,0},{2,3},{3,2},{4,5},{5,4},{6,7},{7,6},{8,9},{9,8},{10,11... | collective-permute-start | bytes 4718600 | tf_op jit(solution)/shard_map/ppermute | solution.py:581
  674.4 2.5 copy-start.3
  676.8 206.3 %copy-start.1 = (f32[32,12]{0,1:T(8,128)S(1)}, f32[32,12]{0,1:T(8,128)}, u32[]{:S(2)}) copy-start(f32[32,12]{0,1:T(8,128)} %param.25) | copy-start | bytes 4612
Sparse Core Ops, SparseCore 0:
  11.4 70.3 all-gather.3
  85.3 61.2 all-gather.5
  150.1 67.9 all-gather.7
  541.6 109.9 reduce-scatter.9
  657.0 104.5 reduce-scatter.5
  768.0 113.4 reduce-scatter.7

commit v2 on v1

--- a/solution.py
+++ b/solution.py
@@ -5,8 +5,13 @@
 
 HEAD_DIM = 64
 LANES = 128
+SUB_TILE = 256
 MASKED = -1000000000.0
 VMEM_LIMIT = 60 << 20
+
+
+def cost(microseconds):
+    return pl.CostEstimate(flops=int(1.1e9 * microseconds), bytes_accessed=1 << 20, transcendentals=0)
 f32, bf16 = jnp.float32, jnp.bfloat16
 
 
@@ -45,7 +50,7 @@
     return jnp.where(lanes == 6, masked, ones).astype(bf16)
 
 
-def forward_kernel(q_tile, k_tile, lengths, offset, q_ref, k_ref, v_ref, bias_ref, out_ref, extra_ref, keys, values, strips, scores):
+def forward_kernel(q_tile, k_tile, lengths, offset, q_ref, k_ref, v_ref, bias_ref, out_ref, extra_ref, keys, values, strips, scores_even, scores_odd):
     slots = k_ref.shape[1]
     tile = pl.program_id(2)
     origin = q_tile + k_tile
@@ -64,37 +69,41 @@
     lanes = lane_iota(q_tile)
     pair = q_ref[0].astype(f32)
     const = jnp.where(lanes == 6, 1.0, 0.0).astype(bf16)
-    weights = jnp.concatenate(
-        [
-            jnp.concatenate([jnp.where((lanes < HEAD_DIM) == (h == 0), pair, 0.0).astype(bf16), const], axis=1)
-            for h in range(2)
-        ],
-        axis=0,
-    )
+    weights = [
+        jnp.concatenate([jnp.where((lanes < HEAD_DIM) == (h == 0), pair, 0.0).astype(bf16), const], axis=1)
+        for h in range(2)
+    ]
     first = offset[0] + tile * q_tile
-    top = jnp.full((8, 2 * q_tile), -jnp.inf, f32)
-    for c in range(chunks):
-        raw = dot_nt(keys[c * k_tile : (c + 1) * k_tile, :], weights)
-        base = jnp.clip(c * k_tile - first, -(k_tile + LANES), q_tile + LANES)
-        for b in range(k_tile // LANES):
-            at = pl.multiple_of(origin - base - b * LANES, LANES)
-            both = jnp.concatenate([strips[h, :, pl.ds(at, q_tile)] for h in range(2)], axis=1)
-            part = raw[b * LANES : (b + 1) * LANES] + both
-            scores[c * k_tile + b * LANES : c * k_tile + (b + 1) * LANES, :] = part
-            top = jnp.maximum(top, jnp.max(part.reshape(LANES // 8, 8, 2 * q_tile), axis=0))
-    top = jnp.max(top, axis=0, keepdims=True)
-    totals = [jnp.zeros((HEAD_DIM + 16, q_tile), f32) for h in range(2)]
-    for c in range(chunks):
-        weight = jnp.exp(scores[c * k_tile : (c + 1) * k_tile, :] - top).astype(bf16)
-        for h in range(2):
-            totals[h] += dot_nn(
-                values[h, :, c * k_tile : (c + 1) * k_tile], weight[:, h * q_tile : (h + 1) * q_tile]
-            )
+    sub = min(SUB_TILE, q_tile)
+    chains = [(u, h) for u in range(q_tile // sub) for h in range(2)]
+    scores = (scores_even, scores_odd)
+    tops, totals = {}, {}
+    for n in range(len(chains) + 1):
+        top = jnp.full((8, sub), -jnp.inf, f32)
+        total = jnp.zeros((HEAD_DIM + 16, sub), f32)
+        for c in range(chunks):
+            rows = slice(c * k_tile, (c + 1) * k_tile)
+            if n < len(chains):
+                u, h = chains[n]
+                raw = dot_nt(keys[rows, :], weights[h][u * sub : (u + 1) * sub])
+                base = jnp.clip(c * k_tile - first - u * sub, -(k_tile + LANES), q_tile + LANES)
+                for b in range(k_tile // LANES):
+                    at = pl.multiple_of(origin - base - b * LANES, LANES)
+                    part = raw[b * LANES : (b + 1) * LANES] + strips[h, :, pl.ds(at, sub)]
+                    scores[n % 2][c * k_tile + b * LANES : c * k_tile + (b + 1) * LANES, :] = part
+                    top = jnp.maximum(top, jnp.max(part.reshape(LANES // 8, 8, sub), axis=0))
+            if n > 0:
+                weight = jnp.exp(scores[(n - 1) % 2][rows, :] - tops[n - 1]).astype(bf16)
+                total += dot_nn(values[chains[n - 1][1], :, rows], weight)
+        tops[n] = jnp.max(top, axis=0, keepdims=True)
+        totals[n - 1] = total
+    top = [jnp.concatenate([tops[n] for n in range(h, len(chains), 2)], axis=1) for h in range(2)]
+    totals = [jnp.concatenate([totals[n] for n in range(h, len(chains), 2)], axis=1) for h in range(2)]
     mixed, pieces = [], []
     for h in range(2):
         total = totals[h][HEAD_DIM : HEAD_DIM + 1]
         mixed.append(totals[h][:HEAD_DIM] / total)
-        pieces += list(three_pieces(-(top[:, h * q_tile : (h + 1) * q_tile] + jnp.log(total))))
+        pieces += list(three_pieces(-(top[h] + jnp.log(total))))
     out_ref[0] = jnp.concatenate(mixed, axis=0).T.astype(bf16)
     rows = lax.broadcasted_iota(jnp.int32, (LANES, q_tile), 0)
     stats = jnp.where(rows == 6, 1.0, 0.0)
@@ -132,7 +141,8 @@
                 pltpu.VMEM((slots, 2 * LANES), bf16),
                 pltpu.VMEM((2, HEAD_DIM + 16, slots), bf16),
                 pltpu.VMEM((2, LANES, width), f32),
-                pltpu.VMEM((slots, 2 * q_tile), f32),
+                pltpu.VMEM((slots, min(SUB_TILE, q_tile)), f32),
+                pltpu.VMEM((slots, min(SUB_TILE, q_tile)), f32),
             ],
         ),
         out_shape=[
@@ -140,6 +150,7 @@
             jax.ShapeDtypeStruct((seqs, pairs, rows, LANES), bf16),
         ],
         compiler_params=pltpu.CompilerParams(vmem_limit_bytes=VMEM_LIMIT),
+        cost_estimate=cost(100),
         name="attention_forward",
     )(lengths, offset, qkv, keys_of, values_of, vector)
 
@@ -185,30 +196,37 @@
 
     def one_tile(i, carried):
         r0 = pl.multiple_of(i * q_tile, q_tile)
-        for c in range(chunks):
+        units = [(c, h) for c in range(chunks) for h in range(2)]
+
+        def products(c, h):
+            cols = slice(c * k_tile, (c + 1) * k_tile)
+            raw = dot_nt(qa[pl.ds(r0, q_tile), :], ka[h, cols, :])
+            back = dot_nt(da[pl.ds(r0, q_tile), :], va[h, cols, :])
+            return raw, back
+
+        ahead = products(*units[0])
+        for n, (c, h) in enumerate(units):
+            raw, back = ahead
+            if n + 1 < len(units):
+                ahead = products(*units[n + 1])
             base = jnp.clip(c * k_tile - offset[0] - r0, -(k_tile + LANES), q_tile + LANES)
             cols = slice(c * k_tile, (c + 1) * k_tile)
-            dq = None
-            for h in range(2):
-                own = slice(h * HEAD_DIM, (h + 1) * HEAD_DIM)
-                raw = dot_nt(qa[pl.ds(r0, q_tile), :], ka[h, cols, :])
-                back = dot_nt(da[pl.ds(r0, q_tile), :], va[h, cols, :])
-                probs, grad = [], []
-                for b in range(q_tile // LANES):
-                    at = pl.multiple_of(origin + base - b * LANES, LANES)
-                    part = slice(b * LANES, (b + 1) * LANES)
-                    p = jnp.exp(raw[part] + strips[h, :, pl.ds(at, k_tile)])
-                    g = p * back[part]
-                    sums[h, :, pl.ds(at, k_tile)] += g
-                    probs.append(p.astype(bf16))
-                    grad.append(g.astype(bf16))
-                probs = jnp.concatenate(probs, axis=0)
-                grad = jnp.concatenate(grad, axis=0)
-                dv_acc[own, cols] += dot_nn(d_turned[own, pl.ds(r0, q_tile)], probs)
-                dk_acc[own, cols] += dot_nn(q_turned[own, pl.ds(r0, q_tile)], grad)
-                more = dot_nn(grad, ka[h, cols, :LANES])
-                dq = more if dq is None else dq + more
-            if c == 0:
+            own = slice(h * HEAD_DIM, (h + 1) * HEAD_DIM)
+            probs, grad = [], []
+            for b in range(q_tile // LANES):
+                at = pl.multiple_of(origin + base - b * LANES, LANES)
+                part = slice(b * LANES, (b + 1) * LANES)
+                p = jnp.exp(raw[part] + strips[h, :, pl.ds(at, k_tile)])
+                g = p * back[part]
+                sums[h, :, pl.ds(at, k_tile)] += g
+                probs.append(p.astype(bf16))
+                grad.append(g.astype(bf16))
+            probs = jnp.concatenate(probs, axis=0)
+            grad = jnp.concatenate(grad, axis=0)
+            dv_acc[own, cols] += dot_nn(d_turned[own, pl.ds(r0, q_tile)], probs)
+            dk_acc[own, cols] += dot_nn(q_turned[own, pl.ds(r0, q_tile)], grad)
+            dq = dot_nn(grad, ka[h, cols, :LANES])
+            if n == 0:
                 dq_acc[...] = dq
             else:
                 dq_acc[...] += dq
@@ -228,13 +246,12 @@
         bias_out[0, 0, h : h + 1, :] = jnp.sum(turned, axis=0, keepdims=True)
 
 
-def attention_backward(qkv, kv, attended, grad, extra, lengths, offset, vector, q_tile, k_tile, pairs):
+def attention_backward(qkv, kv, attended, grad, extra, lengths, offset, vector, q_tile, k_tile, low, pairs):
     seqs, rows, _ = qkv.shape
     keys_of, values_of, k_at, v_at = kv
     slots = keys_of.shape[1]
     width = strip_width(q_tile, k_tile)
     pair_of = lambda at: lambda s, p, *_: (s, 0, p + at)
-    one = pl.Buffered(2)
     spec = lambda r, at: pl.BlockSpec((1, r, LANES), pair_of(at))
     return pl.pallas_call(
         functools.partial(backward_kernel, q_tile, k_tile),
@@ -242,9 +259,9 @@
             num_scalar_prefetch=2,
             grid=(seqs, pairs),
             in_specs=[
-                spec(rows, 0), spec(slots, k_at), spec(slots, v_at), spec(rows, 0), spec(rows, 0),
-                pl.BlockSpec((1, 1, rows, LANES), lambda s, p, *_: (s, p, 0, 0)),
-                pl.BlockSpec((1, 2, width), lambda s, p, *_: (p, 0, 0)),
+                spec(rows, low), spec(slots, k_at + low), spec(slots, v_at + low), spec(rows, low), spec(rows, low),
+                pl.BlockSpec((1, 1, rows, LANES), lambda s, p, *_: (s, p + low, 0, 0)),
+                pl.BlockSpec((1, 2, width), lambda s, p, *_: (p + low, 0, 0)),
             ],
             out_specs=[
                 spec(rows, 0), spec(slots, 0), spec(slots, 0),
@@ -271,6 +288,7 @@
             jax.ShapeDtypeStruct((seqs, pairs, 2, width), f32),
         ],
         compiler_params=pltpu.CompilerParams(vmem_limit_bytes=VMEM_LIMIT),
+        cost_estimate=cost(30 * pairs),
         name="attention_backward",
     )(lengths, offset, qkv, keys_of, values_of, attended, grad, extra, vector)
 
@@ -308,6 +326,10 @@
 PRECISE = lax.Precision.HIGHEST
 BOTH = ("dp", "fsdp")
 FF_CHUNK = 512
+WO = slice(FF_CHUNK, FF_CHUNK + D)
+GROUP = 2
+FORWARD_TILES = (1024, 512)
+BACKWARD_TILES = (512, 256)
 
 
 def rms_factor(values):
@@ -342,12 +364,13 @@
         out_specs=pl.BlockSpec((tile, 3 * D), lambda i: (i, 0)),
         out_shape=jax.ShapeDtypeStruct((tokens, 3 * D), bf16),
         compiler_params=pltpu.CompilerParams(vmem_limit_bytes=VMEM_LIMIT),
+        cost_estimate=cost(12),
         name="project",
     )(x, weights, gain)
 
 
 def ffn_kernel(
-    tile, rows, away, lengths, place, x_ref, a_ref, c_ref, wod_ref, wgu_ref, gain_ref,
+    tile, rows, away, lengths, place, x_ref, a_ref, c_ref, one_ref, two_ref, wgu_ref, gain_ref,
     own_ref, away_ref, gh_ref, ga_ref, dod_out, dgu_out, gain_out,
     dod, dgu, gain_acc, hidden_ref, nf_ref, seed_ref, out_acc, dnf_acc, sems,
 ):
@@ -365,7 +388,7 @@
     seq = at // per_seq
     first = place[1] + (at - seq * per_seq) * tile
     position = first + lax.broadcasted_iota(jnp.int32, (tile, D), 0)
-    hidden_ref[...] = x_ref[...].astype(f32) + dot_nt(a_ref[...], wod_ref[:, :D])
+    hidden_ref[...] = x_ref[...].astype(f32) + dot_nt(a_ref[...], two_ref[:, WO])
     hidden = hidden_ref[...]
     factor = rms_factor(hidden)
     gain = gain_ref[...]
@@ -374,14 +397,14 @@
     out_acc[...] = hidden
     dnf_acc[...] = jnp.zeros_like(dnf_acc)
 
-    def chunk(c, carried):
-        f0 = pl.multiple_of(c * FF_CHUNK, FF_CHUNK)
-        ff = pl.ds(f0, FF_CHUNK)
-        down = pl.ds(pl.multiple_of(D + f0, LANES), FF_CHUNK)
+    for f0 in range(0, FF, FF_CHUNK):
+        ff = slice(f0, f0 + FF_CHUNK)
+        down = slice(D + f0, D + f0 + FF_CHUNK)
+        w_down = one_ref[:, ff] if f0 < 2 * D else two_ref[:, :FF_CHUNK]
         nf, seed = nf_ref[...], seed_ref[...]
         gate = dot_nt(nf, wgu_ref[ff, :D])
         up = dot_nt(nf, wgu_ref[ff, D:])
-        back = dot_nn(seed, wod_ref[:, down])
+        back = dot_nn(seed, w_down)
         square = gate * gate
         root = 0.7978845608028654
         tanh = jnp.tanh(gate * (root + (root * 0.044715) * square))
@@ -391,14 +414,11 @@
         activated = (active * up).astype(bf16)
         grad_gate = (back * up * slope).astype(bf16)
         grad_up = (back * active).astype(bf16)
-        out_acc[...] += dot_nt(activated, wod_ref[:, down])
+        out_acc[...] += dot_nt(activated, w_down)
         dnf_acc[...] += dot_nn(grad_gate, wgu_ref[ff, :D]) + dot_nn(grad_up, wgu_ref[ff, D:])
         dod[:, down] += dot_tn(seed, activated)
         dgu[ff, :D] += dot_tn(grad_gate, nf)
         dgu[ff, D:] += dot_tn(grad_up, nf)
-        return carried
-
-    lax.fori_loop(0, FF // FF_CHUNK, chunk, 0)
     hidden = hidden_ref[...]
     factor = rms_factor(hidden)
     dnf = dnf_acc[...]
@@ -406,7 +426,7 @@
     grad_hidden = seed_ref[...].astype(f32) + norm_back(dnf, hidden, factor, gain)
     gh_ref[...] = grad_hidden
     branch = grad_hidden.astype(bf16)
-    ga_ref[...] = dot_nn(branch, wod_ref[:, :D]).astype(bf16)
+    ga_ref[...] = dot_nn(branch, two_ref[:, WO]).astype(bf16)
     dod[:, :D] += dot_tn(branch, a_ref[...])
 
     @pl.when(step < away)
@@ -442,7 +462,7 @@
     return lambda i, *_: (jnp.maximum(i - away, 0), 0)
 
 
-def ffn(x, attended, cotangent, wod, wgu, gain, lengths, place, tile, rows, away):
+def ffn(x, attended, cotangent, w_one, w_two, wgu, gain, lengths, place, tile, rows, away):
     tokens = x.shape[0]
     steps = tokens // tile
     by_tile = lambda i, lengths, place: (tile_at(i, place, away, steps), 0)
@@ -457,7 +477,8 @@
                 pl.BlockSpec((tile, D), by_tile),
                 pl.BlockSpec((tile, D), by_tile),
                 pl.BlockSpec((tile, D), by_tile),
-                pl.BlockSpec((D, D + FF), whole, pipeline_mode=single),
+                pl.BlockSpec((D, 2 * D), whole, pipeline_mode=single),
+                pl.BlockSpec((D, 2 * D), whole, pipeline_mode=single),
                 pl.BlockSpec((FF, 2 * D), whole, pipeline_mode=single),
                 pl.BlockSpec((1, D), whole),
             ],
@@ -492,34 +513,63 @@
             jax.ShapeDtypeStruct((1, D), f32),
         ],
         compiler_params=pltpu.CompilerParams(vmem_limit_bytes=VMEM_LIMIT),
+        cost_estimate=cost(95),
         name="ffn",
-    )(lengths, place, x, attended, cotangent, wod, wgu, gain)
-
-
-def finish_kernel(
-    away, place, x_ref, dq_ref, dk_ref, dv_ref, gh_ref, w_ref, gain_ref, gain_two_ref,
-    own_ref, away_ref, dw_ref, acc,
-):
+    )(lengths, place, x, attended, cotangent, w_one, w_two, wgu, gain)
+
+
+def weights_kernel(pieces, x_ref, gain_ref, *refs):
+    grads, dw_ref = refs[:-1], refs[-1]
+
+    @pl.when(pl.program_id(0) == 0)
+    def _():
+        dw_ref[...] = jnp.zeros_like(dw_ref)
+
+    x = x_ref[...].astype(f32)
+    normed = (x * rms_factor(x) * gain_ref[...]).astype(bf16)
+    for n in range(3):
+        row = 0
+        for ref in grads[n * pieces : (n + 1) * pieces]:
+            rows = slice(row, row + ref.shape[1])
+            dw_ref[rows, n * D : (n + 1) * D] += dot_tn(ref[...], normed)
+            row += ref.shape[1]
+
+
+def finish_weights(x, gain, dq, dk, dv, tile):
+    tokens = x.shape[0]
+    grads = [*dq, *dk, *dv]
+    return pl.pallas_call(
+        functools.partial(weights_kernel, len(dq)),
+        grid=(tokens // tile,),
+        in_specs=[pl.BlockSpec((tile, D), lambda i: (i, 0)), pl.BlockSpec((1, D), lambda i: (0, 0))]
+        + [pl.BlockSpec((tile, g.shape[1]), lambda i: (i, 0)) for g in grads],
+        out_specs=pl.BlockSpec((sum(g.shape[1] for g in dq), 3 * D), lambda i: (0, 0)),
+        out_shape=jax.ShapeDtypeStruct((sum(g.shape[1] for g in dq), 3 * D), f32),
+        compiler_params=pltpu.CompilerParams(vmem_limit_bytes=VMEM_LIMIT),
+        cost_estimate=cost(14),
+        name="finish_weights",
+    )(x, gain, *grads)
+
+
+def finish_kernel(away, pieces, place, x_ref, gh_ref, w_ref, gain_ref, *refs):
+    grads, (own_ref, away_ref, gain_out) = refs[:-3], refs[-3:]
     step = pl.program_id(0)
 
     @pl.when(step == 0)
     def _():
-        dw_ref[...] = jnp.zeros_like(dw_ref)
-        acc[...] = jnp.zeros_like(acc)
-
+        gain_out[...] = jnp.zeros_like(gain_out)
+
+    grad_normed = None
+    for n in range(3):
+        row = 0
+        for ref in grads[n * pieces : (n + 1) * pieces]:
+            more = dot_nn(ref[...], w_ref[row : row + ref.shape[1], n * D : (n + 1) * D])
+            grad_normed = more if grad_normed is None else grad_normed + more
+            row += ref.shape[1]
     x = x_ref[...].astype(f32)
     factor = rms_factor(x)
-    gain = gain_ref[...]
-    normed = (x * factor * gain).astype(bf16)
-    grad_normed = None
-    for n, ref in enumerate((dq_ref, dk_ref, dv_ref)):
-        part = slice(n * D, (n + 1) * D)
-        grad = ref[...]
-        dw_ref[:, part] += dot_tn(grad, normed)
-        more = dot_nn(grad, w_ref[:, part])
-        grad_normed = more if grad_normed is None else grad_normed + more
-    acc[...] += jnp.sum(grad_normed * x * factor, axis=0, keepdims=True)
-    grad_x = gh_ref[...] + norm_back(grad_normed, x, factor, gain)
+    gain_out[...] += jnp.sum(grad_normed * x * factor, axis=0, keepdims=True)
+    grad_x = gh_ref[...] + norm_back(grad_normed, x, factor, gain_ref[...])
 
     @pl.when(step < away)
     def _():
@@ -529,56 +579,121 @@
     def _():
         own_ref[...] = grad_x
 
-    @pl.when(step == pl.num_programs(0) - 1)
-    def _():
-        rows = lax.broadcasted_iota(jnp.int32, (LANES, D), 0)
-        both = jnp.where(rows == 0, acc[...], jnp.where(rows == 1, gain_two_ref[...], 0.0))
-        dw_ref[:, 3 * D :] = both.T
-
-
-def finish(x, dq, dk, dv, gh, weights, gain, gain_two_grad, place, tile, away):
+
+def finish_inputs(x, gh, weights, gain, dq, dk, dv, place, tile, away):
     tokens = x.shape[0]
     steps = tokens // tile
     by_tile = lambda i, place: (tile_at(i, place, away, steps), 0)
     whole = lambda i, *_: (0, 0)
-    block = pl.BlockSpec((tile, D), by_tile)
+    grads = [*dq, *dk, *dv]
     return pl.pallas_call(
-        functools.partial(finish_kernel, away),
+        functools.partial(finish_kernel, away, len(dq)),
         grid_spec=pltpu.PrefetchScalarGridSpec(
             num_scalar_prefetch=1,
             grid=(steps,),
             in_specs=[
-                block, block, block, block, block,
+                pl.BlockSpec((tile, D), by_tile),
+                pl.BlockSpec((tile, D), by_tile),
                 pl.BlockSpec((D, 3 * D), whole),
                 pl.BlockSpec((1, D), whole),
-                pl.BlockSpec((1, D), whole),
-            ],
+            ]
+            + [pl.BlockSpec((tile, g.shape[1]), by_tile) for g in grads],
             out_specs=[
                 pl.BlockSpec((tile, D), own_index(away)),
                 pl.BlockSpec((tile, D), away_index(away)),
-                pl.BlockSpec((D, 3 * D + LANES), whole),
-            ],
-            scratch_shapes=[pltpu.VMEM((1, D), f32)],
+                pl.BlockSpec((1, D), whole),
+            ],
         ),
         out_shape=[
             jax.ShapeDtypeStruct((tokens - away * tile, D), f32),
             jax.ShapeDtypeStruct((max(away, 1) * tile, D), bf16),
-            jax.ShapeDtypeStruct((D, 3 * D + LANES), f32),
+            jax.ShapeDtypeStruct((1, D), f32),
         ],
         compiler_params=pltpu.CompilerParams(vmem_limit_bytes=VMEM_LIMIT),
-        name="finish",
-    )(place, x, dq, dk, dv, gh, weights, gain, gain_two_grad)
-
-
-def swap_in(block, side):
+        cost_estimate=cost(16),
+        name="finish_inputs",
+    )(place, x, gh, weights, gain, *grads)
+
+
+Y, CORE, X, Z = 1, 2, 4, 8
+SQUARE_DEVICES = 32
+
+
+def from_peer(value, flip):
+    return lax.ppermute(value, BOTH, [(n, n ^ flip) for n in range(SQUARE_DEVICES)])
+
+
+def bit(me, which):
+    return (me // which) % 2
+
+
+def gather_rows(shard, *alongside):
+    me = lax.axis_index(BOTH)
+    n, lanes = shard.shape
+    z = me // Z
+    parts = [shard] + [from_peer(shard, k * Z) for k in (1, 2, 3)]
+    parts = after(parts, *alongside[0:1])
+    column = jnp.stack([pick(parts, z ^ at) for at in range(4)])
+    square = [column] + [from_peer(column, k) for k in (Y, X, X + Y)]
+    square = after(square, *alongside[1:2])
+    corner = bit(me, X) * 2 + bit(me, Y)
+    plane = jnp.stack([pick(square, corner ^ at) for at in range(4)], axis=1).reshape(4, 2, 2, n, lanes)
+    other = after(from_peer(plane, CORE), *alongside[2:3])
+    core = bit(me, CORE)
+    both = jnp.stack([jnp.where(core == 0, plane, other), jnp.where(core == 0, other, plane)], axis=2)
+    return both.reshape(32 * n, lanes)
+
+
+def pick(parts, at):
+    out = parts[0]
+    for n in range(1, len(parts)):
+        out = jnp.where(at == n, parts[n], out)
+    return out
+
+
+def scatter_rows(total):
+    me = lax.axis_index(BOTH)
+    n, lanes = total.shape[0] // 32, total.shape[1]
+    blocks = total.reshape(4, 2, 2, 2, n, lanes)
+    core, x, y, z = bit(me, CORE), bit(me, X), bit(me, Y), me // Z
+    take = lambda a, at, axis: lax.dynamic_index_in_dim(a, at, axis, keepdims=False)
+    sent = from_peer(take(blocks, 1 - core, 2).astype(bf16), CORE)
+    sent = yield sent
+    mine = (take(blocks, core, 2) + sent.astype(f32)).reshape(4, 4, n, lanes)
+    corner = 2 * x + y
+    sent = [from_peer(take(mine, corner ^ k, 1).astype(bf16), (k // 2) * X + (k % 2) * Y) for k in (1, 2, 3)]
+    sent = yield sent
+    mine = take(mine, corner, 1) + (sent[0].astype(f32) + sent[1].astype(f32) + sent[2].astype(f32))
+    sent = [from_peer(take(mine, z ^ k, 0).astype(bf16), k * Z) for k in (1, 2, 3)]
+    sent = yield sent
+    yield take(mine, z, 0) + (sent[0].astype(f32) + sent[1].astype(f32) + sent[2].astype(f32))
+
+
+def scatter_plain(total):
+    sent = yield total.astype(bf16)
+    sent = yield sent
+    sent = yield sent
+    yield lax.psum_scatter(sent, BOTH, scatter_dimension=0, tiled=True).astype(f32)
+
+
+def sum_all(value):
+    value = value + from_peer(value, CORE)
+    value = value + (from_peer(value, Y) + from_peer(value, X) + from_peer(value, X + Y))
+    return value + (from_peer(value, Z) + from_peer(value, 2 * Z) + from_peer(value, 3 * Z))
+
+
+def swap_start(block, side):
+    other = lax.dynamic_index_in_dim(block, 1 - side, 0, keepdims=False)
+    return lax.ppermute(other, "fsdp", [(0, 1), (1, 0)])
+
+
+def swap_in(block, come, side):
     mine = lax.dynamic_index_in_dim(block, side, 0, keepdims=False)
-    other = lax.dynamic_index_in_dim(block, 1 - side, 0, keepdims=False)
-    come = lax.ppermute(other, "fsdp", [(0, 1), (1, 0)])
     return jnp.where(side == 0, jnp.concatenate([mine, come]), jnp.concatenate([come, mine]))
 
 
-def swap_out(own, away, side):
-    come = lax.ppermute(away, "fsdp", [(0, 1), (1, 0)]).astype(f32)
+def swap_out(own, come, side):
+    come = come.astype(f32)
     return jnp.where(side == 0, jnp.stack([own, come]), jnp.stack([come, own]))
 
 
@@ -586,70 +701,135 @@
     return weight.astype(bf16).T
 
 
+def after(value, *others):
+    if not others:
+        return value
+    return lax.optimization_barrier((value, *others))[0]
+
+
 def per_device(
-    sides, inputs, cotangent, lengths, w_query, w_key, w_value, w_out, w_gate, w_up, w_down,
+    sizes, inputs, cotangent, lengths, w_query, w_key, w_value, w_out, w_gate, w_up, w_down,
     gain_attn, gain_ffn, bias_table,
 ):
     seqs, own_rows, _ = inputs.shape
+    sides = sizes["fsdp"]
     slots = own_rows * sides
     side = lax.axis_index("fsdp")
-    share = gain_attn.shape[0]
+    swap = seqs == 2 and sides == 2
+    if sizes["dp"] * sides == SQUARE_DEVICES and sides == 2:
+        gather, scatter, total = gather_rows, scatter_rows, sum_all
+    else:
+        gather = lambda a, *b: lax.all_gather(a, BOTH, axis=0, tiled=True)
+        scatter = scatter_plain
+        total = lambda a: lax.psum(a, BOTH)
+    if swap:
+        other = lax.dynamic_index_in_dim(inputs, 1 - side, 0, keepdims=False)
+        other, w_query, w_key, w_value = lax.optimization_barrier((other, w_query, w_key, w_value))
+        come = [lax.ppermute(part, "fsdp", [(0, 1), (1, 0)]) for part in jnp.split(other, (384, 768))]
+    else:
+        come = []
     gains = jnp.pad(jnp.stack([gain_attn, gain_ffn], axis=1).astype(bf16), ((0, 0), (0, LANES - 2)))
     packed = jnp.concatenate([turned(w_query), turned(w_key), turned(w_value), gains], axis=1)
-    wqkv = lax.all_gather(packed, BOTH, axis=0, tiled=True)
+    w_out, w_gate, w_up, w_down, packed = lax.optimization_barrier((w_out, w_gate, w_up, w_down, packed))
+    wqkv = gather(packed, *come)
     gain_rows = wqkv[:, 3 * D : 3 * D + 2].astype(f32).T
-    wod = lax.all_gather(jnp.concatenate([turned(w_out), turned(w_down)], axis=1), BOTH, axis=0, tiled=True)
-    wgu = lax.all_gather(jnp.concatenate([turned(w_gate), turned(w_up)], axis=1), BOTH, axis=0, tiled=True)
-    swap = seqs == 2 and sides == 2
+    rest = jnp.concatenate(
+        [
+            turned(w_down)[:, : 2 * D],
+            jnp.pad(jnp.concatenate([turned(w_down)[:, 2 * D :], turned(w_out)], axis=1), ((0, 0), (0, 256))),
+            jnp.concatenate([turned(w_gate), turned(w_up)], axis=1),
+        ]
+    )
+    rest = lax.all_gather(after(rest, wqkv), BOTH)
+    share, ff_share = gain_attn.shape[0], w_gate.shape[1]
+    w_one = rest[:, :share].reshape(D, 2 * D)
+    w_two = rest[:, share : 2 * share].reshape(D, 2 * D)
+    wgu = rest[:, 2 * share :].reshape(FF, 2 * D)
     if swap:
-        x, seed = swap_in(inputs, side), swap_in(cotangent, side)
+        x = swap_in(inputs, jnp.concatenate(come), side)
         lengths = lax.dynamic_slice_in_dim(lengths, side, 1)
         seqs, rows, first = 1, slots, jnp.zeros((), jnp.int32)
     else:
-        x, seed = inputs.reshape(-1, D), cotangent.reshape(-1, D)
+        x = inputs.reshape(-1, D)
         rows, first = own_rows, side * own_rows
     tile = min(512, own_rows)
     away = own_rows // tile if swap else 0
     place = jnp.stack([side, first]).astype(jnp.int32)
     origin = place[1:]
-    one_hot = bias_onehot(tile, 512, False)
+    ahead_tiles = (min(FORWARD_TILES[0], rows), FORWARD_TILES[1])
+    back_tiles = (min(BACKWARD_TILES[0], rows), BACKWARD_TILES[1])
+    one_hot = bias_onehot(*back_tiles, False)
     vector = jnp.dot(one_hot, bias_table, precision=PRECISE).T.reshape(PAIRS, 2, -1)
-    flipped = jnp.dot(bias_onehot(tile, 512, True), bias_table, precision=PRECISE).T.reshape(PAIRS, 2, -1)
+    flipped = jnp.dot(bias_onehot(*ahead_tiles, True), bias_table, precision=PRECISE).T.reshape(PAIRS, 2, -1)
 
     qkv = project(x, wqkv, gain_rows[0:1], tile).reshape(seqs, rows, 3 * D)
+    if swap:
+        cotangent = after(cotangent, x)
+        seed_come = swap_start(cotangent, side)
     if rows < slots:
         kv = lax.all_gather(qkv[:, :, D:], "fsdp", axis=1, tiled=True)
         sources = (kv, kv, 0, PAIRS)
     else:
         sources = (qkv, qkv, PAIRS, 2 * PAIRS)
-    attended, extra = attention_forward(qkv, sources, lengths, origin, flipped, tile, 512, PAIRS)
+    attended, extra = attention_forward(qkv, sources, lengths, origin, flipped, *ahead_tiles, PAIRS)
+    if swap:
+        seed = swap_in(cotangent, after(seed_come, attended), side)
+    else:
+        seed = cotangent.reshape(-1, D)
     own, away_out, grad_hidden, grad_attended, dod, dgu, gain_two = ffn(
-        x, attended.reshape(-1, D), seed, wod, wgu, gain_rows[1:2], lengths, place, tile, rows, away
+        x, attended.reshape(-1, D), seed, w_one, w_two, wgu, gain_rows[1:2], lengths, place, tile, rows, away
     )
+    grad_attended = grad_attended.reshape(seqs, rows, D)
+    dq, dk, dv, strips = [], [], [], []
+    scatters = [scatter(dod), scatter(dgu)]
+    moving = [next(s) for s in scatters]
+    back = []
     if swap:
-        output = swap_out(own, away_out, side)
+        back = [lax.ppermute(away_out, "fsdp", [(0, 1), (1, 0)])]
+    for low in range(0, PAIRS, GROUP):
+        one, two, three, strip = attention_backward(
+            qkv, sources, attended, grad_attended, extra, lengths, origin, vector, *back_tiles, low, GROUP
+        )
+        if rows < slots:
+            two = lax.psum_scatter(two, "fsdp", scatter_dimension=1, tiled=True)
+            three = lax.psum_scatter(three, "fsdp", scatter_dimension=1, tiled=True)
+        dq.append(one.reshape(-1, GROUP * LANES))
+        dk.append(two.reshape(-1, GROUP * LANES))
+        dv.append(three.reshape(-1, GROUP * LANES))
+        strips.append(strip)
+        moving, back, extra, dq, dk, dv = lax.optimization_barrier((moving, back, extra, dq, dk, dv))
+        moving = [s.send(m) for s, m in zip(scatters, moving)]
+    out_down, gate_up = moving
+    if swap:
+        output = swap_out(own, back[0], side)
     else:
         output = own.reshape(seqs, rows, D)
-    out_down = lax.psum_scatter(dod.astype(bf16), BOTH, scatter_dimension=0, tiled=True).astype(f32)
-    gate_up = lax.psum_scatter(dgu.astype(bf16), BOTH, scatter_dimension=0, tiled=True).astype(f32)
-    dq, dk, dv, strips = attention_backward(
-        qkv, sources, attended, grad_attended.reshape(seqs, rows, D), extra, lengths, origin, vector,
-        tile, 512, PAIRS,
+    dq = after(dq, output)
+    dw = finish_weights(x, gain_rows[0:1], dq, dk, dv, tile)
+    scatter_qk = scatter(dw)
+    moving = next(scatter_qk)
+    own, away_grad, gain_one = finish_inputs(
+        x, grad_hidden, wqkv, gain_rows[0:1], after(dq, dw), dk, dv, place, tile, away
     )
-    if rows < slots:
-        dk = lax.psum_scatter(dk, "fsdp", scatter_dimension=1, tiled=True)
-        dv = lax.psum_scatter(dv, "fsdp", scatter_dimension=1, tiled=True)
-    diagonals = jnp.sum(strips, axis=0).reshape(HEADS, -1)
-    table = lax.psum(jnp.dot(diagonals, one_hot, precision=PRECISE).T, BOTH)
-    flat = lambda a: a.reshape(-1, D)
-    own, away_grad, dw = finish(
-        x, flat(dq), flat(dk), flat(dv), grad_hidden, wqkv, gain_rows[0:1], gain_two, place, tile, away
-    )
+    moving, own, gain_one = lax.optimization_barrier((moving, own, gain_one))
     if swap:
-        grad_inputs = swap_out(own, away_grad, side)
+        back = [lax.ppermute(part, "fsdp", [(0, 1), (1, 0)]) for part in jnp.split(away_grad, 2)]
+    else:
+        back = [own, own]
+    moving = scatter_qk.send(moving)
+    diagonals = jnp.sum(jnp.concatenate(strips, axis=1), axis=0).reshape(HEADS, -1)
+    table = jnp.dot(diagonals, one_hot, precision=PRECISE).T
+    small = jnp.concatenate([gain_one, gain_two, jnp.pad(table.reshape(1, -1), ((0, 0), (0, D - BUCKETS * HEADS)))])
+    small = total(small)
+    moving, back[0], small = lax.optimization_barrier((moving, back[0], small))
+    moving = scatter_qk.send(moving)
+    moving, back[1] = lax.optimization_barrier((moving, back[1]))
+    query_key = scatter_qk.send(moving)
+    gain_shares = lax.dynamic_slice_in_dim(small[:2], lax.axis_index(BOTH) * gain_attn.shape[0], gain_attn.shape[0], 1)
+    if swap:
+        grad_inputs = swap_out(own, jnp.concatenate(back), side)
     else:
         grad_inputs = own.reshape(seqs, rows, D)
-    query_key = lax.psum_scatter(dw.astype(bf16), BOTH, scatter_dimension=0, tiled=True).astype(f32)
     return (
         output,
         grad_inputs,
@@ -660,9 +840,9 @@
         gate_up[:, :D].T,
         gate_up[:, D:].T,
         out_down[:, D:].T,
-        query_key[:, 3 * D],
-        query_key[:, 3 * D + 1],
-        table,
+        gain_shares[0],
+        gain_shares[1],
+        small[2, : BUCKETS * HEADS].reshape(BUCKETS, HEADS),
     )
 
 
@@ -670,7 +850,7 @@
     tokens = P("dp", "fsdp", None)
     columns = P(None, BOTH)
     return jax.shard_map(
-        functools.partial(per_device, mesh.shape["fsdp"]),
+        functools.partial(per_device, dict(mesh.shape)),
         mesh=mesh,
         in_specs=(tokens, tokens, P("dp")) + (columns,) * 7 + (P(BOTH), P(BOTH), P()),
         out_specs=(tokens, tokens) + (columns,) * 7 + (P(BOTH), P(BOTH), P()),

time: 898 us -> 657 us (0.73)
  waiting for transfers between devices: 265 us -> 82 us
  blocking collectives: 111 us -> 0 us
  starting transfers between devices: 5.32 us -> 50 us
  local copies, waits for them, and re-layouts: 11.9 us -> 48.4 us
  Pallas kernels: 431 us -> 404 us
    reduce_scatter x2 -> x0, waiting for transfers between devices: 197 us -> none  [the longest x1 118 us: per_device(): lax.psum_scatter(dgu.astype(bf16), BOTH, scatter_dimension=0, tiled=True)]
    psum x1 -> x0, blocking collectives: 111 us -> none  [per_device(): table = lax.psum(jnp.dot(diagonals, one_hot, precision=PRECISE).T, BOTH)]
    ppermute x4 -> x42, starting transfers between devices: 5.07 us -> 50 us  [the longest x35 40.8 us: from_peer(): lax.ppermute(value, BOTH, [(n, n ^ flip) for n in range(SQUARE_DEVICES)])]
    convert_element_type x6 -> x1, other arithmetic: 22.3 us -> 1.6 us  [swap_out(): come = come.astype(f32)]
    add x0 -> x12, other arithmetic: none -> 16.6 us  [the longest x3 9.4 us: scatter_rows(): mine = (take(blocks, core, 2) + sent.astype(f32)).reshape(4, 4, n, lanes)]
    pallas_call x1 -> x3, Pallas kernels: 190 us -> 174 us  [attention_backward(): pl.pallas_call(functools.partial(backward_kernel, q_tile, k_tile), grid_s...]
    convert_element_type x0 -> x9, local copies, waits for them, and re-layouts: none -> 15.1 us  [the longest x3 10.4 us: scatter_rows(): sent = from_peer(take(blocks, 1 - core, 2).astype(bf16), CORE)]
    ppermute x4 -> x42, waiting for transfers between devices: 67.4 us -> 82 us  [the longest x35 57.9 us: from_peer(): lax.ppermute(value, BOTH, [(n, n ^ flip) for n in range(SQUARE_DEVICES)])]
  transfers between devices with their start and end apart: 10 -> 43, of which waited for: 4 -> 14; matrix products, arithmetic and copies ran while one was open for 6% -> 7% of each run, Pallas kernels for 13% -> 46%
where the time goes in v2:
time: 657 us; the launch traced here: 646 us
  Pallas kernels  404 us (61%)
  waiting for transfers between devices  82 us (12%)
  starting transfers between devices  50 us (8%)
  local copies, waits for them, and re-layouts  48.4 us (7%)
  other arithmetic  44.3 us (7%)
  between operations  15.1 us (2%)
    pallas_call x3, Pallas kernels, attention_backward(): pl.pallas_call(functools.partial(backward_kernel, q_tile, k_tile), grid_s...  174 us
    pallas_call x1, Pallas kernels, ffn(): pl.pallas_call(functools.partial(ffn_kernel, tile, rows, away), grid_spec...  93.4 us
    pallas_call x1, Pallas kernels, attention_forward(): pl.pallas_call(functools.partial(forward_kernel, q_tile, k_tile), grid_sp...  93 us
    ppermute x35, waiting for transfers between devices, from_peer(): lax.ppermute(value, BOTH, [(n, n ^ flip) for n in range(SQUARE_DEVICES)])  57.9 us
    ppermute x35, starting transfers between devices, from_peer(): lax.ppermute(value, BOTH, [(n, n ^ flip) for n in range(SQUARE_DEVICES)])  40.8 us
    ppermute x5, waiting for transfers between devices, per_device(): lax.ppermute(part, 'fsdp', [(0, 1), (1, 0)])  24 us
    pallas_call x1, Pallas kernels, finish_inputs(): pl.pallas_call(functools.partial(finish_kernel, away, len(dq)), grid_spec...  16.4 us
    pallas_call x1, Pallas kernels, finish_weights(): pl.pallas_call(functools.partial(weights_kernel, len(dq)), grid=(tokens /...  14.6 us
  transfers between devices with their start and end apart: 43, of which 14 were waited for; matrix products, arithmetic and copies ran while one was open for 7% of the time, Pallas kernels for 46%

profile of v2, /device:TPU:0, one launch (start us, length us, event | category | flops | bytes accessed | tf_op | source)
XLA Modules:
  0.0 646.3 jit_solution(353731343640319896)
XLA Ops:
  7.3 3.3 dynamic-slice_bitcast_fusion.3
  20.9 7.1 %collective-permute-done.4 = bf16[24,2432]{1,0:T(8,128)(2,1)} collective-permute-done((bf16[24,2432]{1,0:T(8,128)(2,1)S(1)}, bf16[24,2432]{1,0:T(8,128)(2,1)}, u32[]{:S(2)}, u32[]{:S(2)}) %collective-permute-start.4) | collective-permute-done | bytes 116768 | tf_op jit(solution)/shard_map/ppermute | solution.py:623
  33.9 9.7 %collective-permute-done.1 = bf16[384,768]{1,0:T(8,128)(2,1)S(1)} collective-permute-done((bf16[384,768]{1,0:T(8,128)(2,1)S(1)}, bf16[384,768]{1,0:T(8,128)(2,1)S(1)}, u32[]{:S(2)}, u32[]{:S(2)}) %collective-permute-start.1) | collective-permute-done | bytes 589856 | tf_op jit(solution)/shard_map/ppermute | solution.py:728
  43.6 17.1 %collective-permute-done.6 = bf16[4,24,2432]{2,1,0:T(8,128)(2,1)} collective-permute-done((bf16[4,24,2432]{2,1,0:T(8,128)(2,1)S(1)}, bf16[4,24,2432]{2,1,0:T(8,128)(2,1)}, u32[]{:S(2)}, u32[]{:S(2)}) %collective-permute-start.6) | collective-permute-done | bytes 466976 | tf_op jit(solution)/shard_map/ppermute | solution.py:623
  69.1 6.3 collective-permute-done.2
  91.2 12.2 %project.1 = bf16[2048,2304]{1,0:T(8,128)(2,1)} custom-call(bf16[2048,768]{1,0:T(8,128)(2,1)} %maximum_select_fusion.2.x_ref, bf16[768,2432]{1,0:T(8,128)(2,1)} %bitcast.184, f32[1,768]{1,0:T(1,128)} %get-tuple-element.292.gain_ref), custom_call_target="tpu_custom_call" | custom-call | flops 13200000000 | bytes 1048576 | tf_op jit(solution)/shard_map/project/pallas_call | solution.py:356
  103.4 93.0 %attention_forward.1 = (bf16[1,2048,768]{2,1,0:T(8,128)(2,1)}, bf16[1,6,2048,128]{3,2,1,0:T(8,128)(2,1)}) custom-call(s32[1]{0:T(128)} %dynamic_slice.118.lengths, s32[1]{0:T(128)} %constant.233.clone.1.offset, bf16[1,2048,2304]{2,1,0:T(8,128)(2,1)} %bitcast.194, bf16[1,2048,2304]{2,1,0:T(8,128)(2,1)} %bitcast.195, bf16[1,2048,2304]{2,1,0:T(8,128)(2,1)} %bitcast.196, ...), custom_call_target="tpu_custom_call" | custom-call | flops 109999996928 | bytes 1048576 | tf_op jit(solution)/shard_map/attention_forward/pallas_call | solution.py:125
  198.5 4.8 fusion.56
  203.3 6.1 slice.84
  209.5 93.4 %ffn.1 = (f32[1024,768]{1,0:T(8,128)}, bf16[1024,768]{1,0:T(8,128)(2,1)}, f32[2048,768]{1,0:T(8,128)}, bf16[2048,768]{1,0:T(8,128)(2,1)}, f32[768,2816]{1,0:T(8,...) custom-call(s32[1]{0:T(128)} %dynamic_slice.118.lengths, s32[2]{0:T(128)} %pad_add_fusion.place, ...), custom_call_target="tpu_custom_call" | custom-call | flops 104500002816 | bytes 1048576 | tf_op jit(solution)/shard_map/ffn/pallas_call | solution.py:471
  302.9 3.8 fusion.1
  306.7 3.2 fusion
  311.0 57.8 %attention_backward.3 = (bf16[1,2048,256]{2,1,0:T(8,128)(2,1)}, bf16[1,2048,256]{2,1,0:T(8,128)(2,1)}, bf16[1,2048,256]{2,1,0:T(8,128)(2,1)}, f32[1,2,2,1792]{3,2,1,0:T(2,128)}) custom-call(s32[1]{0:T(128)} %dynamic_slice.118.lengths, s32[1]{0:T(128)} %constant.233.clone.1.offset, bf16[1,2048,2304]{2,1,0:T(8,128)(2,1)} %bitcast.197, ...), custom_call_target="tpu_custom_call" | custom-call | flops 65999998976 | bytes 1048576 | tf_op jit(solution)/shard_map/attention_backward/pallas_call | solution.py:256
  368.8 3.5 bitcast_add_fusion.1
  391.7 58.1 %attention_backward.4 = (bf16[1,2048,256]{2,1,0:T(8,128)(2,1)}, bf16[1,2048,256]{2,1,0:T(8,128)(2,1)}, bf16[1,2048,256]{2,1,0:T(8,128)(2,1)}, f32[1,2,2,1792]{3,2,1,0:T(2,128)}) custom-call(s32[1]{0:T(128)} %dynamic_slice.118.lengths, s32[1]{0:T(128)} %constant.233.clone.1.offset, bf16[1,2048,2304]{2,1,0:T(8,128)(2,1)} %bitcast.200, ...), custom_call_target="tpu_custom_call" | custom-call | flops 65999998976 | bytes 1048576 | tf_op jit(solution)/shard_map/attention_backward/pallas_call | solution.py:256
  461.2 3.5 collective-permute-start.24
  464.7 58.2 %attention_backward.5 = (bf16[1,2048,256]{2,1,0:T(8,128)(2,1)}, bf16[1,2048,256]{2,1,0:T(8,128)(2,1)}, bf16[1,2048,256]{2,1,0:T(8,128)(2,1)}, f32[1,2,2,1792]{3,2,1,0:T(2,128)}) custom-call(s32[1]{0:T(128)} %dynamic_slice.118.lengths, s32[1]{0:T(128)} %constant.233.clone.1.offset, bf16[1,2048,2304]{2,1,0:T(8,128)(2,1)} %bitcast.203, ...), custom_call_target="tpu_custom_call" | custom-call | flops 65999998976 | bytes 1048576 | tf_op jit(solution)/shard_map/attention_backward/pallas_call | solution.py:256
  526.7 5.3 collective-permute-done.25
  536.6 14.6 %finish_weights.1 = f32[768,2304]{1,0:T(8,128)} custom-call(bf16[2048,768]{1,0:T(8,128)(2,1)} %maximum_select_fusion.2.x_ref, f32[1,768]{1,0:T(1,128)} %get-tuple-element.292.gain_ref, bf16[2048,256]{1,0:T(8,128)(2,1)} %bitcast.210, bf16[2048,256]{1,0:T(8,128)(2,1)} %bitcast.216, bf16[2048,256]{1,0:T(8,128)(2,1)} %bitcast.222, bf16[2048,256]{1,0:T(8,128)(2,1)} %bitcast.212, ...), custom_call_target="tpu_custom_call" | custom-call | flops 15399999488 | bytes 1048576 | tf_op jit(solution)/shard_map/finish_weights/pallas_call | solution.py:541
  551.2 3.4 fusion.2
  554.5 16.4 %finish_inputs.1 = (f32[1024,768]{1,0:T(8,128)}, bf16[1024,768]{1,0:T(8,128)(2,1)}, f32[1,768]{1,0:T(1,128)}) custom-call(s32[2]{0:T(128)} %pad_add_fusion.place, bf16[2048,768]{1,0:T(8,128)(2,1)} %maximum_select_fusion.2.x_ref, f32[2048,768]{1,0:T(8,128)} %get-tuple-element.183.gh_ref, bf16[768,2432]{1,0:T(8,128)(2,1)} %bitcast.185, ...), custom_call_target="tpu_custom_call" | custom-call | flops 17600000000 | bytes 1048576 | tf_op jit(solution)/shard_map/finish_inputs/pallas_call | solution.py:589
  584.0 9.8 %collective-permute-done.32 = f32[3,768]{1,0:T(4,128)S(1)} collective-permute-done((f32[3,768]{1,0:T(4,128)S(1)}, f32[3,768]{1,0:T(4,128)S(1)}, u32[]{:S(2)}, u32[]{:S(2)}) %collective-permute-start.32) | collective-permute-done | bytes 9248 | tf_op jit(solution)/shard_map/ppermute | solution.py:623
  606.1 11.6 %collective-permute-done.27 = bf16[4,24,2304]{2,1,0:T(8,128)(2,1)S(1)} collective-permute-done((bf16[4,24,2304]{2,1,0:T(8,128)(2,1)S(1)}, bf16[4,24,2304]{2,1,0:T(8,128)(2,1)S(1)}, u32[]{:S(2)}, u32[]{:S(2)}) %collective-permute-start.27) | collective-permute-done | bytes 442400 | tf_op jit(solution)/shard_map/ppermute | solution.py:623
  625.8 7.1 %collective-permute-done.41 = bf16[512,768]{1,0:T(8,128)(2,1)} collective-permute-done((bf16[512,768]{1,0:T(8,128)(2,1)}, bf16[512,768]{1,0:T(8,128)(2,1)}, u32[]{:S(2)}, u32[]{:S(2)}) %collective-permute-start.41) | collective-permute-done | bytes 786464 | tf_op jit(solution)/shard_map/ppermute | solution.py:816
  (226 shorter events, 121.7 us)
Async XLA Ops:
  7.2 191.3 %all-gather.3.cloned.1.call-start = ((), (), s32[]{:S(2)}) async-start(), calls=%async_computation | async-start | bytes 11354112 | tf_op jit(solution)/shard_map/all_gather | solution.py:743
  19.1 24.5 %collective-permute-start.1 = (bf16[384,768]{1,0:T(8,128)(2,1)S(1)}, bf16[384,768]{1,0:T(8,128)(2,1)S(1)}, u32[]{:S(2)}, u32[]{:S(2)}) collective-permute-start(bf16[384,768]{1,0:T(8,128)(2,1)S(1)} %get-tuple-element.275), channel_id=1, source_target_pairs={{0,1},{1,0},{2,3},{3,2},{4,5},{5,4},{6,7},{7,6},{8,9},{9,8},{10,11... | collective-permute-start | bytes 1769480 | tf_op jit(solution)/shard_map/ppermute | solution.py:728
  30.2 30.5 %collective-permute-start.6 = (bf16[4,24,2432]{2,1,0:T(8,128)(2,1)S(1)}, bf16[4,24,2432]{2,1,0:T(8,128)(2,1)}, u32[]{:S(2)}, u32[]{:S(2)}) collective-permute-start(bf16[4,24,2432]{2,1,0:T(8,128)(2,1)S(1)} %pad_maximum_fusion.2), channel_id=1, source_target_pairs={{0,1},{1,0},{2,3},{3,2},{4,5},{5,4},{6,7},{7,6},{8,9},{9,8},{10,11... | collective-permute-start | bytes 1400840 | tf_op jit(solution)/shard_map/ppermute | solution.py:623
  32.3 28.4 %collective-permute-start.7 = (bf16[4,24,2432]{2,1,0:T(8,128)(2,1)S(1)}, bf16[4,24,2432]{2,1,0:T(8,128)(2,1)}, u32[]{:S(2)}, u32[]{:S(2)}) collective-permute-start(bf16[4,24,2432]{2,1,0:T(8,128)(2,1)S(1)} %pad_maximum_fusion.2), channel_id=1, source_target_pairs={{0,4},{1,5},{2,6},{3,7},{4,0},{5,1},{6,2},{7,3},{8,12},{9,13},{10,... | collective-permute-start | bytes 1400840 | tf_op jit(solution)/shard_map/ppermute | solution.py:623
  33.8 26.9 %collective-permute-start.8 = (bf16[4,24,2432]{2,1,0:T(8,128)(2,1)S(1)}, bf16[4,24,2432]{2,1,0:T(8,128)(2,1)}, u32[]{:S(2)}, u32[]{:S(2)}) collective-permute-start(bf16[4,24,2432]{2,1,0:T(8,128)(2,1)S(1)} %pad_maximum_fusion.2), channel_id=1, source_target_pairs={{0,5},{1,4},{2,7},{3,6},{4,1},{5,0},{6,3},{7,2},{8,13},{9,12},{10,... | collective-permute-start | bytes 1400840 | tf_op jit(solution)/shard_map/ppermute | solution.py:623
  87.7 108.7 %collective-permute-start.10 = (bf16[1024,768]{1,0:T(8,128)(2,1)}, bf16[1024,768]{1,0:T(8,128)(2,1)S(1)}, u32[]{:S(2)}, u32[]{:S(2)}) collective-permute-start(bf16[1024,768]{1,0:T(8,128)(2,1)} %get-tuple-element.262), channel_id=1, source_target_pairs={{0,1},{1,0},{2,3},{3,2},{4,5},{5,4},{6,7},{7,6},{8,9},{9,8},{10,11... | collective-permute-start | bytes 4718600 | tf_op jit(solution)/shard_map/ppermute | solution.py:687
  306.7 62.1 %collective-permute-start.11 = (bf16[4,2,2,24,2816]{4,3,2,1,0:T(8,128)(2,1)}, bf16[4,2,2,24,2816]{4,3,2,1,0:T(8,128)(2,1)}, u32[]{:S(2)}, u32[]{:S(2)}) collective-permute-start(bf16[4,2,2,24,2816]{4,3,2,1,0:T(8,128)(2,1)} %fusion.1), channel_id=1, source_target_pairs={{0,2},{1,3},{2,0},{3,1},{4,6},{5,7},{6,4},{7,5},{8,10},{9,11},{10,... | collective-permute-start | bytes 6488072 | tf_op jit(solution)/shard_map/ppermute | solution.py:623
  309.9 58.9 %collective-permute-start.12 = (bf16[4,2,2,64,1536]{4,3,2,1,0:T(8,128)(2,1)S(1)}, bf16[4,2,2,64,1536]{4,3,2,1,0:T(8,128)(2,1)}, u32[]{:S(2)}, u32[]{:S(2)}) collective-permute-start(bf16[4,2,2,64,1536]{4,3,2,1,0:T(8,128)(2,1)S(1)} %fusion), channel_id=1, source_target_pairs={{0,2},{1,3},{2,0},{3,1},{4,6},{5,7},{6,4},{7,5},{8,10},{9,11},{10,... | collective-permute-start | bytes 9437192 | tf_op jit(solution)/shard_map/ppermute | solution.py:623
  310.5 58.3 %collective-permute-start.13 = (bf16[1024,768]{1,0:T(8,128)(2,1)}, bf16[1024,768]{1,0:T(8,128)(2,1)}, u32[]{:S(2)}, u32[]{:S(2)}) collective-permute-start(bf16[1024,768]{1,0:T(8,128)(2,1)} %get-tuple-element.137), channel_id=1, source_target_pairs={{0,1},{1,0},{2,3},{3,2},{4,5},{5,4},{6,7},{7,6},{8,9},{9,8},{10,11... | collective-permute-start | bytes 4718600 | tf_op jit(solution)/shard_map/ppermute | solution.py:788
  375.4 74.4 %collective-permute-start.15 = (bf16[4,24,2816]{2,1,0:T(8,128)(2,1)}, bf16[4,24,2816]{2,1,0:T(8,128)(2,1)}, u32[]{:S(2)}, u32[]{:S(2)}) collective-permute-start(bf16[4,24,2816]{2,1,0:T(8,128)(2,1)} %get-tuple-element.254), channel_id=1, source_target_pairs={{0,4},{1,5},{2,6},{3,7},{4,0},{5,1},{6,2},{7,3},{8,12},{9,13},{10,... | collective-permute-start | bytes 1622024 | tf_op jit(solution)/shard_map/ppermute | solution.py:623
  376.9 72.9 %collective-permute-start.16 = (bf16[4,24,2816]{2,1,0:T(8,128)(2,1)}, bf16[4,24,2816]{2,1,0:T(8,128)(2,1)}, u32[]{:S(2)}, u32[]{:S(2)}) collective-permute-start(bf16[4,24,2816]{2,1,0:T(8,128)(2,1)} %get-tuple-element.253), channel_id=1, source_target_pairs={{0,5},{1,4},{2,7},{3,6},{4,1},{5,0},{6,3},{7,2},{8,13},{9,12},{10,... | collective-permute-start | bytes 1622024 | tf_op jit(solution)/shard_map/ppermute | solution.py:623
  385.3 64.5 %collective-permute-start.17 = (bf16[4,64,1536]{2,1,0:T(8,128)(2,1)}, bf16[4,64,1536]{2,1,0:T(8,128)(2,1)S(1)}, u32[]{:S(2)}, u32[]{:S(2)}) collective-permute-start(bf16[4,64,1536]{2,1,0:T(8,128)(2,1)} %get-tuple-element.252), channel_id=1, source_target_pairs={{0,1},{1,0},{2,3},{3,2},{4,5},{5,4},{6,7},{7,6},{8,9},{9,8},{10,11... | collective-permute-start | bytes 2359304 | tf_op jit(solution)/shard_map/ppermute | solution.py:623
  386.4 63.4 %collective-permute-start.18 = (bf16[4,64,1536]{2,1,0:T(8,128)(2,1)S(1)}, bf16[4,64,1536]{2,1,0:T(8,128)(2,1)S(1)}, u32[]{:S(2)}, u32[]{:S(2)}) collective-permute-start(bf16[4,64,1536]{2,1,0:T(8,128)(2,1)S(1)} %get-tuple-element.251), channel_id=1, source_target_pairs={{0,4},{1,5},{2,6},{3,7},{4,0},{5,1},{6,2},{7,3},{8,12},{9,13},{10,... | collective-permute-start | bytes 2359304 | tf_op jit(solution)/shard_map/ppermute | solution.py:623
  389.0 60.8 %collective-permute-start.19 = (bf16[4,64,1536]{2,1,0:T(8,128)(2,1)S(1)}, bf16[4,64,1536]{2,1,0:T(8,128)(2,1)S(1)}, u32[]{:S(2)}, u32[]{:S(2)}) collective-permute-start(bf16[4,64,1536]{2,1,0:T(8,128)(2,1)S(1)} %get-tuple-element.250), channel_id=1, source_target_pairs={{0,5},{1,4},{2,7},{3,6},{4,1},{5,0},{6,3},{7,2},{8,13},{9,12},{10,... | collective-permute-start | bytes 2359304 | tf_op jit(solution)/shard_map/ppermute | solution.py:623
  453.1 71.4 %collective-permute-start.20 = (bf16[24,2816]{1,0:T(8,128)(2,1)}, bf16[24,2816]{1,0:T(8,128)(2,1)}, u32[]{:S(2)}, u32[]{:S(2)}) collective-permute-start(bf16[24,2816]{1,0:T(8,128)(2,1)} %get-tuple-element.278), channel_id=1, source_target_pairs={{0,8},{1,9},{2,10},{3,11},{4,12},{5,13},{6,14},{7,15},{8,0},{9,1},... | collective-permute-start | bytes 405512 | tf_op jit(solution)/shard_map/ppermute | solution.py:623
  454.6 72.0 %collective-permute-start.21 = (bf16[24,2816]{1,0:T(8,128)(2,1)}, bf16[24,2816]{1,0:T(8,128)(2,1)}, u32[]{:S(2)}, u32[]{:S(2)}) collective-permute-start(bf16[24,2816]{1,0:T(8,128)(2,1)} %get-tuple-element.277), channel_id=1, source_target_pairs={{0,16},{1,17},{2,18},{3,19},{4,20},{5,21},{6,22},{7,23},{8,24},{9,... | collective-permute-start | bytes 405512 | tf_op jit(solution)/shard_map/ppermute | solution.py:623
  457.2 69.4 %collective-permute-start.22 = (bf16[24,2816]{1,0:T(8,128)(2,1)}, bf16[24,2816]{1,0:T(8,128)(2,1)}, u32[]{:S(2)}, u32[]{:S(2)}) collective-permute-start(bf16[24,2816]{1,0:T(8,128)(2,1)} %get-tuple-element.276), channel_id=1, source_target_pairs={{0,24},{1,25},{2,26},{3,27},{4,28},{5,29},{6,30},{7,31},{8,16},{9,... | collective-permute-start | bytes 405512 | tf_op jit(solution)/shard_map/ppermute | solution.py:623
  460.5 66.1 %collective-permute-start.23 = (bf16[64,1536]{1,0:T(8,128)(2,1)}, bf16[64,1536]{1,0:T(8,128)(2,1)S(1)}, u32[]{:S(2)}, u32[]{:S(2)}) collective-permute-start(bf16[64,1536]{1,0:T(8,128)(2,1)} %get-tuple-element.273), channel_id=1, source_target_pairs={{0,8},{1,9},{2,10},{3,11},{4,12},{5,13},{6,14},{7,15},{8,0},{9,1},... | collective-permute-start | bytes 589832 | tf_op jit(solution)/shard_map/ppermute | solution.py:623
  461.2 65.4 %collective-permute-start.24 = (bf16[64,1536]{1,0:T(8,128)(2,1)}, bf16[64,1536]{1,0:T(8,128)(2,1)S(1)}, u32[]{:S(2)}, u32[]{:S(2)}) collective-permute-start(bf16[64,1536]{1,0:T(8,128)(2,1)} %get-tuple-element.272), channel_id=1, source_target_pairs={{0,16},{1,17},{2,18},{3,19},{4,20},{5,21},{6,22},{7,23},{8,24},{9,... | collective-permute-start | bytes 589832 | tf_op jit(solution)/shard_map/ppermute | solution.py:623
  554.5 21.4 %collective-permute-start.26 = (bf16[4,2,2,24,2304]{4,3,2,1,0:T(8,128)(2,1)}, bf16[4,2,2,24,2304]{4,3,2,1,0:T(8,128)(2,1)}, u32[]{:S(2)}, u32[]{:S(2)}) collective-permute-start(bf16[4,2,2,24,2304]{4,3,2,1,0:T(8,128)(2,1)} %fusion.2), channel_id=1, source_target_pairs={{0,2},{1,3},{2,0},{3,1},{4,6},{5,7},{6,4},{7,5},{8,10},{9,11},{10,... | collective-permute-start | bytes 5308424 | tf_op jit(solution)/shard_map/ppermute | solution.py:623
  573.4 32.7 %collective-permute-start.30 = (bf16[512,768]{1,0:T(8,128)(2,1)S(1)}, bf16[512,768]{1,0:T(8,128)(2,1)S(1)}, u32[]{:S(2)}, u32[]{:S(2)}) collective-permute-start(bf16[512,768]{1,0:T(8,128)(2,1)S(1)} %get-tuple-element.270), channel_id=1, source_target_pairs={{0,1},{1,0},{2,3},{3,2},{4,5},{5,4},{6,7},{7,6},{8,9},{9,8},{10,11... | collective-permute-start | bytes 2359304 | tf_op jit(solution)/shard_map/ppermute | solution.py:816
  595.2 22.5 %collective-permute-start.27 = (bf16[4,24,2304]{2,1,0:T(8,128)(2,1)S(1)}, bf16[4,24,2304]{2,1,0:T(8,128)(2,1)S(1)}, u32[]{:S(2)}, u32[]{:S(2)}) collective-permute-start(bf16[4,24,2304]{2,1,0:T(8,128)(2,1)S(1)} %get-tuple-element.260), channel_id=1, source_target_pairs={{0,1},{1,0},{2,3},{3,2},{4,5},{5,4},{6,7},{7,6},{8,9},{9,8},{10,11... | collective-permute-start | bytes 1327112 | tf_op jit(solution)/shard_map/ppermute | solution.py:623
  595.9 21.7 %collective-permute-start.28 = (bf16[4,24,2304]{2,1,0:T(8,128)(2,1)S(1)}, bf16[4,24,2304]{2,1,0:T(8,128)(2,1)S(1)}, u32[]{:S(2)}, u32[]{:S(2)}) collective-permute-start(bf16[4,24,2304]{2,1,0:T(8,128)(2,1)S(1)} %get-tuple-element.259), channel_id=1, source_target_pairs={{0,4},{1,5},{2,6},{3,7},{4,0},{5,1},{6,2},{7,3},{8,12},{9,13},{10,... | collective-permute-start | bytes 1327112 | tf_op jit(solution)/shard_map/ppermute | solution.py:623
  604.7 28.2 %collective-permute-start.41 = (bf16[512,768]{1,0:T(8,128)(2,1)}, bf16[512,768]{1,0:T(8,128)(2,1)}, u32[]{:S(2)}, u32[]{:S(2)}) collective-permute-start(bf16[512,768]{1,0:T(8,128)(2,1)} %get-tuple-element.269), channel_id=1, source_target_pairs={{0,1},{1,0},{2,3},{3,2},{4,5},{5,4},{6,7},{7,6},{8,9},{9,8},{10,11... | collective-permute-start | bytes 2359304 | tf_op jit(solution)/shard_map/ppermute | solution.py:816
  (54 other events, 652.0 us)
Sparse Core Ops, SparseCore 0:
  79.9 93.8 all-gather.2

commit v3 on v2

--- a/solution.py
+++ b/solution.py
@@ -166,12 +166,12 @@
     chunks = slots // k_tile
     length = lengths[pl.program_id(0)]
     lanes_k, lanes_q = lane_iota(slots), lane_iota(rows)
-    keys, values = k_ref[0].astype(f32), v_ref[0].astype(f32)
+    half = lax.broadcasted_iota(jnp.int32, (1, LANES), 1) < HEAD_DIM
     for h in range(2):
-        mine = (lanes_k < HEAD_DIM) == (h == 0)
-        ka[h, :, :LANES] = jnp.where(mine, keys, 0.0).astype(bf16)
+        mine = (half == (h == 0)).astype(f32).astype(bf16)
+        ka[h, :, :LANES] = k_ref[0] * mine
         ka[h, :, LANES:] = key_extra(slots, length, 3 * h, 3 * h + 3)
-        va[h, :, :LANES] = jnp.where(mine, values, 0.0).astype(bf16)
+        va[h, :, :LANES] = v_ref[0] * mine
         va[h, :, LANES:] = ((lanes_k >= 3 * h) & (lanes_k < 3 * h + 3)).astype(f32).astype(bf16)
         strips[h] = skewed(bias_ref[0, h : h + 1, :], width)
     qa[:, :LANES] = q_ref[0]
@@ -188,8 +188,8 @@
     which = lanes_q % 3
     da[:, :LANES] = d_ref[0]
     da[:, LANES:] = jnp.where(which == 0, one, jnp.where(which == 1, two, three)).astype(bf16)
-    q_turned[...] = q_ref[0].astype(f32).T.astype(bf16)
-    d_turned[...] = grads.T.astype(bf16)
+    q_turned[...] = q_ref[0].T
+    d_turned[...] = d_ref[0].T
     dk_acc[...] = jnp.zeros_like(dk_acc)
     dv_acc[...] = jnp.zeros_like(dv_acc)
     sums[...] = jnp.zeros_like(sums)
@@ -327,7 +327,7 @@
 BOTH = ("dp", "fsdp")
 FF_CHUNK = 512
 WO = slice(FF_CHUNK, FF_CHUNK + D)
-GROUP = 2
+GROUPS = (1, 2, 1, 2)
 FORWARD_TILES = (1024, 512)
 BACKWARD_TILES = (512, 256)
 
@@ -402,8 +402,11 @@
         down = slice(D + f0, D + f0 + FF_CHUNK)
         w_down = one_ref[:, ff] if f0 < 2 * D else two_ref[:, :FF_CHUNK]
         nf, seed = nf_ref[...], seed_ref[...]
-        gate = dot_nt(nf, wgu_ref[ff, :D])
-        up = dot_nt(nf, wgu_ref[ff, D:])
+        each = wgu_ref.shape[1]
+        w_gate = wgu_ref[f0 // each : (f0 + FF_CHUNK) // each, :, :D].reshape(FF_CHUNK, D)
+        w_up = wgu_ref[f0 // each : (f0 + FF_CHUNK) // each, :, D:].reshape(FF_CHUNK, D)
+        gate = dot_nt(nf, w_gate)
+        up = dot_nt(nf, w_up)
         back = dot_nn(seed, w_down)
         square = gate * gate
         root = 0.7978845608028654
@@ -415,7 +418,7 @@
         grad_gate = (back * up * slope).astype(bf16)
         grad_up = (back * active).astype(bf16)
         out_acc[...] += dot_nt(activated, w_down)
-        dnf_acc[...] += dot_nn(grad_gate, wgu_ref[ff, :D]) + dot_nn(grad_up, wgu_ref[ff, D:])
+        dnf_acc[...] += dot_nn(grad_gate, w_gate) + dot_nn(grad_up, w_up)
         dod[:, down] += dot_tn(seed, activated)
         dgu[ff, :D] += dot_tn(grad_gate, nf)
         dgu[ff, D:] += dot_tn(grad_up, nf)
@@ -462,7 +465,7 @@
     return lambda i, *_: (jnp.maximum(i - away, 0), 0)
 
 
-def ffn(x, attended, cotangent, w_one, w_two, wgu, gain, lengths, place, tile, rows, away):
+def ffn(x, attended, cotangent, w_one, w_two, rest, ff_share, gain, lengths, place, tile, rows, away):
     tokens = x.shape[0]
     steps = tokens // tile
     by_tile = lambda i, lengths, place: (tile_at(i, place, away, steps), 0)
@@ -479,7 +482,7 @@
                 pl.BlockSpec((tile, D), by_tile),
                 pl.BlockSpec((D, 2 * D), whole, pipeline_mode=single),
                 pl.BlockSpec((D, 2 * D), whole, pipeline_mode=single),
-                pl.BlockSpec((FF, 2 * D), whole, pipeline_mode=single),
+                pl.BlockSpec((rest.shape[0], ff_share, 2 * D), lambda i, *_: (0, 0, 0), pipeline_mode=single),
                 pl.BlockSpec((1, D), whole),
             ],
             out_specs=[
@@ -515,7 +518,7 @@
         compiler_params=pltpu.CompilerParams(vmem_limit_bytes=VMEM_LIMIT),
         cost_estimate=cost(95),
         name="ffn",
-    )(lengths, place, x, attended, cotangent, w_one, w_two, wgu, gain)
+    )(lengths, place, x, attended, cotangent, w_one, w_two, rest, gain)
 
 
 def weights_kernel(pieces, x_ref, gain_ref, *refs):
@@ -735,16 +738,15 @@
     gain_rows = wqkv[:, 3 * D : 3 * D + 2].astype(f32).T
     rest = jnp.concatenate(
         [
+            jnp.concatenate([turned(w_gate), turned(w_up)], axis=1),
             turned(w_down)[:, : 2 * D],
             jnp.pad(jnp.concatenate([turned(w_down)[:, 2 * D :], turned(w_out)], axis=1), ((0, 0), (0, 256))),
-            jnp.concatenate([turned(w_gate), turned(w_up)], axis=1),
         ]
     )
     rest = lax.all_gather(after(rest, wqkv), BOTH)
     share, ff_share = gain_attn.shape[0], w_gate.shape[1]
-    w_one = rest[:, :share].reshape(D, 2 * D)
-    w_two = rest[:, share : 2 * share].reshape(D, 2 * D)
-    wgu = rest[:, 2 * share :].reshape(FF, 2 * D)
+    w_one = rest[:, ff_share : ff_share + share].reshape(D, 2 * D)
+    w_two = rest[:, ff_share + share :].reshape(D, 2 * D)
     if swap:
         x = swap_in(inputs, jnp.concatenate(come), side)
         lengths = lax.dynamic_slice_in_dim(lengths, side, 1)
@@ -777,7 +779,7 @@
     else:
         seed = cotangent.reshape(-1, D)
     own, away_out, grad_hidden, grad_attended, dod, dgu, gain_two = ffn(
-        x, attended.reshape(-1, D), seed, w_one, w_two, wgu, gain_rows[1:2], lengths, place, tile, rows, away
+        x, attended.reshape(-1, D), seed, w_one, w_two, rest, ff_share, gain_rows[1:2], lengths, place, tile, rows, away
     )
     grad_attended = grad_attended.reshape(seqs, rows, D)
     dq, dk, dv, strips = [], [], [], []
@@ -786,19 +788,24 @@
     back = []
     if swap:
         back = [lax.ppermute(away_out, "fsdp", [(0, 1), (1, 0)])]
-    for low in range(0, PAIRS, GROUP):
+    low = 0
+    for stage, group in enumerate(GROUPS):
         one, two, three, strip = attention_backward(
-            qkv, sources, attended, grad_attended, extra, lengths, origin, vector, *back_tiles, low, GROUP
+            qkv, sources, attended, grad_attended, extra, lengths, origin, vector, *back_tiles, low, group
         )
         if rows < slots:
             two = lax.psum_scatter(two, "fsdp", scatter_dimension=1, tiled=True)
             three = lax.psum_scatter(three, "fsdp", scatter_dimension=1, tiled=True)
-        dq.append(one.reshape(-1, GROUP * LANES))
-        dk.append(two.reshape(-1, GROUP * LANES))
-        dv.append(three.reshape(-1, GROUP * LANES))
+        dq.append(one.reshape(-1, group * LANES))
+        dk.append(two.reshape(-1, group * LANES))
+        dv.append(three.reshape(-1, group * LANES))
         strips.append(strip)
-        moving, back, extra, dq, dk, dv = lax.optimization_barrier((moving, back, extra, dq, dk, dv))
-        moving = [s.send(m) for s, m in zip(scatters, moving)]
+        low += group
+        if stage < 3:
+            moving, extra, dq, dk, dv = lax.optimization_barrier((moving, extra, dq, dk, dv))
+            moving = [s.send(m) for s, m in zip(scatters, moving)]
+        else:
+            moving, back, dq, dk, dv = lax.optimization_barrier((moving, back, dq, dk, dv))
     out_down, gate_up = moving
     if swap:
         output = swap_out(own, back[0], side)

time: 657 us -> 652 us (level); the launches traced: 646 us -> 654 us
  Pallas kernels: 404 us -> 418 us
    pallas_call x1, Pallas kernels: 93.4 us -> 106 us  [ffn(): pl.pallas_call(functools.partial(ffn_kernel, tile, rows, away), grid_spec...]
    pallas_call x3 -> x4, Pallas kernels: 174 us -> 173 us  [attention_backward(): pl.pallas_call(functools.partial(backward_kernel, q_tile, k_tile), grid_s...]
  transfers between devices with their start and end apart: 43 -> 43, of which waited for: 14 -> 13; matrix products, arithmetic and copies ran while one was open for 7% -> 6% of each run, Pallas kernels for 46% -> 46%
where the time goes in v3:
time: 652 us; the launch traced here: 654 us
  Pallas kernels  418 us (64%)
  waiting for transfers between devices  79.4 us (12%)
  starting transfers between devices  51.1 us (8%)
  other arithmetic  44.9 us (7%)
  local copies, waits for them, and re-layouts  43 us (7%)
  between operations  15.2 us (2%)
    pallas_call x4, Pallas kernels, attention_backward(): pl.pallas_call(functools.partial(backward_kernel, q_tile, k_tile), grid_s...  173 us
    pallas_call x1, Pallas kernels, ffn(): pl.pallas_call(functools.partial(ffn_kernel, tile, rows, away), grid_spec...  106 us
    pallas_call x1, Pallas kernels, attention_forward(): pl.pallas_call(functools.partial(forward_kernel, q_tile, k_tile), grid_sp...  93 us
    ppermute x35, waiting for transfers between devices, from_peer(): lax.ppermute(value, BOTH, [(n, n ^ flip) for n in range(SQUARE_DEVICES)])  54.1 us
    ppermute x35, starting transfers between devices, from_peer(): lax.ppermute(value, BOTH, [(n, n ^ flip) for n in range(SQUARE_DEVICES)])  41.7 us
    ppermute x5, waiting for transfers between devices, per_device(): lax.ppermute(part, 'fsdp', [(0, 1), (1, 0)])  25.2 us
    pallas_call x1, Pallas kernels, finish_inputs(): pl.pallas_call(functools.partial(finish_kernel, away, len(dq)), grid_spec...  19.2 us
    pallas_call x1, Pallas kernels, finish_weights(): pl.pallas_call(functools.partial(weights_kernel, len(dq)), grid=(tokens /...  14.6 us
  transfers between devices with their start and end apart: 43, of which 13 were waited for; matrix products, arithmetic and copies ran while one was open for 6% of the time, Pallas kernels for 46%

profile of v3, /device:TPU:0, one launch (start us, length us, event | category | flops | bytes accessed | tf_op | source)
XLA Modules:
  0.0 653.9 jit_solution(16977045990109715099)
XLA Ops:
  7.3 3.3 dynamic-slice_bitcast_fusion.3
  11.5 3.0 collective-permute-start
  20.9 7.1 %collective-permute-done.4 = bf16[24,2432]{1,0:T(8,128)(2,1)} collective-permute-done((bf16[24,2432]{1,0:T(8,128)(2,1)S(1)}, bf16[24,2432]{1,0:T(8,128)(2,1)}, u32[]{:S(2)}, u32[]{:S(2)}) %collective-permute-start.4) | collective-permute-done | bytes 116768 | tf_op jit(solution)/shard_map/ppermute | solution.py:626
  33.9 9.7 %collective-permute-done.1 = bf16[384,768]{1,0:T(8,128)(2,1)S(1)} collective-permute-done((bf16[384,768]{1,0:T(8,128)(2,1)S(1)}, bf16[384,768]{1,0:T(8,128)(2,1)S(1)}, u32[]{:S(2)}, u32[]{:S(2)}) %collective-permute-start.1) | collective-permute-done | bytes 589856 | tf_op jit(solution)/shard_map/ppermute | solution.py:731
  43.6 17.1 %collective-permute-done.6 = bf16[4,24,2432]{2,1,0:T(8,128)(2,1)} collective-permute-done((bf16[4,24,2432]{2,1,0:T(8,128)(2,1)S(1)}, bf16[4,24,2432]{2,1,0:T(8,128)(2,1)}, u32[]{:S(2)}, u32[]{:S(2)}) %collective-permute-start.6) | collective-permute-done | bytes 466976 | tf_op jit(solution)/shard_map/ppermute | solution.py:626
  68.2 7.2 %collective-permute-done.2 = bf16[256,768]{1,0:T(8,128)(2,1)S(1)} collective-permute-done((bf16[256,768]{1,0:T(8,128)(2,1)}, bf16[256,768]{1,0:T(8,128)(2,1)S(1)}, u32[]{:S(2)}, u32[]{:S(2)}) %collective-permute-start.2) | collective-permute-done | bytes 393248 | tf_op jit(solution)/shard_map/ppermute | solution.py:731
  83.6 3.0 maximum_select_fusion.2.x_ref
  91.4 12.1 %project.1 = bf16[2048,2304]{1,0:T(8,128)(2,1)} custom-call(bf16[2048,768]{1,0:T(8,128)(2,1)} %maximum_select_fusion.2.x_ref, bf16[768,2432]{1,0:T(8,128)(2,1)} %bitcast.183, f32[1,768]{1,0:T(1,128)} %get-tuple-element.330.gain_ref), custom_call_target="tpu_custom_call" | custom-call | flops 13200000000 | bytes 1048576 | tf_op jit(solution)/shard_map/project/pallas_call | solution.py:356
  103.5 93.0 %attention_forward.1 = (bf16[1,2048,768]{2,1,0:T(8,128)(2,1)}, bf16[1,6,2048,128]{3,2,1,0:T(8,128)(2,1)}) custom-call(s32[1]{0:T(128)} %dynamic_slice.118.lengths, s32[1]{0:T(128)} %constant.233.clone.1.offset, bf16[1,2048,2304]{2,1,0:T(8,128)(2,1)} %bitcast.195, bf16[1,2048,2304]{2,1,0:T(8,128)(2,1)} %bitcast.196, bf16[1,2048,2304]{2,1,0:T(8,128)(2,1)} %bitcast.197, ...), custom_call_target="tpu_custom_call" | custom-call | flops 109999996928 | bytes 1048576 | tf_op jit(solution)/shard_map/attention_forward/pallas_call | solution.py:125
  198.6 4.8 fusion.56
  203.5 106.0 %ffn.1 = (f32[1024,768]{1,0:T(8,128)}, bf16[1024,768]{1,0:T(8,128)(2,1)}, f32[2048,768]{1,0:T(8,128)}, bf16[2048,768]{1,0:T(8,128)(2,1)}, f32[768,2816]{1,0:T(8,...) custom-call(s32[1]{0:T(128)} %dynamic_slice.118.lengths, s32[2]{0:T(128)} %pad_add_fusion.place, ...), custom_call_target="tpu_custom_call" | custom-call | flops 104500002816 | bytes 1048576 | tf_op jit(solution)/shard_map/ffn/pallas_call | solution.py:474
  309.5 3.2 fusion
  312.8 3.8 fusion.1
  317.0 29.7 %attention_backward.4 = (bf16[1,2048,128]{2,1,0:T(8,128)(2,1)}, bf16[1,2048,128]{2,1,0:T(8,128)(2,1)}, bf16[1,2048,128]{2,1,0:T(8,128)(2,1)}, f32[1,1,2,1792]{3,2,1,0:T(2,128)}) custom-call(s32[1]{0:T(128)} %dynamic_slice.118.lengths, s32[1]{0:T(128)} %constant.233.clone.1.offset, bf16[1,2048,2304]{2,1,0:T(8,128)(2,1)} %bitcast.198, ...), custom_call_target="tpu_custom_call" | custom-call | flops 32999999488 | bytes 1048576 | tf_op jit(solution)/shard_map/attention_backward/pallas_call | solution.py:256
  346.7 3.5 bitcast_add_fusion.1
  355.4 3.0 bitcast_add_fusion
  370.8 57.0 %attention_backward.5 = (bf16[1,2048,256]{2,1,0:T(8,128)(2,1)}, bf16[1,2048,256]{2,1,0:T(8,128)(2,1)}, bf16[1,2048,256]{2,1,0:T(8,128)(2,1)}, f32[1,2,2,1792]{3,2,1,0:T(2,128)}) custom-call(s32[1]{0:T(128)} %dynamic_slice.118.lengths, s32[1]{0:T(128)} %constant.233.clone.1.offset, bf16[1,2048,2304]{2,1,0:T(8,128)(2,1)} %bitcast.201, ...), custom_call_target="tpu_custom_call" | custom-call | flops 65999998976 | bytes 1048576 | tf_op jit(solution)/shard_map/attention_backward/pallas_call | solution.py:256
  443.3 29.6 %attention_backward.6 = (bf16[1,2048,128]{2,1,0:T(8,128)(2,1)}, bf16[1,2048,128]{2,1,0:T(8,128)(2,1)}, bf16[1,2048,128]{2,1,0:T(8,128)(2,1)}, f32[1,1,2,1792]{3,2,1,0:T(2,128)}) custom-call(s32[1]{0:T(128)} %dynamic_slice.118.lengths, s32[1]{0:T(128)} %constant.233.clone.1.offset, bf16[1,2048,2304]{2,1,0:T(8,128)(2,1)} %bitcast.204, ...), custom_call_target="tpu_custom_call" | custom-call | flops 32999999488 | bytes 1048576 | tf_op jit(solution)/shard_map/attention_backward/pallas_call | solution.py:256
  474.5 57.2 %attention_backward.7 = (bf16[1,2048,256]{2,1,0:T(8,128)(2,1)}, bf16[1,2048,256]{2,1,0:T(8,128)(2,1)}, bf16[1,2048,256]{2,1,0:T(8,128)(2,1)}, f32[1,2,2,1792]{3,2,1,0:T(2,128)}) custom-call(s32[1]{0:T(128)} %dynamic_slice.118.lengths, s32[1]{0:T(128)} %constant.233.clone.1.offset, bf16[1,2048,2304]{2,1,0:T(8,128)(2,1)} %bitcast.207, ...), custom_call_target="tpu_custom_call" | custom-call | flops 65999998976 | bytes 1048576 | tf_op jit(solution)/shard_map/attention_backward/pallas_call | solution.py:256
  541.3 14.6 %finish_weights.1 = f32[768,2304]{1,0:T(8,128)} custom-call(bf16[2048,768]{1,0:T(8,128)(2,1)} %maximum_select_fusion.2.x_ref, f32[1,768]{1,0:T(1,128)} %get-tuple-element.330.gain_ref, bf16[2048,128]{1,0:T(8,128)(2,1)} %bitcast.227, bf16[2048,256]{1,0:T(8,128)(2,1)} %bitcast.215, bf16[2048,128]{1,0:T(8,128)(2,1)} %bitcast.233, bf16[2048,256]{1,0:T(8,128)(2,1)} %bitcast.221, ...), custom_call_target="tpu_custom_call" | custom-call | flops 15399999488 | bytes 1048576 | tf_op jit(solution)/shard_map/finish_weights/pallas_call | solution.py:544
  558.2 19.2 %finish_inputs.1 = (f32[1024,768]{1,0:T(8,128)}, bf16[1024,768]{1,0:T(8,128)(2,1)}, f32[1,768]{1,0:T(1,128)}) custom-call(s32[2]{0:T(128)} %pad_add_fusion.place, bf16[2048,768]{1,0:T(8,128)(2,1)} %maximum_select_fusion.2.x_ref, f32[2048,768]{1,0:T(8,128)} %get-tuple-element.223.gh_ref, bf16[768,2432]{1,0:T(8,128)(2,1)} %bitcast.184, ...), custom_call_target="tpu_custom_call" | custom-call | flops 17600000000 | bytes 1048576 | tf_op jit(solution)/shard_map/finish_inputs/pallas_call | solution.py:592
  588.7 11.6 %collective-permute-done.32 = f32[3,768]{1,0:T(4,128)S(1)} collective-permute-done((f32[3,768]{1,0:T(4,128)S(1)}, f32[3,768]{1,0:T(4,128)S(1)}, u32[]{:S(2)}, u32[]{:S(2)}) %collective-permute-start.32) | collective-permute-done | bytes 9248 | tf_op jit(solution)/shard_map/ppermute | solution.py:626
  612.5 13.0 %collective-permute-done.27 = bf16[4,24,2304]{2,1,0:T(8,128)(2,1)S(1)} collective-permute-done((bf16[4,24,2304]{2,1,0:T(8,128)(2,1)S(1)}, bf16[4,24,2304]{2,1,0:T(8,128)(2,1)S(1)}, u32[]{:S(2)}, u32[]{:S(2)}) %collective-permute-start.27) | collective-permute-done | bytes 442400 | tf_op jit(solution)/shard_map/ppermute | solution.py:626
  633.1 7.5 %collective-permute-done.41 = bf16[512,768]{1,0:T(8,128)(2,1)} collective-permute-done((bf16[512,768]{1,0:T(8,128)(2,1)}, bf16[512,768]{1,0:T(8,128)(2,1)}, u32[]{:S(2)}, u32[]{:S(2)}) %collective-permute-start.41) | collective-permute-done | bytes 786464 | tf_op jit(solution)/shard_map/ppermute | solution.py:823
  (238 shorter events, 119.6 us)
Async XLA Ops:
  7.2 191.4 %all-gather.3.cloned.1.call-start = ((), (), s32[]{:S(2)}) async-start(), calls=%async_computation | async-start | bytes 11354112 | tf_op jit(solution)/shard_map/all_gather | solution.py:746
  19.1 24.5 %collective-permute-start.1 = (bf16[384,768]{1,0:T(8,128)(2,1)S(1)}, bf16[384,768]{1,0:T(8,128)(2,1)S(1)}, u32[]{:S(2)}, u32[]{:S(2)}) collective-permute-start(bf16[384,768]{1,0:T(8,128)(2,1)S(1)} %get-tuple-element.313), channel_id=1, source_target_pairs={{0,1},{1,0},{2,3},{3,2},{4,5},{5,4},{6,7},{7,6},{8,9},{9,8},{10,11... | collective-permute-start | bytes 1769480 | tf_op jit(solution)/shard_map/ppermute | solution.py:731
  30.2 30.5 %collective-permute-start.6 = (bf16[4,24,2432]{2,1,0:T(8,128)(2,1)S(1)}, bf16[4,24,2432]{2,1,0:T(8,128)(2,1)}, u32[]{:S(2)}, u32[]{:S(2)}) collective-permute-start(bf16[4,24,2432]{2,1,0:T(8,128)(2,1)S(1)} %pad_maximum_fusion.2), channel_id=1, source_target_pairs={{0,1},{1,0},{2,3},{3,2},{4,5},{5,4},{6,7},{7,6},{8,9},{9,8},{10,11... | collective-permute-start | bytes 1400840 | tf_op jit(solution)/shard_map/ppermute | solution.py:626
  32.3 28.4 %collective-permute-start.7 = (bf16[4,24,2432]{2,1,0:T(8,128)(2,1)S(1)}, bf16[4,24,2432]{2,1,0:T(8,128)(2,1)}, u32[]{:S(2)}, u32[]{:S(2)}) collective-permute-start(bf16[4,24,2432]{2,1,0:T(8,128)(2,1)S(1)} %pad_maximum_fusion.2), channel_id=1, source_target_pairs={{0,4},{1,5},{2,6},{3,7},{4,0},{5,1},{6,2},{7,3},{8,12},{9,13},{10,... | collective-permute-start | bytes 1400840 | tf_op jit(solution)/shard_map/ppermute | solution.py:626
  33.8 26.9 %collective-permute-start.8 = (bf16[4,24,2432]{2,1,0:T(8,128)(2,1)S(1)}, bf16[4,24,2432]{2,1,0:T(8,128)(2,1)}, u32[]{:S(2)}, u32[]{:S(2)}) collective-permute-start(bf16[4,24,2432]{2,1,0:T(8,128)(2,1)S(1)} %pad_maximum_fusion.2), channel_id=1, source_target_pairs={{0,5},{1,4},{2,7},{3,6},{4,1},{5,0},{6,3},{7,2},{8,13},{9,12},{10,... | collective-permute-start | bytes 1400840 | tf_op jit(solution)/shard_map/ppermute | solution.py:626
  87.9 108.6 %collective-permute-start.10 = (bf16[1024,768]{1,0:T(8,128)(2,1)}, bf16[1024,768]{1,0:T(8,128)(2,1)S(1)}, u32[]{:S(2)}, u32[]{:S(2)}) collective-permute-start(bf16[1024,768]{1,0:T(8,128)(2,1)} %get-tuple-element.300), channel_id=1, source_target_pairs={{0,1},{1,0},{2,3},{3,2},{4,5},{5,4},{6,7},{7,6},{8,9},{9,8},{10,11... | collective-permute-start | bytes 4718600 | tf_op jit(solution)/shard_map/ppermute | solution.py:690
  312.7 34.0 %collective-permute-start.12 = (bf16[4,2,2,64,1536]{4,3,2,1,0:T(8,128)(2,1)S(1)}, bf16[4,2,2,64,1536]{4,3,2,1,0:T(8,128)(2,1)}, u32[]{:S(2)}, u32[]{:S(2)}) collective-permute-start(bf16[4,2,2,64,1536]{4,3,2,1,0:T(8,128)(2,1)S(1)} %fusion), channel_id=1, source_target_pairs={{0,2},{1,3},{2,0},{3,1},{4,6},{5,7},{6,4},{7,5},{8,10},{9,11},{10,... | collective-permute-start | bytes 9437192 | tf_op jit(solution)/shard_map/ppermute | solution.py:626
  316.5 30.1 %collective-permute-start.11 = (bf16[4,2,2,24,2816]{4,3,2,1,0:T(8,128)(2,1)}, bf16[4,2,2,24,2816]{4,3,2,1,0:T(8,128)(2,1)}, u32[]{:S(2)}, u32[]{:S(2)}) collective-permute-start(bf16[4,2,2,24,2816]{4,3,2,1,0:T(8,128)(2,1)} %fusion.1), channel_id=1, source_target_pairs={{0,2},{1,3},{2,0},{3,1},{4,6},{5,7},{6,4},{7,5},{8,10},{9,11},{10,... | collective-permute-start | bytes 6488072 | tf_op jit(solution)/shard_map/ppermute | solution.py:626
  362.7 65.0 %collective-permute-start.16 = (bf16[4,64,1536]{2,1,0:T(8,128)(2,1)}, bf16[4,64,1536]{2,1,0:T(8,128)(2,1)S(1)}, u32[]{:S(2)}, u32[]{:S(2)}) collective-permute-start(bf16[4,64,1536]{2,1,0:T(8,128)(2,1)} %get-tuple-element.290), channel_id=1, source_target_pairs={{0,1},{1,0},{2,3},{3,2},{4,5},{5,4},{6,7},{7,6},{8,9},{9,8},{10,11... | collective-permute-start | bytes 2359304 | tf_op jit(solution)/shard_map/ppermute | solution.py:626
  363.2 64.6 %collective-permute-start.17 = (bf16[4,64,1536]{2,1,0:T(8,128)(2,1)S(1)}, bf16[4,64,1536]{2,1,0:T(8,128)(2,1)S(1)}, u32[]{:S(2)}, u32[]{:S(2)}) collective-permute-start(bf16[4,64,1536]{2,1,0:T(8,128)(2,1)S(1)} %get-tuple-element.289), channel_id=1, source_target_pairs={{0,4},{1,5},{2,6},{3,7},{4,0},{5,1},{6,2},{7,3},{8,12},{9,13},{10,... | collective-permute-start | bytes 2359304 | tf_op jit(solution)/shard_map/ppermute | solution.py:626
  364.8 63.0 %collective-permute-start.18 = (bf16[4,64,1536]{2,1,0:T(8,128)(2,1)S(1)}, bf16[4,64,1536]{2,1,0:T(8,128)(2,1)S(1)}, u32[]{:S(2)}, u32[]{:S(2)}) collective-permute-start(bf16[4,64,1536]{2,1,0:T(8,128)(2,1)S(1)} %get-tuple-element.288), channel_id=1, source_target_pairs={{0,5},{1,4},{2,7},{3,6},{4,1},{5,0},{6,3},{7,2},{8,13},{9,12},{10,... | collective-permute-start | bytes 2359304 | tf_op jit(solution)/shard_map/ppermute | solution.py:626
  366.2 61.5 %collective-permute-start.14 = (bf16[4,24,2816]{2,1,0:T(8,128)(2,1)}, bf16[4,24,2816]{2,1,0:T(8,128)(2,1)}, u32[]{:S(2)}, u32[]{:S(2)}) collective-permute-start(bf16[4,24,2816]{2,1,0:T(8,128)(2,1)} %get-tuple-element.292), channel_id=1, source_target_pairs={{0,4},{1,5},{2,6},{3,7},{4,0},{5,1},{6,2},{7,3},{8,12},{9,13},{10,... | collective-permute-start | bytes 1622024 | tf_op jit(solution)/shard_map/ppermute | solution.py:626
  369.2 58.5 %collective-permute-start.15 = (bf16[4,24,2816]{2,1,0:T(8,128)(2,1)}, bf16[4,24,2816]{2,1,0:T(8,128)(2,1)}, u32[]{:S(2)}, u32[]{:S(2)}) collective-permute-start(bf16[4,24,2816]{2,1,0:T(8,128)(2,1)} %get-tuple-element.291), channel_id=1, source_target_pairs={{0,5},{1,4},{2,7},{3,6},{4,1},{5,0},{6,3},{7,2},{8,13},{9,12},{10,... | collective-permute-start | bytes 1622024 | tf_op jit(solution)/shard_map/ppermute | solution.py:626
  435.0 39.4 %collective-permute-start.22 = (bf16[64,1536]{1,0:T(8,128)(2,1)S(1)}, bf16[64,1536]{1,0:T(8,128)(2,1)S(1)}, u32[]{:S(2)}, u32[]{:S(2)}) collective-permute-start(bf16[64,1536]{1,0:T(8,128)(2,1)S(1)} %get-tuple-element.311), channel_id=1, source_target_pairs={{0,8},{1,9},{2,10},{3,11},{4,12},{5,13},{6,14},{7,15},{8,0},{9,1},... | collective-permute-start | bytes 589832 | tf_op jit(solution)/shard_map/ppermute | solution.py:626
  435.5 38.9 %collective-permute-start.23 = (bf16[64,1536]{1,0:T(8,128)(2,1)S(1)}, bf16[64,1536]{1,0:T(8,128)(2,1)S(1)}, u32[]{:S(2)}, u32[]{:S(2)}) collective-permute-start(bf16[64,1536]{1,0:T(8,128)(2,1)S(1)} %get-tuple-element.310), channel_id=1, source_target_pairs={{0,16},{1,17},{2,18},{3,19},{4,20},{5,21},{6,22},{7,23},{8,24},{9,... | collective-permute-start | bytes 589832 | tf_op jit(solution)/shard_map/ppermute | solution.py:626
  438.1 36.4 %collective-permute-start.24 = (bf16[64,1536]{1,0:T(8,128)(2,1)S(1)}, bf16[64,1536]{1,0:T(8,128)(2,1)S(1)}, u32[]{:S(2)}, u32[]{:S(2)}) collective-permute-start(bf16[64,1536]{1,0:T(8,128)(2,1)S(1)} %get-tuple-element.309), channel_id=1, source_target_pairs={{0,24},{1,25},{2,26},{3,27},{4,28},{5,29},{6,30},{7,31},{8,16},{9,... | collective-permute-start | bytes 589832 | tf_op jit(solution)/shard_map/ppermute | solution.py:626
  439.4 33.4 %collective-permute-start.20 = (bf16[24,2816]{1,0:T(8,128)(2,1)}, bf16[24,2816]{1,0:T(8,128)(2,1)S(1)}, u32[]{:S(2)}, u32[]{:S(2)}) collective-permute-start(bf16[24,2816]{1,0:T(8,128)(2,1)} %get-tuple-element.315), channel_id=1, source_target_pairs={{0,16},{1,17},{2,18},{3,19},{4,20},{5,21},{6,22},{7,23},{8,24},{9,... | collective-permute-start | bytes 405512 | tf_op jit(solution)/shard_map/ppermute | solution.py:626
  441.1 33.3 %collective-permute-start.21 = (bf16[24,2816]{1,0:T(8,128)(2,1)}, bf16[24,2816]{1,0:T(8,128)(2,1)}, u32[]{:S(2)}, u32[]{:S(2)}) collective-permute-start(bf16[24,2816]{1,0:T(8,128)(2,1)} %get-tuple-element.314), channel_id=1, source_target_pairs={{0,24},{1,25},{2,26},{3,27},{4,28},{5,29},{6,30},{7,31},{8,16},{9,... | collective-permute-start | bytes 405512 | tf_op jit(solution)/shard_map/ppermute | solution.py:626
  472.9 63.9 %collective-permute-start.25 = (bf16[1024,768]{1,0:T(8,128)(2,1)}, bf16[1024,768]{1,0:T(8,128)(2,1)}, u32[]{:S(2)}, u32[]{:S(2)}) collective-permute-start(bf16[1024,768]{1,0:T(8,128)(2,1)} %get-tuple-element.192), channel_id=1, source_target_pairs={{0,1},{1,0},{2,3},{3,2},{4,5},{5,4},{6,7},{7,6},{8,9},{9,8},{10,11... | collective-permute-start | bytes 4718600 | tf_op jit(solution)/shard_map/ppermute | solution.py:790
  558.1 23.0 %collective-permute-start.26 = (bf16[4,2,2,24,2304]{4,3,2,1,0:T(8,128)(2,1)S(1)}, bf16[4,2,2,24,2304]{4,3,2,1,0:T(8,128)(2,1)S(1)}, u32[]{:S(2)}, u32[]{:S(2)}) collective-permute-start(bf16[4,2,2,24,2304]{4,3,2,1,0:T(8,128)(2,1)S(1)} %fusion.2), channel_id=1, source_target_pairs={{0,2},{1,3},{2,0},{3,1},{4,6},{5,7},{6,4},{7,5},{8,10},{9,11},{10,... | collective-permute-start | bytes 5308424 | tf_op jit(solution)/shard_map/ppermute | solution.py:626
  579.9 32.6 %collective-permute-start.30 = (bf16[512,768]{1,0:T(8,128)(2,1)S(1)}, bf16[512,768]{1,0:T(8,128)(2,1)S(1)}, u32[]{:S(2)}, u32[]{:S(2)}) collective-permute-start(bf16[512,768]{1,0:T(8,128)(2,1)S(1)} %get-tuple-element.308), channel_id=1, source_target_pairs={{0,1},{1,0},{2,3},{3,2},{4,5},{5,4},{6,7},{7,6},{8,9},{9,8},{10,11... | collective-permute-start | bytes 2359304 | tf_op jit(solution)/shard_map/ppermute | solution.py:823
  602.8 22.6 %collective-permute-start.27 = (bf16[4,24,2304]{2,1,0:T(8,128)(2,1)S(1)}, bf16[4,24,2304]{2,1,0:T(8,128)(2,1)S(1)}, u32[]{:S(2)}, u32[]{:S(2)}) collective-permute-start(bf16[4,24,2304]{2,1,0:T(8,128)(2,1)S(1)} %get-tuple-element.298), channel_id=1, source_target_pairs={{0,1},{1,0},{2,3},{3,2},{4,5},{5,4},{6,7},{7,6},{8,9},{9,8},{10,11... | collective-permute-start | bytes 1327112 | tf_op jit(solution)/shard_map/ppermute | solution.py:626
  603.4 22.0 %collective-permute-start.28 = (bf16[4,24,2304]{2,1,0:T(8,128)(2,1)S(1)}, bf16[4,24,2304]{2,1,0:T(8,128)(2,1)S(1)}, u32[]{:S(2)}, u32[]{:S(2)}) collective-permute-start(bf16[4,24,2304]{2,1,0:T(8,128)(2,1)S(1)} %get-tuple-element.297), channel_id=1, source_target_pairs={{0,4},{1,5},{2,6},{3,7},{4,0},{5,1},{6,2},{7,3},{8,12},{9,13},{10,... | collective-permute-start | bytes 1327112 | tf_op jit(solution)/shard_map/ppermute | solution.py:626
  611.9 28.7 %collective-permute-start.41 = (bf16[512,768]{1,0:T(8,128)(2,1)}, bf16[512,768]{1,0:T(8,128)(2,1)}, u32[]{:S(2)}, u32[]{:S(2)}) collective-permute-start(bf16[512,768]{1,0:T(8,128)(2,1)} %get-tuple-element.307), channel_id=1, source_target_pairs={{0,1},{1,0},{2,3},{3,2},{4,5},{5,4},{6,7},{7,6},{8,9},{9,8},{10,11... | collective-permute-start | bytes 2359304 | tf_op jit(solution)/shard_map/ppermute | solution.py:823
  (60 other events, 874.8 us)
Sparse Core Ops, SparseCore 0:
  80.0 93.8 all-gather.2

commit v4 on v3

--- a/solution.py
+++ b/solution.py
@@ -521,8 +521,8 @@
     )(lengths, place, x, attended, cotangent, w_one, w_two, rest, gain)
 
 
-def weights_kernel(pieces, x_ref, gain_ref, *refs):
-    grads, dw_ref = refs[:-1], refs[-1]
+def weights_kernel(pieces, x_ref, gain_ref, w_ref, *refs):
+    grads, (dw_ref, gain_out) = refs[:-2], refs[-2:]
 
     @pl.when(pl.program_id(0) == 0)
     def _():
@@ -537,30 +537,38 @@
             dw_ref[rows, n * D : (n + 1) * D] += dot_tn(ref[...], normed)
             row += ref.shape[1]
 
-
-def finish_weights(x, gain, dq, dk, dv, tile):
+    @pl.when(pl.program_id(0) == pl.num_programs(0) - 1)
+    def _():
+        together = 0.0
+        for n in range(3):
+            part = slice(n * D, (n + 1) * D)
+            together += jnp.sum(dw_ref[:, part] * w_ref[:, part].astype(f32), axis=0, keepdims=True)
+        gain_out[...] = together / gain_ref[...]
+
+
+def finish_weights(x, gain, weights, dq, dk, dv, tile):
     tokens = x.shape[0]
     grads = [*dq, *dk, *dv]
     return pl.pallas_call(
         functools.partial(weights_kernel, len(dq)),
         grid=(tokens // tile,),
-        in_specs=[pl.BlockSpec((tile, D), lambda i: (i, 0)), pl.BlockSpec((1, D), lambda i: (0, 0))]
+        in_specs=[
+            pl.BlockSpec((tile, D), lambda i: (i, 0)),
+            pl.BlockSpec((1, D), lambda i: (0, 0)),
+            pl.BlockSpec((D, 3 * D), lambda i: (0, 0)),
+        ]
         + [pl.BlockSpec((tile, g.shape[1]), lambda i: (i, 0)) for g in grads],
-        out_specs=pl.BlockSpec((sum(g.shape[1] for g in dq), 3 * D), lambda i: (0, 0)),
-        out_shape=jax.ShapeDtypeStruct((sum(g.shape[1] for g in dq), 3 * D), f32),
+        out_specs=[pl.BlockSpec((D, 3 * D), lambda i: (0, 0)), pl.BlockSpec((1, D), lambda i: (0, 0))],
+        out_shape=[jax.ShapeDtypeStruct((D, 3 * D), f32), jax.ShapeDtypeStruct((1, D), f32)],
         compiler_params=pltpu.CompilerParams(vmem_limit_bytes=VMEM_LIMIT),
         cost_estimate=cost(14),
         name="finish_weights",
-    )(x, gain, *grads)
+    )(x, gain, weights, *grads)
 
 
 def finish_kernel(away, pieces, place, x_ref, gh_ref, w_ref, gain_ref, *refs):
-    grads, (own_ref, away_ref, gain_out) = refs[:-3], refs[-3:]
+    grads, (own_ref, away_ref) = refs[:-2], refs[-2:]
     step = pl.program_id(0)
-
-    @pl.when(step == 0)
-    def _():
-        gain_out[...] = jnp.zeros_like(gain_out)
 
     grad_normed = None
     for n in range(3):
@@ -571,7 +579,6 @@
             row += ref.shape[1]
     x = x_ref[...].astype(f32)
     factor = rms_factor(x)
-    gain_out[...] += jnp.sum(grad_normed * x * factor, axis=0, keepdims=True)
     grad_x = gh_ref[...] + norm_back(grad_normed, x, factor, gain_ref[...])
 
     @pl.when(step < away)
@@ -604,13 +611,11 @@
             out_specs=[
                 pl.BlockSpec((tile, D), own_index(away)),
                 pl.BlockSpec((tile, D), away_index(away)),
-                pl.BlockSpec((1, D), whole),
             ],
         ),
         out_shape=[
             jax.ShapeDtypeStruct((tokens - away * tile, D), f32),
             jax.ShapeDtypeStruct((max(away, 1) * tile, D), bf16),
-            jax.ShapeDtypeStruct((1, D), f32),
         ],
         compiler_params=pltpu.CompilerParams(vmem_limit_bytes=VMEM_LIMIT),
         cost_estimate=cost(16),
@@ -681,8 +686,8 @@
 
 def sum_all(value):
     value = value + from_peer(value, CORE)
-    value = value + (from_peer(value, Y) + from_peer(value, X) + from_peer(value, X + Y))
-    return value + (from_peer(value, Z) + from_peer(value, 2 * Z) + from_peer(value, 3 * Z))
+    value = value + (from_peer(value, Z) + from_peer(value, 2 * Z) + from_peer(value, 3 * Z))
+    return value + (from_peer(value, Y) + from_peer(value, X) + from_peer(value, X + Y))
 
 
 def swap_start(block, side):
@@ -811,26 +816,20 @@
         output = swap_out(own, back[0], side)
     else:
         output = own.reshape(seqs, rows, D)
-    dq = after(dq, output)
-    dw = finish_weights(x, gain_rows[0:1], dq, dk, dv, tile)
+    diagonals = jnp.sum(jnp.concatenate(strips, axis=1), axis=0).reshape(HEADS, -1)
+    table = jnp.dot(diagonals, one_hot, precision=PRECISE).T
+    table = jnp.pad(table.reshape(1, -1), ((0, 0), (0, D - BUCKETS * HEADS)))
+    dq = after(dq, output, table)
+    dw, gain_one = finish_weights(x, gain_rows[0:1], wqkv, dq, dk, dv, tile)
     scatter_qk = scatter(dw)
     moving = next(scatter_qk)
-    own, away_grad, gain_one = finish_inputs(
-        x, grad_hidden, wqkv, gain_rows[0:1], after(dq, dw), dk, dv, place, tile, away
-    )
-    moving, own, gain_one = lax.optimization_barrier((moving, own, gain_one))
-    if swap:
-        back = [lax.ppermute(part, "fsdp", [(0, 1), (1, 0)]) for part in jnp.split(away_grad, 2)]
-    else:
-        back = [own, own]
+    moving, dq = lax.optimization_barrier((moving, dq))
     moving = scatter_qk.send(moving)
-    diagonals = jnp.sum(jnp.concatenate(strips, axis=1), axis=0).reshape(HEADS, -1)
-    table = jnp.dot(diagonals, one_hot, precision=PRECISE).T
-    small = jnp.concatenate([gain_one, gain_two, jnp.pad(table.reshape(1, -1), ((0, 0), (0, D - BUCKETS * HEADS)))])
-    small = total(small)
-    moving, back[0], small = lax.optimization_barrier((moving, back[0], small))
+    small = total(jnp.concatenate([gain_one, gain_two, table]))
+    own, away_grad = finish_inputs(x, grad_hidden, wqkv, gain_rows[0:1], dq, dk, dv, place, tile, away)
+    moving, small, own, away_grad = lax.optimization_barrier((moving, small, own, away_grad))
+    back = [lax.ppermute(away_grad, "fsdp", [(0, 1), (1, 0)])] if swap else []
     moving = scatter_qk.send(moving)
-    moving, back[1] = lax.optimization_barrier((moving, back[1]))
     query_key = scatter_qk.send(moving)
     gain_shares = lax.dynamic_slice_in_dim(small[:2], lax.axis_index(BOTH) * gain_attn.shape[0], gain_attn.shape[0], 1)
     if swap:

time: 652 us -> 647 us (level)
  waiting for transfers between devices: 79.4 us -> 68.7 us
    ppermute x35, waiting for transfers between devices: 54.1 us -> 33.8 us  [from_peer(): lax.ppermute(value, BOTH, [(n, n ^ flip) for n in range(SQUARE_DEVICES)])]
    ppermute x0 -> x1, waiting for transfers between devices: none -> 17.1 us  [per_device(): back = [lax.ppermute(away_grad, 'fsdp', [(0, 1), (1, 0)])] if swap else []]
    ppermute x5 -> x3, waiting for transfers between devices: 25.2 us -> 17.8 us  [per_device(): lax.ppermute(part, 'fsdp', [(0, 1), (1, 0)])]
  transfers between devices with their start and end apart: 43 -> 42, of which waited for: 13 -> 13; matrix products, arithmetic and copies ran while one was open for 6% -> 7% of each run, Pallas kernels for 46% -> 46%
where the time goes in v4:
time: 647 us; the launch traced here: 649 us
  Pallas kernels  420 us (65%)
  waiting for transfers between devices  68.7 us (11%)
  starting transfers between devices  51.8 us (8%)
  other arithmetic  46.6 us (7%)
  local copies, waits for them, and re-layouts  44.5 us (7%)
  between operations  15.2 us (2%)
    pallas_call x4, Pallas kernels, attention_backward(): pl.pallas_call(functools.partial(backward_kernel, q_tile, k_tile), grid_s...  173 us
    pallas_call x1, Pallas kernels, ffn(): pl.pallas_call(functools.partial(ffn_kernel, tile, rows, away), grid_spec...  106 us
    pallas_call x1, Pallas kernels, attention_forward(): pl.pallas_call(functools.partial(forward_kernel, q_tile, k_tile), grid_sp...  93 us
    ppermute x35, starting transfers between devices, from_peer(): lax.ppermute(value, BOTH, [(n, n ^ flip) for n in range(SQUARE_DEVICES)])  42 us
    ppermute x35, waiting for transfers between devices, from_peer(): lax.ppermute(value, BOTH, [(n, n ^ flip) for n in range(SQUARE_DEVICES)])  33.8 us
    pallas_call x1, Pallas kernels, finish_inputs(): pl.pallas_call(functools.partial(finish_kernel, away, len(dq)), grid_spec...  18.7 us
    ppermute x3, waiting for transfers between devices, per_device(): lax.ppermute(part, 'fsdp', [(0, 1), (1, 0)])  17.8 us
    ppermute x1, waiting for transfers between devices, per_device(): back = [lax.ppermute(away_grad, 'fsdp', [(0, 1), (1, 0)])] if swap else []  17.1 us
  transfers between devices with their start and end apart: 42, of which 13 were waited for; matrix products, arithmetic and copies ran while one was open for 7% of the time, Pallas kernels for 46%

profile of v4, /device:TPU:0, one launch (start us, length us, event | category | flops | bytes accessed | tf_op | source)
XLA Modules:
  0.0 648.6 jit_solution(752872706648137787)
XLA Ops:
  7.3 3.3 dynamic-slice_bitcast_fusion.3
  11.5 3.0 collective-permute-start
  20.9 7.1 %collective-permute-done.4 = bf16[24,2432]{1,0:T(8,128)(2,1)} collective-permute-done((bf16[24,2432]{1,0:T(8,128)(2,1)S(1)}, bf16[24,2432]{1,0:T(8,128)(2,1)}, u32[]{:S(2)}, u32[]{:S(2)}) %collective-permute-start.4) | collective-permute-done | bytes 116768 | tf_op jit(solution)/shard_map/ppermute | solution.py:631
  33.9 9.7 %collective-permute-done.1 = bf16[384,768]{1,0:T(8,128)(2,1)S(1)} collective-permute-done((bf16[384,768]{1,0:T(8,128)(2,1)S(1)}, bf16[384,768]{1,0:T(8,128)(2,1)S(1)}, u32[]{:S(2)}, u32[]{:S(2)}) %collective-permute-start.1) | collective-permute-done | bytes 589856 | tf_op jit(solution)/shard_map/ppermute | solution.py:736
  43.6 17.1 %collective-permute-done.6 = bf16[4,24,2432]{2,1,0:T(8,128)(2,1)} collective-permute-done((bf16[4,24,2432]{2,1,0:T(8,128)(2,1)S(1)}, bf16[4,24,2432]{2,1,0:T(8,128)(2,1)}, u32[]{:S(2)}, u32[]{:S(2)}) %collective-permute-start.6) | collective-permute-done | bytes 466976 | tf_op jit(solution)/shard_map/ppermute | solution.py:631
  68.2 7.2 %collective-permute-done.2 = bf16[256,768]{1,0:T(8,128)(2,1)S(1)} collective-permute-done((bf16[256,768]{1,0:T(8,128)(2,1)}, bf16[256,768]{1,0:T(8,128)(2,1)S(1)}, u32[]{:S(2)}, u32[]{:S(2)}) %collective-permute-start.2) | collective-permute-done | bytes 393248 | tf_op jit(solution)/shard_map/ppermute | solution.py:736
  83.6 3.0 maximum_select_fusion.2.x_ref
  91.4 12.1 %project.1 = bf16[2048,2304]{1,0:T(8,128)(2,1)} custom-call(bf16[2048,768]{1,0:T(8,128)(2,1)} %maximum_select_fusion.2.x_ref, bf16[768,2432]{1,0:T(8,128)(2,1)} %bitcast.184, f32[1,768]{1,0:T(1,128)} %get-tuple-element.320.gain_ref), custom_call_target="tpu_custom_call" | custom-call | flops 13200000000 | bytes 1048576 | tf_op jit(solution)/shard_map/project/pallas_call | solution.py:356
  103.6 93.0 %attention_forward.1 = (bf16[1,2048,768]{2,1,0:T(8,128)(2,1)}, bf16[1,6,2048,128]{3,2,1,0:T(8,128)(2,1)}) custom-call(s32[1]{0:T(128)} %dynamic_slice.118.lengths, s32[1]{0:T(128)} %constant.233.clone.1.offset, bf16[1,2048,2304]{2,1,0:T(8,128)(2,1)} %bitcast.196, bf16[1,2048,2304]{2,1,0:T(8,128)(2,1)} %bitcast.197, bf16[1,2048,2304]{2,1,0:T(8,128)(2,1)} %bitcast.198, ...), custom_call_target="tpu_custom_call" | custom-call | flops 109999996928 | bytes 1048576 | tf_op jit(solution)/shard_map/attention_forward/pallas_call | solution.py:125
  198.7 4.8 fusion.56
  203.5 106.0 %ffn.1 = (f32[1024,768]{1,0:T(8,128)}, bf16[1024,768]{1,0:T(8,128)(2,1)}, f32[2048,768]{1,0:T(8,128)}, bf16[2048,768]{1,0:T(8,128)(2,1)}, f32[768,2816]{1,0:T(8,...) custom-call(s32[1]{0:T(128)} %dynamic_slice.118.lengths, s32[2]{0:T(128)} %pad_add_fusion.place, ...), custom_call_target="tpu_custom_call" | custom-call | flops 104500002816 | bytes 1048576 | tf_op jit(solution)/shard_map/ffn/pallas_call | solution.py:474
  309.5 3.2 fusion
  312.8 3.8 fusion.1
  317.1 29.6 %attention_backward.4 = (bf16[1,2048,128]{2,1,0:T(8,128)(2,1)}, bf16[1,2048,128]{2,1,0:T(8,128)(2,1)}, bf16[1,2048,128]{2,1,0:T(8,128)(2,1)}, f32[1,1,2,1792]{3,2,1,0:T(2,128)}) custom-call(s32[1]{0:T(128)} %dynamic_slice.118.lengths, s32[1]{0:T(128)} %constant.233.clone.1.offset, bf16[1,2048,2304]{2,1,0:T(8,128)(2,1)} %bitcast.199, ...), custom_call_target="tpu_custom_call" | custom-call | flops 32999999488 | bytes 1048576 | tf_op jit(solution)/shard_map/attention_backward/pallas_call | solution.py:256
  346.7 3.5 bitcast_add_fusion.1
  355.4 3.0 bitcast_add_fusion
  370.8 56.9 %attention_backward.5 = (bf16[1,2048,256]{2,1,0:T(8,128)(2,1)}, bf16[1,2048,256]{2,1,0:T(8,128)(2,1)}, bf16[1,2048,256]{2,1,0:T(8,128)(2,1)}, f32[1,2,2,1792]{3,2,1,0:T(2,128)}) custom-call(s32[1]{0:T(128)} %dynamic_slice.118.lengths, s32[1]{0:T(128)} %constant.233.clone.1.offset, bf16[1,2048,2304]{2,1,0:T(8,128)(2,1)} %bitcast.202, ...), custom_call_target="tpu_custom_call" | custom-call | flops 65999998976 | bytes 1048576 | tf_op jit(solution)/shard_map/attention_backward/pallas_call | solution.py:256
  443.3 29.6 %attention_backward.6 = (bf16[1,2048,128]{2,1,0:T(8,128)(2,1)}, bf16[1,2048,128]{2,1,0:T(8,128)(2,1)}, bf16[1,2048,128]{2,1,0:T(8,128)(2,1)}, f32[1,1,2,1792]{3,2,1,0:T(2,128)}) custom-call(s32[1]{0:T(128)} %dynamic_slice.118.lengths, s32[1]{0:T(128)} %constant.233.clone.1.offset, bf16[1,2048,2304]{2,1,0:T(8,128)(2,1)} %bitcast.205, ...), custom_call_target="tpu_custom_call" | custom-call | flops 32999999488 | bytes 1048576 | tf_op jit(solution)/shard_map/attention_backward/pallas_call | solution.py:256
  474.5 57.0 %attention_backward.7 = (bf16[1,2048,256]{2,1,0:T(8,128)(2,1)}, bf16[1,2048,256]{2,1,0:T(8,128)(2,1)}, bf16[1,2048,256]{2,1,0:T(8,128)(2,1)}, f32[1,2,2,1792]{3,2,1,0:T(2,128)}) custom-call(s32[1]{0:T(128)} %dynamic_slice.118.lengths, s32[1]{0:T(128)} %constant.233.clone.1.offset, bf16[1,2048,2304]{2,1,0:T(8,128)(2,1)} %bitcast.208, ...), custom_call_target="tpu_custom_call" | custom-call | flops 65999998976 | bytes 1048576 | tf_op jit(solution)/shard_map/attention_backward/pallas_call | solution.py:256
  538.0 2.9 maximum_select_fusion
  540.9 16.9 %finish_weights.1 = (f32[768,2304]{1,0:T(8,128)}, f32[1,768]{1,0:T(1,128)}) custom-call(bf16[2048,768]{1,0:T(8,128)(2,1)} %maximum_select_fusion.2.x_ref, f32[1,768]{1,0:T(1,128)} %get-tuple-element.320.gain_ref, bf16[768,2432]{1,0:T(8,128)(2,1)} %bitcast.185, bf16[2048,128]{1,0:T(8,128)(2,1)} %bitcast.228, bf16[2048,256]{1,0:T(8,128)(2,1)} %bitcast.216, ...), custom_call_target="tpu_custom_call" | custom-call | flops 15399999488 | bytes 1048576 | tf_op jit(solution)/shard_map/finish_weights/pallas_call | solution.py:552
  585.4 18.7 %finish_inputs.1 = (f32[1024,768]{1,0:T(8,128)}, bf16[1024,768]{1,0:T(8,128)(2,1)}) custom-call(s32[2]{0:T(128)} %pad_add_fusion.place, bf16[2048,768]{1,0:T(8,128)(2,1)} %maximum_select_fusion.2.x_ref, f32[2048,768]{1,0:T(8,128)} %get-tuple-element.227.gh_ref, bf16[768,2432]{1,0:T(8,128)(2,1)} %bitcast.186, f32[1,768]{1,0:T(1,128)} %get-tuple-element.320.gain_ref, ...), custom_call_target="tpu_custom_call" | custom-call | flops 17600000000 | bytes 1048576 | tf_op jit(solution)/shard_map/finish_inputs/pallas_call | solution.py:599
  614.8 3.2 collective-permute-done.40
  619.8 17.1 %collective-permute-done.37 = bf16[1024,768]{1,0:T(8,128)(2,1)} collective-permute-done((bf16[1024,768]{1,0:T(8,128)(2,1)}, bf16[1024,768]{1,0:T(8,128)(2,1)}, u32[]{:S(2)}, u32[]{:S(2)}) %collective-permute-start.37) | collective-permute-done | bytes 1572896 | tf_op jit(solution)/shard_map/ppermute | solution.py:831
  (231 shorter events, 121.4 us)
Async XLA Ops:
  7.2 191.5 %all-gather.3.cloned.1.call-start = ((), (), s32[]{:S(2)}) async-start(), calls=%async_computation | async-start | bytes 11354112 | tf_op jit(solution)/shard_map/all_gather | solution.py:751
  19.1 24.5 %collective-permute-start.1 = (bf16[384,768]{1,0:T(8,128)(2,1)S(1)}, bf16[384,768]{1,0:T(8,128)(2,1)S(1)}, u32[]{:S(2)}, u32[]{:S(2)}) collective-permute-start(bf16[384,768]{1,0:T(8,128)(2,1)S(1)} %get-tuple-element.303), channel_id=1, source_target_pairs={{0,1},{1,0},{2,3},{3,2},{4,5},{5,4},{6,7},{7,6},{8,9},{9,8},{10,11... | collective-permute-start | bytes 1769480 | tf_op jit(solution)/shard_map/ppermute | solution.py:736
  30.2 30.5 %collective-permute-start.6 = (bf16[4,24,2432]{2,1,0:T(8,128)(2,1)S(1)}, bf16[4,24,2432]{2,1,0:T(8,128)(2,1)}, u32[]{:S(2)}, u32[]{:S(2)}) collective-permute-start(bf16[4,24,2432]{2,1,0:T(8,128)(2,1)S(1)} %pad_maximum_fusion.2), channel_id=1, source_target_pairs={{0,1},{1,0},{2,3},{3,2},{4,5},{5,4},{6,7},{7,6},{8,9},{9,8},{10,11... | collective-permute-start | bytes 1400840 | tf_op jit(solution)/shard_map/ppermute | solution.py:631
  32.3 28.4 %collective-permute-start.7 = (bf16[4,24,2432]{2,1,0:T(8,128)(2,1)S(1)}, bf16[4,24,2432]{2,1,0:T(8,128)(2,1)}, u32[]{:S(2)}, u32[]{:S(2)}) collective-permute-start(bf16[4,24,2432]{2,1,0:T(8,128)(2,1)S(1)} %pad_maximum_fusion.2), channel_id=1, source_target_pairs={{0,4},{1,5},{2,6},{3,7},{4,0},{5,1},{6,2},{7,3},{8,12},{9,13},{10,... | collective-permute-start | bytes 1400840 | tf_op jit(solution)/shard_map/ppermute | solution.py:631
  33.8 26.9 %collective-permute-start.8 = (bf16[4,24,2432]{2,1,0:T(8,128)(2,1)S(1)}, bf16[4,24,2432]{2,1,0:T(8,128)(2,1)}, u32[]{:S(2)}, u32[]{:S(2)}) collective-permute-start(bf16[4,24,2432]{2,1,0:T(8,128)(2,1)S(1)} %pad_maximum_fusion.2), channel_id=1, source_target_pairs={{0,5},{1,4},{2,7},{3,6},{4,1},{5,0},{6,3},{7,2},{8,13},{9,12},{10,... | collective-permute-start | bytes 1400840 | tf_op jit(solution)/shard_map/ppermute | solution.py:631
  88.0 108.6 %collective-permute-start.10 = (bf16[1024,768]{1,0:T(8,128)(2,1)}, bf16[1024,768]{1,0:T(8,128)(2,1)S(1)}, u32[]{:S(2)}, u32[]{:S(2)}) collective-permute-start(bf16[1024,768]{1,0:T(8,128)(2,1)} %get-tuple-element.292), channel_id=1, source_target_pairs={{0,1},{1,0},{2,3},{3,2},{4,5},{5,4},{6,7},{7,6},{8,9},{9,8},{10,11... | collective-permute-start | bytes 4718600 | tf_op jit(solution)/shard_map/ppermute | solution.py:695
  312.7 34.0 %collective-permute-start.12 = (bf16[4,2,2,64,1536]{4,3,2,1,0:T(8,128)(2,1)S(1)}, bf16[4,2,2,64,1536]{4,3,2,1,0:T(8,128)(2,1)}, u32[]{:S(2)}, u32[]{:S(2)}) collective-permute-start(bf16[4,2,2,64,1536]{4,3,2,1,0:T(8,128)(2,1)S(1)} %fusion), channel_id=1, source_target_pairs={{0,2},{1,3},{2,0},{3,1},{4,6},{5,7},{6,4},{7,5},{8,10},{9,11},{10,... | collective-permute-start | bytes 9437192 | tf_op jit(solution)/shard_map/ppermute | solution.py:631
  316.6 30.1 %collective-permute-start.11 = (bf16[4,2,2,24,2816]{4,3,2,1,0:T(8,128)(2,1)}, bf16[4,2,2,24,2816]{4,3,2,1,0:T(8,128)(2,1)}, u32[]{:S(2)}, u32[]{:S(2)}) collective-permute-start(bf16[4,2,2,24,2816]{4,3,2,1,0:T(8,128)(2,1)} %fusion.1), channel_id=1, source_target_pairs={{0,2},{1,3},{2,0},{3,1},{4,6},{5,7},{6,4},{7,5},{8,10},{9,11},{10,... | collective-permute-start | bytes 6488072 | tf_op jit(solution)/shard_map/ppermute | solution.py:631
  362.8 65.0 %collective-permute-start.16 = (bf16[4,64,1536]{2,1,0:T(8,128)(2,1)}, bf16[4,64,1536]{2,1,0:T(8,128)(2,1)S(1)}, u32[]{:S(2)}, u32[]{:S(2)}) collective-permute-start(bf16[4,64,1536]{2,1,0:T(8,128)(2,1)} %get-tuple-element.282), channel_id=1, source_target_pairs={{0,1},{1,0},{2,3},{3,2},{4,5},{5,4},{6,7},{7,6},{8,9},{9,8},{10,11... | collective-permute-start | bytes 2359304 | tf_op jit(solution)/shard_map/ppermute | solution.py:631
  363.2 64.6 %collective-permute-start.17 = (bf16[4,64,1536]{2,1,0:T(8,128)(2,1)S(1)}, bf16[4,64,1536]{2,1,0:T(8,128)(2,1)S(1)}, u32[]{:S(2)}, u32[]{:S(2)}) collective-permute-start(bf16[4,64,1536]{2,1,0:T(8,128)(2,1)S(1)} %get-tuple-element.281), channel_id=1, source_target_pairs={{0,4},{1,5},{2,6},{3,7},{4,0},{5,1},{6,2},{7,3},{8,12},{9,13},{10,... | collective-permute-start | bytes 2359304 | tf_op jit(solution)/shard_map/ppermute | solution.py:631
  364.9 62.9 %collective-permute-start.18 = (bf16[4,64,1536]{2,1,0:T(8,128)(2,1)S(1)}, bf16[4,64,1536]{2,1,0:T(8,128)(2,1)S(1)}, u32[]{:S(2)}, u32[]{:S(2)}) collective-permute-start(bf16[4,64,1536]{2,1,0:T(8,128)(2,1)S(1)} %get-tuple-element.280), channel_id=1, source_target_pairs={{0,5},{1,4},{2,7},{3,6},{4,1},{5,0},{6,3},{7,2},{8,13},{9,12},{10,... | collective-permute-start | bytes 2359304 | tf_op jit(solution)/shard_map/ppermute | solution.py:631
  366.2 61.5 %collective-permute-start.14 = (bf16[4,24,2816]{2,1,0:T(8,128)(2,1)}, bf16[4,24,2816]{2,1,0:T(8,128)(2,1)}, u32[]{:S(2)}, u32[]{:S(2)}) collective-permute-start(bf16[4,24,2816]{2,1,0:T(8,128)(2,1)} %get-tuple-element.284), channel_id=1, source_target_pairs={{0,4},{1,5},{2,6},{3,7},{4,0},{5,1},{6,2},{7,3},{8,12},{9,13},{10,... | collective-permute-start | bytes 1622024 | tf_op jit(solution)/shard_map/ppermute | solution.py:631
  369.3 58.5 %collective-permute-start.15 = (bf16[4,24,2816]{2,1,0:T(8,128)(2,1)}, bf16[4,24,2816]{2,1,0:T(8,128)(2,1)}, u32[]{:S(2)}, u32[]{:S(2)}) collective-permute-start(bf16[4,24,2816]{2,1,0:T(8,128)(2,1)} %get-tuple-element.283), channel_id=1, source_target_pairs={{0,5},{1,4},{2,7},{3,6},{4,1},{5,0},{6,3},{7,2},{8,13},{9,12},{10,... | collective-permute-start | bytes 1622024 | tf_op jit(solution)/shard_map/ppermute | solution.py:631
  435.0 39.4 %collective-permute-start.22 = (bf16[64,1536]{1,0:T(8,128)(2,1)S(1)}, bf16[64,1536]{1,0:T(8,128)(2,1)S(1)}, u32[]{:S(2)}, u32[]{:S(2)}) collective-permute-start(bf16[64,1536]{1,0:T(8,128)(2,1)S(1)} %get-tuple-element.301), channel_id=1, source_target_pairs={{0,8},{1,9},{2,10},{3,11},{4,12},{5,13},{6,14},{7,15},{8,0},{9,1},... | collective-permute-start | bytes 589832 | tf_op jit(solution)/shard_map/ppermute | solution.py:631
  435.5 38.9 %collective-permute-start.23 = (bf16[64,1536]{1,0:T(8,128)(2,1)S(1)}, bf16[64,1536]{1,0:T(8,128)(2,1)S(1)}, u32[]{:S(2)}, u32[]{:S(2)}) collective-permute-start(bf16[64,1536]{1,0:T(8,128)(2,1)S(1)} %get-tuple-element.300), channel_id=1, source_target_pairs={{0,16},{1,17},{2,18},{3,19},{4,20},{5,21},{6,22},{7,23},{8,24},{9,... | collective-permute-start | bytes 589832 | tf_op jit(solution)/shard_map/ppermute | solution.py:631
  438.1 36.3 %collective-permute-start.24 = (bf16[64,1536]{1,0:T(8,128)(2,1)S(1)}, bf16[64,1536]{1,0:T(8,128)(2,1)S(1)}, u32[]{:S(2)}, u32[]{:S(2)}) collective-permute-start(bf16[64,1536]{1,0:T(8,128)(2,1)S(1)} %get-tuple-element.299), channel_id=1, source_target_pairs={{0,24},{1,25},{2,26},{3,27},{4,28},{5,29},{6,30},{7,31},{8,16},{9,... | collective-permute-start | bytes 589832 | tf_op jit(solution)/shard_map/ppermute | solution.py:631
  439.5 33.5 %collective-permute-start.20 = (bf16[24,2816]{1,0:T(8,128)(2,1)}, bf16[24,2816]{1,0:T(8,128)(2,1)S(1)}, u32[]{:S(2)}, u32[]{:S(2)}) collective-permute-start(bf16[24,2816]{1,0:T(8,128)(2,1)} %get-tuple-element.305), channel_id=1, source_target_pairs={{0,16},{1,17},{2,18},{3,19},{4,20},{5,21},{6,22},{7,23},{8,24},{9,... | collective-permute-start | bytes 405512 | tf_op jit(solution)/shard_map/ppermute | solution.py:631
  441.1 33.3 %collective-permute-start.21 = (bf16[24,2816]{1,0:T(8,128)(2,1)}, bf16[24,2816]{1,0:T(8,128)(2,1)}, u32[]{:S(2)}, u32[]{:S(2)}) collective-permute-start(bf16[24,2816]{1,0:T(8,128)(2,1)} %get-tuple-element.304), channel_id=1, source_target_pairs={{0,24},{1,25},{2,26},{3,27},{4,28},{5,29},{6,30},{7,31},{8,16},{9,... | collective-permute-start | bytes 405512 | tf_op jit(solution)/shard_map/ppermute | solution.py:631
  472.9 63.4 %collective-permute-start.25 = (bf16[1024,768]{1,0:T(8,128)(2,1)}, bf16[1024,768]{1,0:T(8,128)(2,1)}, u32[]{:S(2)}, u32[]{:S(2)}) collective-permute-start(bf16[1024,768]{1,0:T(8,128)(2,1)} %get-tuple-element.188), channel_id=1, source_target_pairs={{0,1},{1,0},{2,3},{3,2},{4,5},{5,4},{6,7},{7,6},{8,9},{9,8},{10,11... | collective-permute-start | bytes 4718600 | tf_op jit(solution)/shard_map/ppermute | solution.py:795
  560.0 18.0 %collective-permute-start.26 = (bf16[4,2,2,24,2304]{4,3,2,1,0:T(8,128)(2,1)S(1)}, bf16[4,2,2,24,2304]{4,3,2,1,0:T(8,128)(2,1)S(1)}, u32[]{:S(2)}, u32[]{:S(2)}) collective-permute-start(bf16[4,2,2,24,2304]{4,3,2,1,0:T(8,128)(2,1)S(1)} %fusion.2), channel_id=1, source_target_pairs={{0,2},{1,3},{2,0},{3,1},{4,6},{5,7},{6,4},{7,5},{8,10},{9,11},{10,... | collective-permute-start | bytes 5308424 | tf_op jit(solution)/shard_map/ppermute | solution.py:631
  581.9 22.2 %collective-permute-start.27 = (bf16[4,24,2304]{2,1,0:T(8,128)(2,1)}, bf16[4,24,2304]{2,1,0:T(8,128)(2,1)S(1)}, u32[]{:S(2)}, u32[]{:S(2)}) collective-permute-start(bf16[4,24,2304]{2,1,0:T(8,128)(2,1)} %get-tuple-element.290), channel_id=1, source_target_pairs={{0,1},{1,0},{2,3},{3,2},{4,5},{5,4},{6,7},{7,6},{8,9},{9,8},{10,11... | collective-permute-start | bytes 1327112 | tf_op jit(solution)/shard_map/ppermute | solution.py:631
  583.4 20.8 %collective-permute-start.28 = (bf16[4,24,2304]{2,1,0:T(8,128)(2,1)}, bf16[4,24,2304]{2,1,0:T(8,128)(2,1)}, u32[]{:S(2)}, u32[]{:S(2)}) collective-permute-start(bf16[4,24,2304]{2,1,0:T(8,128)(2,1)} %get-tuple-element.289), channel_id=1, source_target_pairs={{0,4},{1,5},{2,6},{3,7},{4,0},{5,1},{6,2},{7,3},{8,12},{9,13},{10,... | collective-permute-start | bytes 1327112 | tf_op jit(solution)/shard_map/ppermute | solution.py:631
  584.9 19.3 %collective-permute-start.29 = (bf16[4,24,2304]{2,1,0:T(8,128)(2,1)}, bf16[4,24,2304]{2,1,0:T(8,128)(2,1)}, u32[]{:S(2)}, u32[]{:S(2)}) collective-permute-start(bf16[4,24,2304]{2,1,0:T(8,128)(2,1)} %get-tuple-element.288), channel_id=1, source_target_pairs={{0,5},{1,4},{2,7},{3,6},{4,1},{5,0},{6,3},{7,2},{8,13},{9,12},{10,... | collective-permute-start | bytes 1327112 | tf_op jit(solution)/shard_map/ppermute | solution.py:631
  604.2 32.7 %collective-permute-start.37 = (bf16[1024,768]{1,0:T(8,128)(2,1)}, bf16[1024,768]{1,0:T(8,128)(2,1)}, u32[]{:S(2)}, u32[]{:S(2)}) collective-permute-start(bf16[1024,768]{1,0:T(8,128)(2,1)} %get-tuple-element.235), channel_id=1, source_target_pairs={{0,1},{1,0},{2,3},{3,2},{4,5},{5,4},{6,7},{7,6},{8,9},{9,8},{10,11... | collective-permute-start | bytes 4718600 | tf_op jit(solution)/shard_map/ppermute | solution.py:831
  (57 other events, 700.8 us)
Sparse Core Ops, SparseCore 0:
  80.0 93.9 all-gather.2
